TPU v7x, 256 devices: a whole 4x4x8 slice. The times are simulated.
256 devices in a mesh: bin: 32 (over y, x, core), gcol: 8 (over z).
Axes of the slice: x: 4, y: 4, z: 8, core: 2. Of those that a mesh axis runs over, the one named last changes fastest.
Arguments:
- pair_rows: bfloat16 [16384, 2, 4096], P('bin', None, 'gcol'), may hold values from -5 to 5
- pair_owner: int32 [16384, 1], P('bin'), may hold values from 0 to 31; in each aligned block of 512 rows (0 to 511, 512 to 1023, ...) at most 32 rows name the same one
- pair_offset: int32 [16384], P('bin'), may hold values from 0 to 7
- pair_frac: float32 [16384], P('bin'), may hold values from 0 to 1
Outputs:
- chi_zero: float32 [256, 2, 128, 4096], P('bin', None, None, 'gcol')
Inputs may be any that keep to these rules, and one draw needn't show every extreme that they name: `pair_owner`: among the rows of one device at most 32 pairs name the same owner, and in every draw some owner is named by exactly 32 rows of some device.
All inputs are finite; a program needn't handle non-finite values.
Results may differ from a plain program's by a relative error of at most 0.0039.
Values may be sent and summed in bfloat16 or wider, within the bound.
No kernel may reach another device: no remote copies, remote signals or barrier semaphores. Data moves between devices by JAX's collectives and lax.ppermute only.
A program may use at most 64 MiB of HBM per device.

v0:
```python
import jax
import jax.numpy as jnp
from jax import lax
from jax.sharding import PartitionSpec as P

NB = 256
GW = 128


def broadcast(shard, axis, root):
    mine = lax.axis_index(axis) == root
    return lax.psum(jnp.where(mine, shard, jnp.zeros_like(shard)), axis)


def from_behind(block, axis, distance):
    devices = range(lax.axis_size(axis))
    route = [(i - distance, i) for i in devices if i - distance in devices]
    return lax.ppermute(block, axis, route)


def hilbert_table(bin_total):
    column = jnp.arange(bin_total, dtype=jnp.float32)
    difference = column[:, None] - column[None, :]
    second = column[:, None] + column[None, :] + 1.0
    real_part = difference / (difference * difference + 1.0) - second / (second * second + 1.0)
    imag_part = 1.0 / (second * second + 1.0) - 1.0 / (difference * difference + 1.0)
    return (real_part, imag_part)


def apply_hilbert(spectral):
    bin_total = spectral.shape[0]
    real_table, imag_table = hilbert_table(bin_total)
    flat_real = spectral[:, 0].astype(jnp.float32).reshape(bin_total, -1)
    flat_imag = spectral[:, 1].astype(jnp.float32).reshape(bin_total, -1)
    highest = lax.Precision.HIGHEST
    out_real = jnp.dot(real_table, flat_real, precision=highest) - jnp.dot(
        imag_table, flat_imag, precision=highest
    )
    out_imag = jnp.dot(real_table, flat_imag, precision=highest) + jnp.dot(
        imag_table, flat_real, precision=highest
    )
    return jnp.stack([out_real, out_imag], axis=1).reshape(spectral.shape)


def weight_table(pair_offset, pair_frac, bin_count):
    lower_weight = (1.0 - pair_frac).astype(jnp.bfloat16)
    upper_weight = pair_frac.astype(jnp.bfloat16)
    column = jnp.arange(bin_count, dtype=jnp.int32)
    nothing = jnp.zeros((), jnp.bfloat16)
    lower_part = jnp.where(column[None, :] == pair_offset[:, None], lower_weight[:, None], nothing)
    upper_part = jnp.where(
        column[None, :] == pair_offset[:, None] + 1, upper_weight[:, None], nothing
    )
    return lower_part + upper_part


def spectral_tile(weights, head_vals, row_data):
    slot_count, bin_count = weights.shape
    scaled = (
        weights.astype(jnp.float32)[:, None, :, None] * head_vals.astype(jnp.float32)[:, :, None, :]
    ).astype(jnp.bfloat16)
    products = lax.dot_general(
        scaled.reshape(slot_count, -1),
        row_data.reshape(slot_count, -1),
        (((0,), (0,)), ((), ())),
        preferred_element_type=jnp.float32,
    )
    products = products.reshape(2, bin_count, head_vals.shape[2], 2, row_data.shape[2])
    real_part = products[0, :, :, 0] + products[1, :, :, 1]
    imag_part = products[0, :, :, 1] - products[1, :, :, 0]
    return jnp.stack([real_part, imag_part], axis=1)


def on_device(pair_rows, pair_owner, pair_offset, pair_frac):
    groups = lax.axis_size("bin")
    pair_count = pair_rows.shape[0]
    col_width = pair_rows.shape[2]
    capacity = 2 * pair_count // groups
    slot_count = groups * capacity
    own_bins = NB // groups
    owners = pair_owner[:, 0]
    weights = weight_table(pair_offset, pair_frac, own_bins + 1)
    onehot = (owners[:, None] == jnp.arange(groups, dtype=jnp.int32)[None, :]).astype(jnp.int32)
    rank_in_owner = jnp.sum((jnp.cumsum(onehot, axis=0) - onehot) * onehot, axis=1)
    target = owners * capacity + rank_in_owner

    def packed(values):
        filled = jnp.zeros((slot_count,) + values.shape[1:], values.dtype).at[target].set(values)
        return filled.reshape((groups, capacity) + values.shape[1:])

    head_vals = broadcast(pair_rows[:, :, :GW], "gcol", 0)
    got_rows, got_weights, got_head = (
        lax.all_to_all(packed(pair_rows), "bin", split_axis=0, concat_axis=0, tiled=True),
        lax.all_to_all(packed(weights), "bin", split_axis=0, concat_axis=0, tiled=True),
        lax.all_to_all(packed(head_vals), "bin", split_axis=0, concat_axis=0, tiled=True),
    )
    got_head = got_head.reshape(slot_count, 2, GW)
    bin_tiles = spectral_tile(
        got_weights.reshape(slot_count, -1), got_head, got_rows.reshape(slot_count, 2, col_width)
    )
    upper_tile = from_behind(bin_tiles[own_bins], "bin", 1)
    lower_tiles = bin_tiles[:own_bins].at[0].add(upper_tile)
    spectral = lower_tiles.astype(jnp.bfloat16)
    return lax.all_to_all(
        apply_hilbert(lax.all_to_all(spectral, "bin", split_axis=2, concat_axis=0, tiled=True)),
        "bin",
        split_axis=0,
        concat_axis=2,
        tiled=True,
    )


def solution(mesh):
    placed = (P("bin", None, "gcol"), P("bin", None), P("bin"), P("bin"))
    return jax.shard_map(
        on_device,
        mesh=mesh,
        in_specs=placed,
        out_specs=P("bin", None, None, "gcol"),
        check_vma=False,
    )
```

profile of v0, /device:TPU:1, one launch (start us, length us, event | category | flops | bytes accessed | tf_op | source)
XLA Modules:
  0.0 347.7 jit_solution(9294233098818899924)
XLA Ops:
  6.5 1.9 broadcast_select_fusion
  10.6 1.2 reduce-window.6
  12.0 0.8 fusion.43
  13.5 2.3 scatter_custom_fusion
  16.8 8.6 %all-to-all-start = ((bf16[32,2,144]{2,1,0:T(2,128)(2,1)}), bf16[32,2,144]{2,1,0:T(2,128)(2,1)S(1)}, u32[]{:S(2)}, u32[]{:S(2)}) async-start(bf16[32,2,144]{2,1,0:T(2,128)(2,1)} %reshape.180), calls=%async_computation | async-start | bytes 65536 | tf_op jit(solution)/shard_map/all_to_all | solution.py:94
  25.4 56.1 %all-reduce.2.cloned.1.call-done = bf16[512,2,128]{2,1,0:T(2,128)(2,1)} async-done(((bf16[512,2,128]{2,1,0:T(2,128)(2,1)}), bf16[512,2,128]{2,1,0:T(2,128)(2,1)}) %all-reduce.2.cloned.1.call-update) | async-done | bytes 262160 | tf_op jit(solution)/shard_map/psum | solution.py:12
  81.8 29.8 %scatter_fusion = bf16[1024,2,128]{2,1,0:T(2,128)(2,1)S(1)} fusion(bf16[1024,2,128]{2,1,0:T(2,128)(2,1)S(1)} %broadcast_in_dim.50, s32[512]{0:T(512)S(1)} %bitcast.125, bf16[512,2,128]{2,1,0:T(2,128)(2,1)} %all-reduce.2.cloned.1.call-done), kind=kCustom, calls=%fused_computation.1 | custom fusion | bytes 788480 | tf_op jit(solution)/shard_map/scatter | solution.py:88
  111.6 0.9 copy.85
  112.5 12.0 %all-to-all-start.1 = ((bf16[32,32,2,128]{3,1,2,0:T(8,128)(2,1)}), bf16[32,32,2,128]{3,1,2,0:T(8,128)(2,1)S(1)}, u32[]{:S(2)}, u32[]{:S(2)}) async-start(bf16[32,32,2,128]{3,1,2,0:T(8,128)(2,1)} %copy.85), calls=%async_computation.1 | async-start | bytes 1048576 | tf_op jit(solution)/shard_map/all_to_all | solution.py:95
  124.6 1.1 broadcast_in_dim.52
  125.6 37.4 %scatter_fusion.1 = bf16[1024,2,512]{2,1,0:T(2,128)(2,1)S(1)} fusion(bf16[1024,2,512]{2,1,0:T(2,128)(2,1)S(1)} %broadcast_in_dim.52, s32[512]{0:T(512)S(1)} %bitcast.126, bf16[512,2,512]{2,1,0:T(2,128)(2,1)} %param.6), kind=kCustom, calls=%fused_computation.2 | custom fusion | bytes 3147776 | tf_op jit(solution)/shard_map/scatter | solution.py:88
  163.0 1.8 copy.89
  164.9 7.4 %all-to-all-start.2 = ((bf16[32,32,2,512]{3,1,2,0:T(8,128)(2,1)}), bf16[32,32,2,512]{3,1,2,0:T(8,128)(2,1)S(1)}, u32[]{:S(2)}, u32[]{:S(2)}) async-start(bf16[32,32,2,512]{3,1,2,0:T(8,128)(2,1)} %copy.89), calls=%async_computation.2 | async-start | bytes 4194304 | tf_op jit(solution)/shard_map/all_to_all | solution.py:93
  172.7 1.3 copy.87
  174.0 26.0 %all-to-all-done.2 = bf16[32,32,2,512]{3,1,2,0:T(8,128)(2,1)S(1)} async-done(((bf16[32,32,2,512]{3,1,2,0:T(8,128)(2,1)}), bf16[32,32,2,512]{3,1,2,0:T(8,128)(2,1)S(1)}, u32[]{:S(2)}, u32[]{:S(2)}) %all-to-all-start.2) | async-done | bytes 2097184 | tf_op jit(solution)/shard_map/all_to_all | solution.py:93
  200.0 2.2 copy.90
  202.8 2.6 copy.91
  205.3 6.7 %fusion.1 = f32[2,9,128,2,512]{4,2,3,1,0:T(8,128)S(1)} fusion(bf16[2,512,1024,1,1]{2,1,0,4,3:T(8,128)(2,1)} %bitcast.118, f32[1024,2,128]{0,2,1:T(8,128)S(1)} %copy-done.1, f32[1024,9]{0,1:T(8,128)S(1)} %reshape.149), kind=kOutput, calls=%fused_computation.9 | convolution fusion | flops 4836556800 | bytes 12619776 | tf_op jit(solution)/shard_map/dot_general | solution.py:62
  213.2 3.6 %collective-permute-start = (f32[2,128,512]{2,1,0:T(8,128)S(1)}, f32[2,128,512]{2,1,0:T(8,128)S(1)}, u32[]{:S(2)}, u32[]{:S(2)}) collective-permute-start(f32[2,128,512]{2,1,0:T(8,128)S(1)} %fusion.14), channel_id=1, source_target_pairs={{0,8},{8,16},{16,24},{24,32},{32,40},{40,48},{48,56},{56,64},{64,7... | collective-permute-start | bytes 1572872 | tf_op jit(solution)/shard_map/ppermute | solution.py:18
  217.2 5.7 %collective-permute-done = f32[2,128,512]{2,1,0:T(8,128)S(1)} collective-permute-done((f32[2,128,512]{2,1,0:T(8,128)S(1)}, f32[2,128,512]{2,1,0:T(8,128)S(1)}, u32[]{:S(2)}, u32[]{:S(2)}) %collective-permute-start) | collective-permute-done | bytes 524320 | tf_op jit(solution)/shard_map/ppermute | solution.py:18
  223.0 1.2 copy.96
  224.2 35.7 %all_to_all.51 = bf16[8,2,128,512]{3,0,1,2:T(8,128)(2,1)S(1)} all-to-all(bf16[8,2,128,512]{3,0,1,2:T(8,128)(2,1)S(1)} %copy.96), channel_id=1, replica_groups=mesh['bin'=32,'gcol'=8] {'bin'}, dimensions={2} | all-to-all | bytes 4194304 | tf_op jit(solution)/shard_map/all_to_all | solution.py:105
  261.4 1.1 fusion.37
  262.5 2.5 fusion.39
  265.0 2.4 convolution_add_fusion
  267.4 2.4 stack.16
  269.8 2.7 convolution_subtract_fusion
  272.5 2.5 stack.15
  275.0 3.3 pad_maximum_fusion
  278.3 54.4 %all_to_all.52 = f32[256,2,4,512]{3,2,1,0:T(4,128)S(1)} all-to-all(f32[256,2,4,512]{3,2,1,0:T(4,128)S(1)} %pad_maximum_fusion), channel_id=1, replica_groups=mesh['bin'=32,'gcol'=8] {'bin'}, dimensions={0} | all-to-all | bytes 8388608 | tf_op jit(solution)/shard_map/all_to_all | solution.py:104
  332.7 2.8 copy.103
  335.5 5.3 %all_to_all.45 = f32[8,2,128,512]{3,2,1,0:T(8,128)} reshape(f32[8,2,32,4,512]{4,3,2,1,0:T(4,128)} %copy.103) | data formatting | bytes 8388608 | tf_op jit(solution)/shard_map/all_to_all | solution.py:104
  (33 shorter events, 8.4 us)
Async XLA Ops:
  6.5 74.9 %all-reduce.2.cloned.1.call-start = ((), (), s32[]{:S(2)}) async-start(), calls=%async_computation.5 | async-start | bytes 524288 | tf_op jit(solution)/shard_map/psum | solution.py:12
  16.8 95.7 %all-to-all-start = ((bf16[32,2,144]{2,1,0:T(2,128)(2,1)}), bf16[32,2,144]{2,1,0:T(2,128)(2,1)S(1)}, u32[]{:S(2)}, u32[]{:S(2)}) async-start(bf16[32,2,144]{2,1,0:T(2,128)(2,1)} %reshape.180), calls=%async_computation | async-start | bytes 65536 | tf_op jit(solution)/shard_map/all_to_all | solution.py:94
  112.5 52.4 %all-to-all-start.1 = ((bf16[32,32,2,128]{3,1,2,0:T(8,128)(2,1)}), bf16[32,32,2,128]{3,1,2,0:T(8,128)(2,1)S(1)}, u32[]{:S(2)}, u32[]{:S(2)}) async-start(bf16[32,32,2,128]{3,1,2,0:T(8,128)(2,1)} %copy.85), calls=%async_computation.1 | async-start | bytes 1048576 | tf_op jit(solution)/shard_map/all_to_all | solution.py:95
  164.9 35.2 %all-to-all-start.2 = ((bf16[32,32,2,512]{3,1,2,0:T(8,128)(2,1)}), bf16[32,32,2,512]{3,1,2,0:T(8,128)(2,1)S(1)}, u32[]{:S(2)}, u32[]{:S(2)}) async-start(bf16[32,32,2,512]{3,1,2,0:T(8,128)(2,1)} %copy.89), calls=%async_computation.2 | async-start | bytes 4194304 | tf_op jit(solution)/shard_map/all_to_all | solution.py:93
  202.8 2.6 copy-start.1
  213.2 9.8 %collective-permute-start = (f32[2,128,512]{2,1,0:T(8,128)S(1)}, f32[2,128,512]{2,1,0:T(8,128)S(1)}, u32[]{:S(2)}, u32[]{:S(2)}) collective-permute-start(f32[2,128,512]{2,1,0:T(8,128)S(1)} %fusion.14), channel_id=1, source_target_pairs={{0,8},{8,16},{16,24},{24,32},{32,40},{40,48},{48,56},{56,64},{64,7... | collective-permute-start | bytes 1572872 | tf_op jit(solution)/shard_map/ppermute | solution.py:18
  260.9 1.7 copy-start
Sparse Core Ops, SparseCore 0:
  9.7 71.7 all-reduce.1
where the time goes:
time: 352 us; the launch traced here: 348 us
  local copies, waits for them, and re-layouts  95.1 us (27%)
  blocking collectives  90.1 us (26%)
  waiting for transfers between devices  87.9 us (25%)
  starting transfers between devices  31.7 us (9%)
  matrix products  15.3 us (4%)
  other arithmetic  13.9 us (4%)
  between operations  13.7 us (4%)
    scatter x2, local copies, waits for them, and re-layouts, packed(): jnp.zeros((slot_count,) + values.shape[1:], values.dtype).at[target]  67.2 us
    psum x1, waiting for transfers between devices, broadcast(): return lax.psum(jnp.where(mine, shard, jnp.zeros_like(shard)), axis)  56.1 us
    all_to_all x1, blocking collectives, on_device(): lax.all_to_all(apply_hilbert(lax.all_to_all(spectral, 'bin', split_axis=2...  54.4 us
    all_to_all x1, blocking collectives, on_device(): lax.all_to_all(spectral, 'bin', split_axis=2, concat_axis=0, tiled=True)  35.7 us
    all_to_all x1, waiting for transfers between devices, on_device(): lax.all_to_all(packed(pair_rows), 'bin', split_axis=0, concat_axis=0, til...  26 us
    all_to_all x1, starting transfers between devices, on_device(): lax.all_to_all(packed(head_vals), 'bin', split_axis=0, concat_axis=0, til...  12 us
    all_to_all x1, starting transfers between devices, on_device(): lax.all_to_all(packed(weights), 'bin', split_axis=0, concat_axis=0, tiled...  8.59 us
    all_to_all x2, local copies, waits for them, and re-layouts, on_device(): lax.all_to_all(apply_hilbert(lax.all_to_all(spectral, 'bin', split_axis=2...  8.1 us
  transfers between devices with their start and end apart: 5, of which 3 were waited for; matrix products, arithmetic and copies ran while one was open for 24% of the time, Pallas kernels for 0%

commit v1 on v0

v1 whole, which is shorter than its diff:
```python
import functools

import jax
import jax.numpy as jnp
from jax import lax
from jax.experimental import pallas as pl
from jax.experimental.pallas import tpu as pltpu
from jax.sharding import PartitionSpec as P

NB = 256
GW = 128
BF16 = jnp.bfloat16
F32 = jnp.float32
VMEM_BYTES = 48 * 1024 * 1024
PARTS = 2


def dot(a, b):
    return jnp.dot(a, b, preferred_element_type=F32)


def iota(shape, axis):
    return lax.broadcasted_iota(jnp.int32, shape, axis)


def call(kernel, out_shape, **options):
    return pl.pallas_call(
        kernel,
        out_shape=out_shape,
        compiler_params=pltpu.CompilerParams(vmem_limit_bytes=VMEM_BYTES),
        **options,
    )


def slot_onehot(target, slot_count):
    pairs = target.shape[1]
    return (iota((slot_count, pairs), 0) == target).astype(F32).astype(BF16)


def pack_rows_kernel(owner_ref, rows_ref, target_ref, *out_refs):
    groups, _, capacity, width = out_refs[0].shape
    pairs = owner_ref.shape[1]
    owner = owner_ref[...]
    named = (iota((groups, pairs), 0) == owner).astype(F32)
    before = (iota((pairs, pairs), 0) < iota((pairs, pairs), 1)).astype(F32).astype(BF16)
    rank = jnp.sum(dot(named.astype(BF16), before) * named, axis=0, keepdims=True)
    target = owner * capacity + rank.astype(jnp.int32)
    target_ref[...] = target
    onehot = slot_onehot(target, groups * capacity)
    for part, out_ref in enumerate(out_refs):
        for c in range(2):
            values = rows_ref[c, :, part * width : (part + 1) * width]
            packed = dot(onehot, values).astype(BF16)
            out_ref[:, c] = packed.reshape(groups, capacity, width)


def pack_heads_kernel(target_ref, head_ref, weight_ref, out_ref):
    groups, capacity, width = out_ref.shape
    onehot = slot_onehot(target_ref[...], groups * capacity)
    head = dot(onehot, head_ref[...]).astype(BF16)
    weight = dot(onehot, weight_ref[...]).astype(BF16)
    split = head_ref.shape[1]
    out_ref[:, :, :split] = head.reshape(groups, capacity, split)
    out_ref[:, :, split:] = weight.reshape(groups, capacity, width - split)


def turn_kernel(in_ref, head_ref, weight_ref):
    groups, capacity, width = in_ref.shape
    turned = in_ref[...].reshape(groups * capacity, width).astype(F32).T
    head_ref[...] = turned[: 2 * GW].astype(BF16)
    weight_ref[...] = turned[2 * GW : 2 * GW + weight_ref.shape[0]]


def row_parts(rows_ref):
    groups, _, capacity, width = rows_ref.shape
    return [rows_ref[:, c].reshape(groups * capacity, width) for c in range(2)]


def complex_dot(left, right):
    real = dot(left[0], right[0]) + dot(left[1], right[1])
    imag = dot(left[0], right[1]) - dot(left[1], right[0])
    return real, imag


def upper_kernel(own_bins, head_ref, weight_ref, rows_ref, out_ref):
    weight = weight_ref[own_bins : own_bins + 1]
    scaled = [
        (head_ref[c * GW : (c + 1) * GW].astype(F32) * weight).astype(BF16) for c in range(2)
    ]
    real, imag = complex_dot(scaled, row_parts(rows_ref))
    out_ref[0] = real
    out_ref[1] = imag


def spectral_kernel(own_bins, head_ref, weight_ref, rows_ref, upper_ref, out_ref):
    chunk, per, _, width = out_ref.shape
    window = chunk * per
    slots = weight_ref.shape[1]
    at = pl.program_id(0) * window
    weight = weight_ref[:own_bins]
    scaled = []
    for c in range(2):
        head = head_ref[pl.ds(pl.multiple_of(c * GW + at, window), window)].astype(F32)
        scaled.append(
            (head[:, None, :] * weight[None]).astype(BF16).reshape(window * own_bins, slots)
        )
    result = complex_dot(scaled, row_parts(rows_ref))
    lowest = iota((window, own_bins, width), 1) == 0
    held = []
    for c in range(2):
        extra = upper_ref[c].reshape(window, 1, width)
        held.append(
            result[c].reshape(window, own_bins, width) + jnp.where(lowest, extra, 0.0)
        )
    out_ref[...] = (
        jnp.concatenate(held, axis=1).astype(BF16).reshape(chunk, per, 2 * own_bins, width)
    )


def hilbert_kernel(high_ref, low_ref, in_ref, out_ref):
    groups, per, depth, width = in_ref.shape
    for g in range(per):
        values = in_ref[:, g].reshape(groups * depth, width)
        result = dot(high_ref[...], values) + dot(low_ref[...], values)
        out_ref[:, g] = result.astype(BF16).reshape(groups, depth, width)


def final_kernel(in_ref, *refs):
    out_ref, wide = refs[-2:]
    step = pl.program_id(0)
    own_bins = pl.num_programs(0)
    rows = in_ref.shape[0] * in_ref.shape[1]
    depth, width = in_ref.shape[2:]

    @pl.when(step == 0)
    def _():
        values = in_ref[...].astype(F32).reshape(rows * depth, width)
        for k in range(width // 128):
            wide[k] = values[:, k * 128 : (k + 1) * 128]

    for c in range(2):
        for k in range(width // 128):
            out_ref[0, c, :, k * 128 : (k + 1) * 128] = wide[
                k, pl.ds(c * (depth // 2) + step, rows, stride=depth), :
            ]


def hilbert_table(bin_total):
    column = jnp.arange(bin_total, dtype=F32)
    difference = column[:, None] - column[None, :]
    second = column[:, None] + column[None, :] + 1.0
    real_part = difference / (difference * difference + 1.0) - second / (second * second + 1.0)
    imag_part = 1.0 / (second * second + 1.0) - 1.0 / (difference * difference + 1.0)
    return (real_part, imag_part)


def split_table(groups, own_bins):
    real, imag = (
        part.reshape(groups, own_bins, groups, own_bins) for part in hilbert_table(NB)
    )
    upper = jnp.stack([real, -imag], axis=3)
    lower = jnp.stack([imag, real], axis=3)
    table = jnp.stack([upper, lower], axis=1).reshape(2 * NB, 2 * NB)
    high = table.astype(BF16)
    low = (table - high.astype(F32)).astype(BF16)
    return high, low


def weight_table(pair_offset, pair_frac, bin_count):
    lower_weight = (1.0 - pair_frac).astype(BF16)
    upper_weight = pair_frac.astype(BF16)
    column = jnp.arange(bin_count, dtype=jnp.int32)
    nothing = jnp.zeros((), BF16)
    lower_part = jnp.where(column[None, :] == pair_offset[:, None], lower_weight[:, None], nothing)
    upper_part = jnp.where(
        column[None, :] == pair_offset[:, None] + 1, upper_weight[:, None], nothing
    )
    return lower_part + upper_part


def from_first(block, axis):
    place = lax.axis_index(axis)
    ahead = lax.ppermute(block, axis, [(0, 3)])
    behind = lax.ppermute(block, axis, [(0, 5)])
    block = jnp.where(place == 3, ahead, jnp.where(place == 5, behind, block))
    ahead = lax.ppermute(block, axis, [(0, 1), (3, 4), (5, 6)])
    behind = lax.ppermute(block, axis, [(0, 7), (3, 2)])
    use_ahead = (place == 1) | (place == 4) | (place == 6)
    use_behind = (place == 7) | (place == 2)
    return jnp.where(use_ahead, ahead, jnp.where(use_behind, behind, block))


def exchange(block):
    return lax.all_to_all(block, "bin", split_axis=0, concat_axis=0, tiled=True)


def on_device(pair_rows, pair_owner, pair_offset, pair_frac):
    groups = lax.axis_size("bin")
    pairs, _, columns = pair_rows.shape
    capacity = 2 * pairs // groups
    slots = groups * capacity
    own_bins = NB // groups
    per = GW // groups
    width = columns // PARTS
    blocks = 4
    shape = jax.ShapeDtypeStruct

    by_part = jnp.swapaxes(pair_rows, 0, 1)
    head = from_first(
        jnp.swapaxes(by_part[:, :, :GW], 0, 1).reshape(pairs, 2 * GW), "gcol"
    )
    target, *packed = call(
        pack_rows_kernel,
        [shape((1, pairs), jnp.int32)]
        + [shape((groups, 2, capacity, width), BF16)] * PARTS,
    )(pair_owner.reshape(1, pairs), by_part)
    weights = weight_table(pair_offset, pair_frac, 128)
    packed_heads = call(pack_heads_kernel, shape((groups, capacity, 2 * GW + 128), BF16))(
        target, head, weights
    )
    got_rows = [None] * PARTS
    got_rows[0] = exchange(packed[0])
    got_heads = exchange(packed_heads)
    for part in range(1, PARTS):
        got_rows[part] = exchange(packed[part])
    high, low = split_table(groups, own_bins)

    turned, got_weights = call(
        turn_kernel, [shape((2 * GW, slots), BF16), shape((16, slots), F32)]
    )(got_heads)

    route = [(i, i + 1) for i in range(groups - 1)]
    whole = lambda *dims: pl.BlockSpec(dims, lambda i: (0,) * len(dims))
    spectral = []
    for part in range(PARTS):
        upper = call(
            functools.partial(upper_kernel, own_bins), shape((2, GW, width), F32)
        )(turned, got_weights, got_rows[part])
        upper = lax.ppermute(upper, "bin", route)
        spectral.append(
            call(
                functools.partial(spectral_kernel, own_bins),
                shape((groups, per, 2 * own_bins, width), BF16),
                grid=(blocks,),
                in_specs=[
                    whole(2 * GW, slots),
                    whole(16, slots),
                    whole(groups, 2, capacity, width),
                    pl.BlockSpec((2, GW // blocks, width), lambda i: (0, i, 0)),
                ],
                out_specs=pl.BlockSpec(
                    (groups // blocks, per, 2 * own_bins, width), lambda i: (i, 0, 0, 0)
                ),
            )(turned, got_weights, got_rows[part], upper)
        )
    spectral = [exchange(block) for block in spectral]
    chi = [
        exchange(call(hilbert_kernel, shape(block.shape, BF16))(high, low, block))
        for block in spectral
    ]
    out = None
    for part in range(PARTS):
        earlier = [] if out is None else [out]
        out = call(
            final_kernel,
            shape((own_bins, 2, GW, columns), F32),
            grid=(own_bins,),
            in_specs=[whole(groups, per, 2 * own_bins, width)]
            + [pl.BlockSpec(memory_space=pl.ANY)] * len(earlier),
            out_specs=pl.BlockSpec((1, 2, GW, width), lambda i, part=part: (i, 0, 0, part)),
            scratch_shapes=[pltpu.VMEM((width // 128, GW * 2 * own_bins, 128), F32)],
            input_output_aliases={1: 0} if earlier else {},
        )(chi[part], *earlier)
    return out


def solution(mesh):
    placed = (P("bin", None, "gcol"), P("bin", None), P("bin"), P("bin"))
    return jax.shard_map(
        on_device,
        mesh=mesh,
        in_specs=placed,
        out_specs=P("bin", None, None, "gcol"),
        check_vma=False,
    )
```

time: 352 us -> 219 us (0.62)
  blocking collectives: 90.1 us -> 17.7 us
  local copies, waits for them, and re-layouts: 95.1 us -> 53 us
  starting transfers between devices: 31.7 us -> 60.2 us
  waiting for transfers between devices: 87.9 us -> 62.8 us
  Pallas kernels: 0 us -> 19.4 us
  matrix products: 15.3 us -> 0 us
  between operations: 13.7 us -> 0.37 us
  other arithmetic: 13.9 us -> 4.01 us
    all_to_all x2 -> x1, blocking collectives: 90.1 us -> 17.7 us  [exchange(): return lax.all_to_all(block, 'bin', split_axis=0, concat_axis=0, tiled=True)]
    scatter x2 -> x0, local copies, waits for them, and re-layouts: 67.2 us -> none  [packed(): jnp.zeros((slot_count,) + values.shape[1:], values.dtype).at[target]]
    psum x1 -> x0, waiting for transfers between devices: 56.1 us -> none  [broadcast(): return lax.psum(jnp.where(mine, shard, jnp.zeros_like(shard)), axis)]
    reshape x3 -> x2, local copies, waits for them, and re-layouts: 2.99 us -> 26.8 us  [the longest x1 26.8 us: split_table(): table = jnp.stack([upper, lower], axis=1).reshape(2 * NB, 2 * NB)]
    ppermute x1 -> x6, waiting for transfers between devices: 5.73 us -> 26.3 us  [the longest x2 20.9 us: on_device(): upper = lax.ppermute(upper, 'bin', route)]
    pallas_call x0 -> x11, Pallas kernels: none -> 19.4 us  [the longest x2 7.21 us: on_device(): call(final_kernel, shape((own_bins, 2, GW, columns), F32), grid=(own_bins...]
    ppermute x1 -> x6, starting transfers between devices: 3.64 us -> 19.6 us  [the longest x1 7.09 us: from_first(): ahead = lax.ppermute(block, axis, [(0, 3)])]
    dot_general x5 -> x0, matrix products: 15.3 us -> none  [the longest x1 6.69 us: spectral_tile(): lax.dot_general(scaled.reshape(slot_count, -1), row_data.reshape(slot_cou...]
  transfers between devices with their start and end apart: 5 -> 12, of which waited for: 3 -> 7; matrix products, arithmetic and copies ran while one was open for 24% -> 23% of each run, Pallas kernels for 0% -> 7%
where the time goes in v1:
time: 219 us; the launch traced here: 218 us
  waiting for transfers between devices  62.8 us (29%)
  starting transfers between devices  60.2 us (27%)
  local copies, waits for them, and re-layouts  53 us (24%)
  Pallas kernels  19.4 us (9%)
  blocking collectives  17.7 us (8%)
  other arithmetic  4.01 us (2%)
    all_to_all x6, starting transfers between devices, exchange(): return lax.all_to_all(block, 'bin', split_axis=0, concat_axis=0, tiled=True)  40.6 us
    all_to_all x6, waiting for transfers between devices, exchange(): return lax.all_to_all(block, 'bin', split_axis=0, concat_axis=0, tiled=True)  36.5 us
    reshape x1, local copies, waits for them, and re-layouts, split_table(): table = jnp.stack([upper, lower], axis=1).reshape(2 * NB, 2 * NB)  26.8 us
    ppermute x2, waiting for transfers between devices, on_device(): upper = lax.ppermute(upper, 'bin', route)  20.9 us
    another operation x1, local copies, waits for them, and re-layouts, split_table(): table = jnp.stack([upper, lower], axis=1).reshape(2 * NB, 2 * NB)  18.8 us
    all_to_all x1, blocking collectives, exchange(): return lax.all_to_all(block, 'bin', split_axis=0, concat_axis=0, tiled=True)  17.7 us
    unnamed x21, local copies, waits for them, and re-layouts  7.33 us
    pallas_call x2, Pallas kernels, on_device(): call(final_kernel, shape((own_bins, 2, GW, columns), F32), grid=(own_bins...  7.21 us
  transfers between devices with their start and end apart: 12, of which 7 were waited for; matrix products, arithmetic and copies ran while one was open for 23% of the time, Pallas kernels for 7%

profile of v1, /device:TPU:1, one launch (start us, length us, event | category | flops | bytes accessed | tf_op | source)
XLA Modules:
  0.0 217.5 jit_solution(4833390780686668825)
XLA Ops:
  0.0 1.4 copy.27
  1.5 7.1 %collective-permute-start = (bf16[512,256]{1,0:T(8,128)(2,1)S(1)}, bf16[512,256]{1,0:T(8,128)(2,1)S(1)}, u32[]{:S(2)}, u32[]{:S(2)}) collective-permute-start(bf16[512,256]{1,0:T(8,128)(2,1)S(1)} %copy_bitcast_fusion.1), channel_id=1, source_target_pairs={{0,3},{8,11},{16,19},{24,27},{32,35},{40,43},{48,51},{56,59},{64,6... | collective-permute-start | bytes 786440 | tf_op jit(solution)/shard_map/ppermute | solution.py:183
  8.6 2.8 %collective-permute-start.1 = (bf16[512,256]{1,0:T(8,128)(2,1)S(1)}, bf16[512,256]{1,0:T(8,128)(2,1)S(1)}, u32[]{:S(2)}, u32[]{:S(2)}) collective-permute-start(bf16[512,256]{1,0:T(8,128)(2,1)S(1)} %copy_bitcast_fusion.1), channel_id=1, source_target_pairs={{0,5},{8,13},{16,21},{24,29},{32,37},{40,45},{48,53},{56,61},{64,6... | collective-permute-start | bytes 786440 | tf_op jit(solution)/shard_map/ppermute | solution.py:184
  11.4 1.9 shard_map.46
  14.2 8.0 %all-to-all-start.4 = ((bf16[32,2,32,256]{3,2,1,0:T(8,128)(2,1)}), bf16[32,2,32,256]{3,2,1,0:T(8,128)(2,1)S(1)}, u32[]{:S(2)}, u32[]{:S(2)}) async-start(bf16[32,2,32,256]{3,2,1,0:T(8,128)(2,1)} %get-tuple-element.14), calls=%async_computation.4 | async-start | bytes 2097152 | tf_op jit(solution)/shard_map/all_to_all | solution.py:194
  22.4 1.3 collective-permute-start.2
  23.7 1.3 collective-permute-start.3
  25.4 4.1 %collective-permute-done.2 = bf16[512,256]{1,0:T(8,128)(2,1)S(1)} collective-permute-done((bf16[512,256]{1,0:T(8,128)(2,1)S(1)}, bf16[512,256]{1,0:T(8,128)(2,1)S(1)}, u32[]{:S(2)}, u32[]{:S(2)}) %collective-permute-start.2) | collective-permute-done | bytes 262176 | tf_op jit(solution)/shard_map/ppermute | solution.py:186
  29.5 1.3 collective-permute-done.3
  31.6 7.9 %all-to-all-done.4.rows_ref = bf16[32,2,32,256]{3,2,1,0:T(8,128)(2,1)S(1)} async-done(((bf16[32,2,32,256]{3,2,1,0:T(8,128)(2,1)}), bf16[32,2,32,256]{3,2,1,0:T(8,128)(2,1)S(1)}, u32[]{:S(2)}, u32[]{:S(2)}) %all-to-all-start.4) | async-done | bytes 1048608 | tf_op jit(solution)/shard_map/all_to_all | solution.py:194
  39.4 17.7 %all_to_all.35.in_ref = bf16[32,32,384]{2,1,0:T(8,128)(2,1)S(1)} all-to-all(bf16[32,32,384]{2,1,0:T(8,128)(2,1)S(1)} %shard_map.47), channel_id=1, replica_groups=mesh['bin'=32,'gcol'=8] {'bin'}, dimensions={0} | all-to-all | bytes 1572864 | tf_op jit(solution)/shard_map/all_to_all | solution.py:194
  57.2 4.2 %all-to-all-start.1 = ((bf16[32,2,32,256]{3,2,1,0:T(8,128)(2,1)}), bf16[32,2,32,256]{3,2,1,0:T(8,128)(2,1)S(1)}, u32[]{:S(2)}, u32[]{:S(2)}) async-start(bf16[32,2,32,256]{3,2,1,0:T(8,128)(2,1)} %copy-done.6), calls=%async_computation.1 | async-start | bytes 2097152 | tf_op jit(solution)/shard_map/all_to_all | solution.py:194
  62.1 3.5 %collective-permute-start.5 = (f32[2,128,256]{2,1,0:T(8,128)S(1)}, f32[2,128,256]{2,1,0:T(8,128)S(1)}, u32[]{:S(2)}, u32[]{:S(2)}) collective-permute-start(f32[2,128,256]{2,1,0:T(8,128)S(1)} %shard_map.52), channel_id=1, source_target_pairs={{0,8},{8,16},{16,24},{24,32},{32,40},{40,48},{48,56},{56,64},{64,7... | collective-permute-start | bytes 786440 | tf_op jit(solution)/shard_map/ppermute | solution.py:239
  65.6 10.4 %collective-permute-done.5.upper_ref = f32[2,128,256]{2,1,0:T(8,128)S(1)} collective-permute-done((f32[2,128,256]{2,1,0:T(8,128)S(1)}, f32[2,128,256]{2,1,0:T(8,128)S(1)}, u32[]{:S(2)}, u32[]{:S(2)}) %collective-permute-start.5) | collective-permute-done | bytes 262176 | tf_op jit(solution)/shard_map/ppermute | solution.py:239
  76.0 3.0 %shard_map.53 = bf16[32,4,16,256]{3,2,1,0:T(8,128)(2,1)S(1)} custom-call(bf16[256,1024]{1,0:T(8,128)(2,1)S(1)} %get-tuple-element.11.head_ref, f32[16,1024]{1,0:T(8,128)S(1)} %get-tuple-element.12.weight_ref, bf16[32,2,32,256]{3,2,1,0:T(8,128)(2,1)S(1)} %all-to-all-done.4.rows_ref, f32[2,128,256]{2,1,0:T(8,128)S(1)} %collective-permute-done.5.upper_ref), custom_call_target="tpu_custom_call" | custom-call | tf_op jit(solution)/shard_map/pallas_call | solution.py:241
  80.0 8.6 %all-to-all-start.5 = ((bf16[32,4,16,256]{3,2,1,0:T(8,128)(2,1)}), bf16[32,4,16,256]{3,2,1,0:T(8,128)(2,1)S(1)}, u32[]{:S(2)}, u32[]{:S(2)}) async-start(bf16[32,4,16,256]{3,2,1,0:T(8,128)(2,1)} %copy-done.3), calls=%async_computation.5 | async-start | bytes 2097152 | tf_op jit(solution)/shard_map/all_to_all | solution.py:194
  89.0 3.5 %collective-permute-start.4 = (f32[2,128,256]{2,1,0:T(8,128)S(1)}, f32[2,128,256]{2,1,0:T(8,128)S(1)}, u32[]{:S(2)}, u32[]{:S(2)}) collective-permute-start(f32[2,128,256]{2,1,0:T(8,128)S(1)} %shard_map.49), channel_id=1, source_target_pairs={{0,8},{8,16},{16,24},{24,32},{32,40},{40,48},{48,56},{56,64},{64,7... | collective-permute-start | bytes 786440 | tf_op jit(solution)/shard_map/ppermute | solution.py:239
  92.6 10.6 %collective-permute-done.4.upper_ref = f32[2,128,256]{2,1,0:T(8,128)S(1)} collective-permute-done((f32[2,128,256]{2,1,0:T(8,128)S(1)}, f32[2,128,256]{2,1,0:T(8,128)S(1)}, u32[]{:S(2)}, u32[]{:S(2)}) %collective-permute-start.4) | collective-permute-done | bytes 262176 | tf_op jit(solution)/shard_map/ppermute | solution.py:239
  103.2 3.0 %shard_map.50 = bf16[32,4,16,256]{3,2,1,0:T(8,128)(2,1)S(1)} custom-call(bf16[256,1024]{1,0:T(8,128)(2,1)S(1)} %get-tuple-element.11.head_ref, f32[16,1024]{1,0:T(8,128)S(1)} %get-tuple-element.12.weight_ref, bf16[32,2,32,256]{3,2,1,0:T(8,128)(2,1)S(1)} %all-to-all-done.1.rows_ref, f32[2,128,256]{2,1,0:T(8,128)S(1)} %collective-permute-done.4.upper_ref), custom_call_target="tpu_custom_call" | custom-call | tf_op jit(solution)/shard_map/pallas_call | solution.py:241
  107.2 8.5 %all-to-all-start.2 = ((bf16[32,4,16,256]{3,2,1,0:T(8,128)(2,1)}), bf16[32,4,16,256]{3,2,1,0:T(8,128)(2,1)S(1)}, u32[]{:S(2)}, u32[]{:S(2)}) async-start(bf16[32,4,16,256]{3,2,1,0:T(8,128)(2,1)} %copy-done.2), calls=%async_computation.2 | async-start | bytes 2097152 | tf_op jit(solution)/shard_map/all_to_all | solution.py:194
  116.7 2.4 %pad_maximum_fusion = f32[32,2,8,32,2,8]{3,5,4,2,0,1:T(8,128)} fusion(f32[32,1,8,32,2,8]{3,5,4,2,0,1:T(8,128)S(1)} %get-tuple-element.18, f32[32,1,8,32,2,8]{3,5,4,2,0,1:T(8,128)S(1)} %get-tuple-element.17), kind=kLoop, calls=%fused_computation | loop fusion | flops 262144 | bytes 2097152 | tf_op jit(solution)/shard_map/stack | solution.py:163
  119.0 18.8 %copy.19 = f32[32,2,8,32,2,8]{5,4,3,2,1,0:T(2,128)} copy(f32[32,2,8,32,2,8]{3,5,4,2,0,1:T(8,128)} %pad_maximum_fusion) | data formatting | bytes 2097152 | tf_op jit(solution)/shard_map/stack | solution.py:163
  137.8 26.8 %reshape.129 = f32[512,512]{1,0:T(8,128)S(1)} reshape(f32[32,2,8,32,2,8]{5,4,3,2,1,0:T(2,128)} %copy.19) | data formatting | bytes 2097152 | tf_op jit(solution)/shard_map/reshape | solution.py:163
  164.8 1.1 copy-done.1
  165.9 1.2 shard_map.54
  168.1 7.4 %all-to-all-start.6 = ((bf16[32,4,16,256]{3,2,1,0:T(8,128)(2,1)}), bf16[32,4,16,256]{3,2,1,0:T(8,128)(2,1)S(1)}, u32[]{:S(2)}, u32[]{:S(2)}) async-start(bf16[32,4,16,256]{3,2,1,0:T(8,128)(2,1)} %copy-done.4), calls=%async_computation.6 | async-start | bytes 2097152 | tf_op jit(solution)/shard_map/all_to_all | solution.py:194
  175.5 1.2 shard_map.51
  177.7 14.9 %all-to-all-done.6.in_ref = bf16[32,4,16,256]{3,2,1,0:T(8,128)(2,1)S(1)} async-done(((bf16[32,4,16,256]{3,2,1,0:T(8,128)(2,1)}), bf16[32,4,16,256]{3,2,1,0:T(8,128)(2,1)S(1)}, u32[]{:S(2)}, u32[]{:S(2)}) %all-to-all-start.6) | async-done | bytes 1048608 | tf_op jit(solution)/shard_map/all_to_all | solution.py:194
  192.7 4.0 %all-to-all-start.3 = ((bf16[32,4,16,256]{3,2,1,0:T(8,128)(2,1)}), bf16[32,4,16,256]{3,2,1,0:T(8,128)(2,1)S(1)}, u32[]{:S(2)}, u32[]{:S(2)}) async-start(bf16[32,4,16,256]{3,2,1,0:T(8,128)(2,1)} %copy-done.5), calls=%async_computation.3 | async-start | bytes 2097152 | tf_op jit(solution)/shard_map/all_to_all | solution.py:194
  196.6 3.6 %shard_map.55.refs_0_ = f32[8,2,128,512]{3,2,1,0:T(8,128)} custom-call(bf16[32,4,16,256]{3,2,1,0:T(8,128)(2,1)S(1)} %all-to-all-done.6.in_ref), custom_call_target="tpu_custom_call" | custom-call | tf_op jit(solution)/shard_map/pallas_call | solution.py:264
  200.3 13.7 %all-to-all-done.3.in_ref = bf16[32,4,16,256]{3,2,1,0:T(8,128)(2,1)S(1)} async-done(((bf16[32,4,16,256]{3,2,1,0:T(8,128)(2,1)}), bf16[32,4,16,256]{3,2,1,0:T(8,128)(2,1)S(1)}, u32[]{:S(2)}, u32[]{:S(2)}) %all-to-all-start.3) | async-done | bytes 1048608 | tf_op jit(solution)/shard_map/all_to_all | solution.py:194
  213.9 3.6 %shard_map.56 = f32[8,2,128,512]{3,2,1,0:T(8,128)} custom-call(bf16[32,4,16,256]{3,2,1,0:T(8,128)(2,1)S(1)} %all-to-all-done.3.in_ref, f32[8,2,128,512]{3,2,1,0:T(8,128)} %shard_map.55.refs_0_), custom_call_target="tpu_custom_call", output_to_operand_aliasing={{}: (1, {})} | custom-call | tf_op jit(solution)/shard_map/pallas_call | solution.py:264
  (39 shorter events, 8.5 us)
Async XLA Ops:
  0.0 11.4 %copy-start.7 = (s32[512,1]{0,1:T(1,128)S(1)}, s32[512,1]{0,1:T(1,128)}, u32[]{:S(2)}) copy-start(s32[512,1]{0,1:T(1,128)} %param.5) | copy-start | bytes 6148
  1.4 20.9 %copy-start.8 = (s32[512]{0:T(512)S(1)}, s32[512]{0:T(512)}, u32[]{:S(2)}) copy-start(s32[512]{0:T(512)} %param.6) | copy-start | bytes 6148
  1.5 20.8 %collective-permute-start = (bf16[512,256]{1,0:T(8,128)(2,1)S(1)}, bf16[512,256]{1,0:T(8,128)(2,1)S(1)}, u32[]{:S(2)}, u32[]{:S(2)}) collective-permute-start(bf16[512,256]{1,0:T(8,128)(2,1)S(1)} %copy_bitcast_fusion.1), channel_id=1, source_target_pairs={{0,3},{8,11},{16,19},{24,27},{32,35},{40,43},{48,51},{56,59},{64,6... | collective-permute-start | bytes 786440 | tf_op jit(solution)/shard_map/ppermute | solution.py:183
  8.6 13.7 %collective-permute-start.1 = (bf16[512,256]{1,0:T(8,128)(2,1)S(1)}, bf16[512,256]{1,0:T(8,128)(2,1)S(1)}, u32[]{:S(2)}, u32[]{:S(2)}) collective-permute-start(bf16[512,256]{1,0:T(8,128)(2,1)S(1)} %copy_bitcast_fusion.1), channel_id=1, source_target_pairs={{0,5},{8,13},{16,21},{24,29},{32,37},{40,45},{48,53},{56,61},{64,6... | collective-permute-start | bytes 786440 | tf_op jit(solution)/shard_map/ppermute | solution.py:184
  11.4 13.7 %copy-start.9 = (f32[512]{0:T(512)S(1)}, f32[512]{0:T(512)}, u32[]{:S(2)}) copy-start(f32[512]{0:T(512)} %param.7) | copy-start | bytes 6148
  13.3 1.0 copy-start.6
  14.2 25.2 %all-to-all-start.4 = ((bf16[32,2,32,256]{3,2,1,0:T(8,128)(2,1)}), bf16[32,2,32,256]{3,2,1,0:T(8,128)(2,1)S(1)}, u32[]{:S(2)}, u32[]{:S(2)}) async-start(bf16[32,2,32,256]{3,2,1,0:T(8,128)(2,1)} %get-tuple-element.14), calls=%async_computation.4 | async-start | bytes 2097152 | tf_op jit(solution)/shard_map/all_to_all | solution.py:194
  22.4 7.1 %collective-permute-start.2 = (bf16[512,256]{1,0:T(8,128)(2,1)S(1)}, bf16[512,256]{1,0:T(8,128)(2,1)S(1)}, u32[]{:S(2)}, u32[]{:S(2)}) collective-permute-start(bf16[512,256]{1,0:T(8,128)(2,1)S(1)} %select_select_fusion.1), channel_id=1, source_target_pairs={{0,1},{3,4},{5,6},{8,9},{11,12},{13,14},{16,17},{19,20},{21,22},{2... | collective-permute-start | bytes 786440 | tf_op jit(solution)/shard_map/ppermute | solution.py:186
  23.7 7.1 %collective-permute-start.3 = (bf16[512,256]{1,0:T(8,128)(2,1)S(1)}, bf16[512,256]{1,0:T(8,128)(2,1)S(1)}, u32[]{:S(2)}, u32[]{:S(2)}) collective-permute-start(bf16[512,256]{1,0:T(8,128)(2,1)S(1)} %select_select_fusion.1), channel_id=1, source_target_pairs={{0,7},{3,2},{8,15},{11,10},{16,23},{19,18},{24,31},{27,26},{32,39}... | collective-permute-start | bytes 786440 | tf_op jit(solution)/shard_map/ppermute | solution.py:187
  57.2 22.8 %all-to-all-start.1 = ((bf16[32,2,32,256]{3,2,1,0:T(8,128)(2,1)}), bf16[32,2,32,256]{3,2,1,0:T(8,128)(2,1)S(1)}, u32[]{:S(2)}, u32[]{:S(2)}) async-start(bf16[32,2,32,256]{3,2,1,0:T(8,128)(2,1)} %copy-done.6), calls=%async_computation.1 | async-start | bytes 2097152 | tf_op jit(solution)/shard_map/all_to_all | solution.py:194
  62.1 13.9 %collective-permute-start.5 = (f32[2,128,256]{2,1,0:T(8,128)S(1)}, f32[2,128,256]{2,1,0:T(8,128)S(1)}, u32[]{:S(2)}, u32[]{:S(2)}) collective-permute-start(f32[2,128,256]{2,1,0:T(8,128)S(1)} %shard_map.52), channel_id=1, source_target_pairs={{0,8},{8,16},{16,24},{24,32},{32,40},{40,48},{48,56},{56,64},{64,7... | collective-permute-start | bytes 786440 | tf_op jit(solution)/shard_map/ppermute | solution.py:239
  79.0 1.0 copy-start.3
  80.0 27.2 %all-to-all-start.5 = ((bf16[32,4,16,256]{3,2,1,0:T(8,128)(2,1)}), bf16[32,4,16,256]{3,2,1,0:T(8,128)(2,1)S(1)}, u32[]{:S(2)}, u32[]{:S(2)}) async-start(bf16[32,4,16,256]{3,2,1,0:T(8,128)(2,1)} %copy-done.3), calls=%async_computation.5 | async-start | bytes 2097152 | tf_op jit(solution)/shard_map/all_to_all | solution.py:194
  89.0 14.2 %collective-permute-start.4 = (f32[2,128,256]{2,1,0:T(8,128)S(1)}, f32[2,128,256]{2,1,0:T(8,128)S(1)}, u32[]{:S(2)}, u32[]{:S(2)}) collective-permute-start(f32[2,128,256]{2,1,0:T(8,128)S(1)} %shard_map.49), channel_id=1, source_target_pairs={{0,8},{8,16},{16,24},{24,32},{32,40},{40,48},{48,56},{56,64},{64,7... | collective-permute-start | bytes 786440 | tf_op jit(solution)/shard_map/ppermute | solution.py:239
  106.2 1.0 copy-start.2
  107.2 9.1 %copy-start = (bf16[32,4,16,256]{3,2,1,0:T(8,128)(2,1)}, bf16[32,4,16,256]{3,2,1,0:T(8,128)(2,1)S(1)}, u32[]{:S(2)}) copy-start(bf16[32,4,16,256]{3,2,1,0:T(8,128)(2,1)S(1)} %all-to-all-done.5.in_ref) | copy-start | bytes 3145732
  107.2 60.9 %all-to-all-start.2 = ((bf16[32,4,16,256]{3,2,1,0:T(8,128)(2,1)}), bf16[32,4,16,256]{3,2,1,0:T(8,128)(2,1)S(1)}, u32[]{:S(2)}, u32[]{:S(2)}) async-start(bf16[32,4,16,256]{3,2,1,0:T(8,128)(2,1)} %copy-done.2), calls=%async_computation.2 | async-start | bytes 2097152 | tf_op jit(solution)/shard_map/all_to_all | solution.py:194
  164.6 1.2 copy-start.1
  167.1 1.0 copy-start.4
  168.1 24.6 %all-to-all-start.6 = ((bf16[32,4,16,256]{3,2,1,0:T(8,128)(2,1)}), bf16[32,4,16,256]{3,2,1,0:T(8,128)(2,1)S(1)}, u32[]{:S(2)}, u32[]{:S(2)}) async-start(bf16[32,4,16,256]{3,2,1,0:T(8,128)(2,1)} %copy-done.4), calls=%async_computation.6 | async-start | bytes 2097152 | tf_op jit(solution)/shard_map/all_to_all | solution.py:194
  176.7 1.0 copy-start.5
  192.7 21.3 %all-to-all-start.3 = ((bf16[32,4,16,256]{3,2,1,0:T(8,128)(2,1)}), bf16[32,4,16,256]{3,2,1,0:T(8,128)(2,1)S(1)}, u32[]{:S(2)}, u32[]{:S(2)}) async-start(bf16[32,4,16,256]{3,2,1,0:T(8,128)(2,1)} %copy-done.5), calls=%async_computation.3 | async-start | bytes 2097152 | tf_op jit(solution)/shard_map/all_to_all | solution.py:194

commit v2 on v1

v2 whole, which is shorter than its diff:
```python
import functools

import jax
import jax.numpy as jnp
from jax import lax
from jax.experimental import pallas as pl
from jax.experimental.pallas import tpu as pltpu
from jax.sharding import PartitionSpec as P

NB = 256
GW = 128
BF16 = jnp.bfloat16
F32 = jnp.float32
VMEM_BYTES = 24 * 1024 * 1024


def dot(a, b):
    return jnp.dot(a, b, preferred_element_type=F32)


def iota(shape, axis):
    return lax.broadcasted_iota(jnp.int32, shape, axis)


def call(kernel, out_shape, **options):
    return pl.pallas_call(
        kernel,
        out_shape=out_shape,
        compiler_params=pltpu.CompilerParams(vmem_limit_bytes=VMEM_BYTES),
        **options,
    )


def pack_kernel(quarter_ref, owner_ref, offset_ref, frac_ref, rows_ref, first_ref, rest_ref):
    groups, _, capacity, _ = rest_ref.shape
    lanes = first_ref.shape[2]
    extra = first_ref.shape[1] - 2 * capacity
    pairs = owner_ref.shape[1]
    owner = owner_ref[...]
    named = (iota((groups, pairs), 0) == owner).astype(F32)
    before = (iota((pairs, pairs), 0) < iota((pairs, pairs), 1)).astype(F32).astype(BF16)
    rank = jnp.sum(dot(named.astype(BF16), before) * named, axis=0, keepdims=True)
    target = owner * capacity + rank.astype(jnp.int32)
    onehot = (iota((groups * capacity, pairs), 0) == target).astype(F32).astype(BF16)
    for c in range(2):
        packed = dot(onehot, rows_ref[c]).astype(BF16).reshape(groups, capacity, -1)
        first_ref[:, c * capacity : (c + 1) * capacity] = packed[:, :, :lanes]
        rest_ref[:, c] = packed[:, :, lanes:]

    frac = frac_ref[...]
    place = iota((extra, pairs), 0)
    weight = jnp.where(place == offset_ref[...], (1.0 - frac).astype(BF16).astype(F32), 0.0)
    weight += jnp.where(place == offset_ref[...] + 1, frac.astype(BF16).astype(F32), 0.0)
    weight = lax.dot_general(
        weight.astype(BF16), onehot, (((1,), (1,)), ((), ())), preferred_element_type=F32
    )
    share = lanes // capacity
    quarter = quarter_ref[0]
    mine = iota((extra, lanes), 1) // capacity == quarter
    for group in range(groups):
        tile = weight[:, group // share * lanes : (group // share + 1) * lanes]
        turn = (quarter + share - group % share) % share * capacity
        tile = jnp.where(mine, pltpu.roll(tile, turn, 1), 0.0)
        first_ref[group, 2 * capacity :] = tile.astype(BF16)


def turn_kernel(own_bins, use_ref, got_ref, *refs):
    heads = refs[:3]
    head_ref, weight_ref, high_ref, low_ref = refs[3:]
    groups, double, lanes = heads[0].shape
    capacity = double // 2
    share = lanes // capacity
    for choice, source in enumerate(heads):

        @pl.when(use_ref[0] == choice)
        def _(source=source):
            for c in range(2):
                part = source[:, c * capacity : (c + 1) * capacity]
                part = part.reshape(groups * capacity, lanes).astype(F32)
                head_ref[c * lanes : (c + 1) * lanes] = part.T.astype(BF16)

    for at in range(groups // share):
        tile = got_ref[share * at, double:].astype(F32)
        for k in range(1, share):
            tile += got_ref[share * at + k, double:].astype(F32)
        weight_ref[:, at * lanes : (at + 1) * lanes] = tile
    table_kernel(own_bins, high_ref, low_ref)


def complex_dot(left, right):
    real = dot(left[0], right[0]) + dot(left[1], right[1])
    imag = dot(left[0], right[1]) - dot(left[1], right[0])
    return real, imag


def spectral_kernel(own_bins, head_ref, weight_ref, first_ref, rest_ref, out_ref, rows):
    groups, _, capacity, _ = rest_ref.shape
    lanes = first_ref.shape[2]
    chunk, depth, width = out_ref.shape
    bins = 2 * own_bins
    per = depth // (bins + 2)
    window = chunk * per
    slots = weight_ref.shape[1]
    at = pl.program_id(0) * window

    @pl.when(pl.program_id(0) == 0)
    def _():
        for c in range(2):
            first = first_ref[:, c * capacity : (c + 1) * capacity]
            rows[c, :, :lanes] = first.reshape(groups * capacity, lanes)
            rows[c, :, lanes:] = rest_ref[:, c].reshape(groups * capacity, -1)

    lower, upper = [], []
    for c in range(2):
        head = head_ref[pl.ds(pl.multiple_of(c * GW + at, window), window)].astype(F32)
        scaled = (head[:, None, :] * weight_ref[:own_bins][None]).astype(BF16)
        lower.append(scaled.reshape(window * own_bins, slots))
        upper.append((head * weight_ref[own_bins : own_bins + 1]).astype(BF16))
    result = [part.reshape(window, own_bins, width) for part in complex_dot(lower, rows)]
    result = jnp.concatenate(result, axis=1).reshape(chunk, per * bins, width)
    extra = [part.reshape(chunk, per, width) for part in complex_dot(upper, rows)]
    out_ref[...] = jnp.concatenate([result] + extra, axis=1).astype(BF16)


def hilbert_kernel(own_bins, high_ref, low_ref, in_ref, out_ref):
    groups, per, bins, width = out_ref.shape
    extra = in_ref[: groups - 1, per * bins :].astype(F32)
    place = iota((groups, bins, width), 1)
    for g in range(per):
        values = in_ref[:, g * bins : (g + 1) * bins].astype(F32)
        for c in range(2):
            at = c * per + g
            behind = jnp.concatenate(
                [jnp.zeros((1, 1, width), F32), extra[:, at : at + 1]], axis=0
            )
            values = values + jnp.where(place == c * own_bins, behind, 0.0)
        values = values.astype(BF16).reshape(groups * bins, width)
        result = dot(high_ref[...], values) + dot(low_ref[...], values)
        out_ref[:, g] = result.astype(BF16).reshape(groups, bins, width)


def final_kernel(in_ref, *refs):
    out_ref, wide = refs[-2:]
    step = pl.program_id(0)
    own_bins = pl.num_programs(0)
    rows = in_ref.shape[0] * in_ref.shape[1]
    depth, width = in_ref.shape[2:]

    @pl.when(step == 0)
    def _():
        values = in_ref[...].astype(F32).reshape(rows * depth, width)
        for k in range(width // 128):
            wide[k] = values[:, k * 128 : (k + 1) * 128]

    for c in range(2):
        for k in range(width // 128):
            out_ref[0, c, :, k * 128 : (k + 1) * 128] = wide[
                k, pl.ds(c * (depth // 2) + step, rows, stride=depth), :
            ]


def table_kernel(own_bins, high_ref, low_ref):
    shape = high_ref.shape
    row = iota(shape, 0)
    column = iota(shape, 1)
    group = 2 * own_bins
    frequency = (row // group * own_bins + row % own_bins).astype(F32)
    bin_at = (column // group * own_bins + column % own_bins).astype(F32)
    row_imag = row // own_bins % 2 == 1
    column_imag = column // own_bins % 2 == 1
    difference = frequency - bin_at
    second = frequency + bin_at + 1.0
    first_scale = 1.0 / (difference * difference + 1.0)
    second_scale = 1.0 / (second * second + 1.0)
    real_part = difference * first_scale - second * second_scale
    imag_part = second_scale - first_scale
    crossed = jnp.where(row_imag, imag_part, -imag_part)
    table = jnp.where(row_imag == column_imag, real_part, crossed)
    high = table.astype(BF16)
    high_ref[...] = high
    low_ref[...] = (table - high.astype(F32)).astype(BF16)


def from_first(block, axis):
    place = lax.axis_index(axis)
    ahead = lax.ppermute(block, axis, [(0, 3)])
    behind = lax.ppermute(block, axis, [(0, 5)])
    block = jnp.where(place == 3, ahead, jnp.where(place == 5, behind, block))
    ahead = lax.ppermute(block, axis, [(0, 1), (3, 4), (5, 6)])
    behind = lax.ppermute(block, axis, [(0, 7), (3, 2)])
    use_ahead = (place == 1) | (place == 4) | (place == 6)
    use_behind = (place == 7) | (place == 2)
    use = jnp.where(use_ahead, 1, jnp.where(use_behind, 2, 0))
    return use.reshape(1), (block, ahead, behind)


def exchange(block):
    return lax.all_to_all(block, "bin", split_axis=0, concat_axis=0, tiled=True)


def on_device(pair_rows, pair_owner, pair_offset, pair_frac):
    groups = lax.axis_size("bin")
    pairs, _, columns = pair_rows.shape
    capacity = 2 * pairs // groups
    slots = groups * capacity
    own_bins = NB // groups
    per = GW // groups
    blocks = 4
    shape = jax.ShapeDtypeStruct
    scalar = pl.BlockSpec(memory_space=pltpu.SMEM)
    here = pl.BlockSpec(memory_space=pltpu.VMEM)

    quarter = lax.axis_index("bin") % (GW // capacity)
    first, rest = call(
        pack_kernel,
        [
            shape((groups, 2 * capacity + 16, GW), BF16),
            shape((groups, 2, capacity, columns - GW), BF16),
        ],
        in_specs=[scalar] + [here] * 4,
    )(
        quarter.reshape(1),
        pair_owner.reshape(1, pairs),
        pair_offset.reshape(1, pairs),
        pair_frac.reshape(1, pairs),
        jnp.swapaxes(pair_rows, 0, 1),
    )
    first = exchange(first)
    rest = exchange(rest)
    use, heads = from_first(first[:, : 2 * capacity], "gcol")
    head, weight, high, low = call(
        functools.partial(turn_kernel, own_bins),
        [
            shape((2 * GW, slots), BF16),
            shape((16, slots), F32),
            shape((2 * NB, 2 * NB), BF16),
            shape((2 * NB, 2 * NB), BF16),
        ],
        in_specs=[scalar] + [here] * 4,
    )(use, first, *heads)

    whole = lambda *dims: pl.BlockSpec(dims, lambda i: (0,) * len(dims))
    depth = per * (2 * own_bins + 2)
    spectral = call(
        functools.partial(spectral_kernel, own_bins),
        shape((groups, depth, columns), BF16),
        grid=(blocks,),
        in_specs=[
            whole(2 * GW, slots),
            whole(16, slots),
            whole(*first.shape),
            whole(*rest.shape),
        ],
        out_specs=pl.BlockSpec((groups // blocks, depth, columns), lambda i: (i, 0, 0)),
        scratch_shapes=[pltpu.VMEM((2, slots, columns), BF16)],
    )(head, weight, first, rest)
    chi = call(
        functools.partial(hilbert_kernel, own_bins),
        shape((groups, per, 2 * own_bins, columns), BF16),
    )(high, low, exchange(spectral))
    chi = exchange(chi)
    return call(
        final_kernel,
        shape((own_bins, 2, GW, columns), F32),
        grid=(own_bins,),
        in_specs=[whole(groups, per, 2 * own_bins, columns)],
        out_specs=pl.BlockSpec((1, 2, GW, columns), lambda i: (i, 0, 0, 0)),
        scratch_shapes=[pltpu.VMEM((columns // 128, GW * 2 * own_bins, 128), F32)],
    )(chi)


def solution(mesh):
    placed = (P("bin", None, "gcol"), P("bin", None), P("bin"), P("bin"))
    return jax.shard_map(
        on_device,
        mesh=mesh,
        in_specs=placed,
        out_specs=P("bin", None, None, "gcol"),
        check_vma=False,
    )
```

time: 219 us -> 158 us (0.72)
  blocking collectives: 17.7 us -> 93.5 us
  local copies, waits for them, and re-layouts: 53 us -> 6.08 us
  waiting for transfers between devices: 62.8 us -> 19.7 us
  starting transfers between devices: 60.2 us -> 18.1 us
  other arithmetic: 4.01 us -> 0.08 us
    all_to_all x1 -> x3, blocking collectives: 17.7 us -> 93.5 us  [exchange(): return lax.all_to_all(block, 'bin', split_axis=0, concat_axis=0, tiled=True)]
    all_to_all x6 -> x1, waiting for transfers between devices: 36.5 us -> 0.01 us  [exchange(): return lax.all_to_all(block, 'bin', split_axis=0, concat_axis=0, tiled=True)]
    all_to_all x6 -> x1, starting transfers between devices: 40.6 us -> 4.17 us  [exchange(): return lax.all_to_all(block, 'bin', split_axis=0, concat_axis=0, tiled=True)]
    reshape x2 -> x0, local copies, waits for them, and re-layouts: 26.8 us -> none  [the longest x1 26.8 us: split_table(): table = jnp.stack([upper, lower], axis=1).reshape(2 * NB, 2 * NB)]
    ppermute x2 -> x0, waiting for transfers between devices: 20.9 us -> none  [on_device(): upper = lax.ppermute(upper, 'bin', route)]
    another operation x1 -> x0, local copies, waits for them, and re-layouts: 18.8 us -> none  [split_table(): table = jnp.stack([upper, lower], axis=1).reshape(2 * NB, 2 * NB)]
    ppermute x1, waiting for transfers between devices: 0.01 us -> 8.82 us  [from_first(): behind = lax.ppermute(block, axis, [(0, 5)])]
    ppermute x2 -> x0, starting transfers between devices: 7.08 us -> none  [on_device(): upper = lax.ppermute(upper, 'bin', route)]
  transfers between devices with their start and end apart: 12 -> 5, of which waited for: 7 -> 4; matrix products, arithmetic and copies ran while one was open for 23% -> 0% of each run, Pallas kernels for 7% -> 1%
where the time goes in v2:
time: 158 us; the launch traced here: 156 us
  blocking collectives  93.5 us (59%)
  waiting for transfers between devices  19.7 us (12%)
  Pallas kernels  18.9 us (12%)
  starting transfers between devices  18.1 us (11%)
  local copies, waits for them, and re-layouts  6.08 us (4%)
    all_to_all x3, blocking collectives, exchange(): return lax.all_to_all(block, 'bin', split_axis=0, concat_axis=0, tiled=True)  93.5 us
    ppermute x1, waiting for transfers between devices, from_first(): behind = lax.ppermute(block, axis, [(0, 5)])  8.82 us
    ppermute x1, starting transfers between devices, from_first(): behind = lax.ppermute(block, axis, [(0, 5)])  8.4 us
    ppermute x1, waiting for transfers between devices, from_first(): behind = lax.ppermute(block, axis, [(0, 7), (3, 2)])  8.19 us
    pallas_call x1, Pallas kernels, on_device(): call(functools.partial(spectral_kernel, own_bins), shape((groups, depth,...  8 us
    unnamed x21, local copies, waits for them, and re-layouts  6.02 us
    pallas_call x1, Pallas kernels, on_device(): call(final_kernel, shape((own_bins, 2, GW, columns), F32), grid=(own_bins...  4.78 us
    all_to_all x1, starting transfers between devices, exchange(): return lax.all_to_all(block, 'bin', split_axis=0, concat_axis=0, tiled=True)  4.17 us
  transfers between devices with their start and end apart: 5, of which 4 were waited for; matrix products, arithmetic and copies ran while one was open for 0% of the time, Pallas kernels for 1%

profile of v2, /device:TPU:1, one launch (start us, length us, event | category | flops | bytes accessed | tf_op | source)
XLA Modules:
  0.0 156.4 jit_solution(13075377223897809410)
XLA Ops:
  0.0 1.4 copy.7
  1.4 0.0 copy-done.9
  1.5 0.0 copy-done.8
  1.5 0.0 copy-done.7
  1.5 1.7 %shard_map.46 = (bf16[32,80,128]{2,1,0:T(8,128)(2,1)S(1)}, bf16[32,2,32,384]{3,2,1,0:T(8,128)(2,1)S(1)}) custom-call(s32[1]{0:T(128)} %bitcast.1.quarter_ref, s32[1,512]{1,0:T(1,128)S(1)} %bitcast.9, s32[1,512]{1,0:T(1,128)S(1)} %bitcast.10, f32[1,512]{1,0:T(1,128)S(1)} %bitcast.11, bf16[2,512,512]{2,1,0:T(8,128)(2,1)S(1)} %bitcast.8), custom_call_target="tpu_custom_call" | custom-call | tf_op jit(solution)/shard_map/pallas_call | solution.py:214
  3.2 0.0 copy-start
  3.2 1.1 copy-done
  4.4 21.3 %all_to_all.20.got_ref.first_ref = bf16[32,80,128]{2,1,0:T(8,128)(2,1)S(1)} all-to-all(bf16[32,80,128]{2,1,0:T(8,128)(2,1)S(1)} %get-tuple-element.11), channel_id=1, replica_groups=mesh['bin'=32,'gcol'=8] {'bin'}, dimensions={0} | all-to-all | bytes 1310720 | tf_op jit(solution)/shard_map/all_to_all | solution.py:198
  25.6 4.2 %all-to-all-start.1 = ((bf16[32,2,32,384]{3,2,1,0:T(8,128)(2,1)}), bf16[32,2,32,384]{3,2,1,0:T(8,128)(2,1)S(1)}, u32[]{:S(2)}, u32[]{:S(2)}) async-start(bf16[32,2,32,384]{3,2,1,0:T(8,128)(2,1)} %copy-done), calls=%async_computation.1 | async-start | bytes 3145728 | tf_op jit(solution)/shard_map/all_to_all | solution.py:198
  29.8 0.1 slice.4
  29.9 8.4 %collective-permute-start.1 = (bf16[32,64,128]{2,1,0:T(8,128)(2,1)S(1)}, bf16[32,64,128]{2,1,0:T(8,128)(2,1)S(1)}, u32[]{:S(2)}, u32[]{:S(2)}) collective-permute-start(bf16[32,64,128]{2,1,0:T(8,128)(2,1)S(1)} %slice.4), channel_id=1, source_target_pairs={{0,5},{8,13},{16,21},{24,29},{32,37},{40,45},{48,53},{56,61},{64,6... | collective-permute-start | bytes 1572872 | tf_op jit(solution)/shard_map/ppermute | solution.py:187
  38.3 2.1 %collective-permute-start = (bf16[32,64,128]{2,1,0:T(8,128)(2,1)S(1)}, bf16[32,64,128]{2,1,0:T(8,128)(2,1)}, u32[]{:S(2)}, u32[]{:S(2)}) collective-permute-start(bf16[32,64,128]{2,1,0:T(8,128)(2,1)S(1)} %slice.4), channel_id=1, source_target_pairs={{0,3},{8,11},{16,19},{24,27},{32,35},{40,43},{48,51},{56,59},{64,6... | collective-permute-start | bytes 1572872 | tf_op jit(solution)/shard_map/ppermute | solution.py:186
  40.4 8.8 %collective-permute-done.1 = bf16[32,64,128]{2,1,0:T(8,128)(2,1)S(1)} collective-permute-done((bf16[32,64,128]{2,1,0:T(8,128)(2,1)S(1)}, bf16[32,64,128]{2,1,0:T(8,128)(2,1)S(1)}, u32[]{:S(2)}, u32[]{:S(2)}) %collective-permute-start.1) | collective-permute-done | bytes 524320 | tf_op jit(solution)/shard_map/ppermute | solution.py:187
  49.2 1.3 collective-permute-done
  50.5 0.1 select_select_fusion.refs_0_
  50.6 1.3 collective-permute-start.3
  51.9 2.1 %collective-permute-start.2 = (bf16[32,64,128]{2,1,0:T(8,128)(2,1)S(1)}, bf16[32,64,128]{2,1,0:T(8,128)(2,1)}, u32[]{:S(2)}, u32[]{:S(2)}) collective-permute-start(bf16[32,64,128]{2,1,0:T(8,128)(2,1)S(1)} %select_select_fusion.refs_0_), channel_id=1, source_target_pairs={{0,1},{3,4},{5,6},{8,9},{11,12},{13,14},{16,17},{19,20},{21,22},{2... | collective-permute-start | bytes 1572872 | tf_op jit(solution)/shard_map/ppermute | solution.py:189
  54.0 8.2 %collective-permute-done.3.refs_2_ = bf16[32,64,128]{2,1,0:T(8,128)(2,1)S(1)} collective-permute-done((bf16[32,64,128]{2,1,0:T(8,128)(2,1)S(1)}, bf16[32,64,128]{2,1,0:T(8,128)(2,1)S(1)}, u32[]{:S(2)}, u32[]{:S(2)}) %collective-permute-start.3) | collective-permute-done | bytes 524320 | tf_op jit(solution)/shard_map/ppermute | solution.py:190
  62.2 1.3 collective-permute-done.2.refs_1_
  63.6 2.0 %shard_map.47 = (bf16[256,1024]{1,0:T(8,128)(2,1)S(1)}, f32[16,1024]{1,0:T(8,128)S(1)}, bf16[512,512]{1,0:T(8,128)(2,1)S(1)}, bf16[512,512]{1,0:T(8,128)(2,1)S(1)}) custom-call(s32[1]{0:T(128)} %bitcast.use_ref, bf16[32,80,128]{2,1,0:T(8,128)(2,1)S(1)} %all_to_all.20.got_ref.first_ref, bf16[32,64,128]{2,1,0:T(8,128)(2,1)S(1)} %select_select_fusion.refs_0_, ...), custom_call_target="tpu_custom_call" | custom-call | tf_op jit(solution)/shard_map/pallas_call | solution.py:231
  65.6 0.0 copy-start.1
  65.6 0.8 copy-done.1
  66.4 0.8 copy-done.3
  67.2 0.8 copy-done.5
  68.0 0.0 all-to-all-done.1.rest_ref
  68.0 1.0 copy-done.2
  69.0 8.0 %shard_map.48 = bf16[32,72,512]{2,1,0:T(8,128)(2,1)S(1)} custom-call(bf16[256,1024]{1,0:T(8,128)(2,1)S(1)} %copy-done.2, f32[16,1024]{1,0:T(8,128)S(1)} %get-tuple-element.15.weight_ref, bf16[32,80,128]{2,1,0:T(8,128)(2,1)S(1)} %all_to_all.20.got_ref.first_ref, bf16[32,2,32,384]{3,2,1,0:T(8,128)(2,1)S(1)} %all-to-all-done.1.rest_ref), custom_call_target="tpu_custom_call" | custom-call | tf_op jit(solution)/shard_map/pallas_call | solution.py:244
  77.0 40.3 %all_to_all.21.in_ref = bf16[32,72,512]{2,1,0:T(8,128)(2,1)S(1)} all-to-all(bf16[32,72,512]{2,1,0:T(8,128)(2,1)S(1)} %shard_map.48), channel_id=1, replica_groups=mesh['bin'=32,'gcol'=8] {'bin'}, dimensions={0} | all-to-all | bytes 4718592 | tf_op jit(solution)/shard_map/all_to_all | solution.py:198
  117.3 0.0 copy-done.4
  117.3 2.4 %shard_map.49 = bf16[32,4,16,512]{3,2,1,0:T(8,128)(2,1)S(1)} custom-call(bf16[512,512]{1,0:T(8,128)(2,1)S(1)} %copy-done.4, bf16[512,512]{1,0:T(8,128)(2,1)S(1)} %copy-done.6, bf16[32,72,512]{2,1,0:T(8,128)(2,1)S(1)} %all_to_all.21.in_ref), custom_call_target="tpu_custom_call" | custom-call | tf_op jit(solution)/shard_map/pallas_call | solution.py:257
  119.8 31.9 %all_to_all.22.in_ref = bf16[32,4,16,512]{3,2,1,0:T(8,128)(2,1)S(1)} all-to-all(bf16[32,4,16,512]{3,2,1,0:T(8,128)(2,1)S(1)} %shard_map.49), channel_id=1, replica_groups=mesh['bin'=32,'gcol'=8] {'bin'}, dimensions={0} | all-to-all | bytes 4194304 | tf_op jit(solution)/shard_map/all_to_all | solution.py:198
  151.6 4.8 %shard_map.50 = f32[8,2,128,512]{3,2,1,0:T(8,128)} custom-call(bf16[32,4,16,512]{3,2,1,0:T(8,128)(2,1)S(1)} %all_to_all.22.in_ref), custom_call_target="tpu_custom_call" | custom-call | tf_op jit(solution)/shard_map/pallas_call | solution.py:262
  (9 shorter events, 0.0 us)
Async XLA Ops:
  0.0 1.5 copy-start.9
  0.0 1.5 copy-start.8
  0.0 1.5 copy-start.7
  3.2 1.1 copy-start
  25.6 42.3 %all-to-all-start.1 = ((bf16[32,2,32,384]{3,2,1,0:T(8,128)(2,1)}), bf16[32,2,32,384]{3,2,1,0:T(8,128)(2,1)S(1)}, u32[]{:S(2)}, u32[]{:S(2)}) async-start(bf16[32,2,32,384]{3,2,1,0:T(8,128)(2,1)} %copy-done), calls=%async_computation.1 | async-start | bytes 3145728 | tf_op jit(solution)/shard_map/all_to_all | solution.py:198
  29.9 19.3 %collective-permute-start.1 = (bf16[32,64,128]{2,1,0:T(8,128)(2,1)S(1)}, bf16[32,64,128]{2,1,0:T(8,128)(2,1)S(1)}, u32[]{:S(2)}, u32[]{:S(2)}) collective-permute-start(bf16[32,64,128]{2,1,0:T(8,128)(2,1)S(1)} %slice.4), channel_id=1, source_target_pairs={{0,5},{8,13},{16,21},{24,29},{32,37},{40,45},{48,53},{56,61},{64,6... | collective-permute-start | bytes 1572872 | tf_op jit(solution)/shard_map/ppermute | solution.py:187
  38.3 12.2 %collective-permute-start = (bf16[32,64,128]{2,1,0:T(8,128)(2,1)S(1)}, bf16[32,64,128]{2,1,0:T(8,128)(2,1)}, u32[]{:S(2)}, u32[]{:S(2)}) collective-permute-start(bf16[32,64,128]{2,1,0:T(8,128)(2,1)S(1)} %slice.4), channel_id=1, source_target_pairs={{0,3},{8,11},{16,19},{24,27},{32,35},{40,43},{48,51},{56,59},{64,6... | collective-permute-start | bytes 1572872 | tf_op jit(solution)/shard_map/ppermute | solution.py:186
  50.6 11.6 %collective-permute-start.3 = (bf16[32,64,128]{2,1,0:T(8,128)(2,1)S(1)}, bf16[32,64,128]{2,1,0:T(8,128)(2,1)S(1)}, u32[]{:S(2)}, u32[]{:S(2)}) collective-permute-start(bf16[32,64,128]{2,1,0:T(8,128)(2,1)S(1)} %select_select_fusion.refs_0_), channel_id=1, source_target_pairs={{0,7},{3,2},{8,15},{11,10},{16,23},{19,18},{24,31},{27,26},{32,39}... | collective-permute-start | bytes 1572872 | tf_op jit(solution)/shard_map/ppermute | solution.py:190
  51.9 11.6 %collective-permute-start.2 = (bf16[32,64,128]{2,1,0:T(8,128)(2,1)S(1)}, bf16[32,64,128]{2,1,0:T(8,128)(2,1)}, u32[]{:S(2)}, u32[]{:S(2)}) collective-permute-start(bf16[32,64,128]{2,1,0:T(8,128)(2,1)S(1)} %select_select_fusion.refs_0_), channel_id=1, source_target_pairs={{0,1},{3,4},{5,6},{8,9},{11,12},{13,14},{16,17},{19,20},{21,22},{2... | collective-permute-start | bytes 1572872 | tf_op jit(solution)/shard_map/ppermute | solution.py:189
  65.6 0.8 copy-start.1
  66.4 0.8 copy-start.3
  67.2 0.8 copy-start.5
  68.0 1.0 copy-start.2
  77.0 40.3 %copy-start.4 = (bf16[512,512]{1,0:T(8,128)(2,1)S(1)}, bf16[512,512]{1,0:T(8,128)(2,1)}, u32[]{:S(2)}) copy-start(bf16[512,512]{1,0:T(8,128)(2,1)} %copy-done.3) | copy-start | bytes 1572868
  77.0 40.3 %copy-start.6 = (bf16[512,512]{1,0:T(8,128)(2,1)S(1)}, bf16[512,512]{1,0:T(8,128)(2,1)}, u32[]{:S(2)}) copy-start(bf16[512,512]{1,0:T(8,128)(2,1)} %copy-done.5) | copy-start | bytes 1572868

commit v3 on v2

v3 whole, which is shorter than its diff:
```python
import functools

import jax
import jax.numpy as jnp
from jax import lax
from jax.experimental import pallas as pl
from jax.experimental.pallas import tpu as pltpu
from jax.sharding import PartitionSpec as P

NB = 256
GW = 128
LANES = 128
EXTRA = 16
BF16 = jnp.bfloat16
F32 = jnp.float32
VMEM_BYTES = 24 * 1024 * 1024


def dot(a, b):
    return jnp.dot(a, b, preferred_element_type=F32)


def iota(shape, axis):
    return lax.broadcasted_iota(jnp.int32, shape, axis)


def call(kernel, out_shape, **options):
    return pl.pallas_call(
        kernel,
        out_shape=out_shape,
        compiler_params=pltpu.CompilerParams(vmem_limit_bytes=VMEM_BYTES),
        **options,
    )


def slot_onehot(target, slots):
    return (iota((slots, target.shape[1]), 0) == target).astype(F32).astype(BF16)


def tile_rows(tile, part, capacity):
    at = (2 * tile + part) * capacity
    return slice(at, at + capacity)


def pack_rows_kernel(
    quarter_ref, owner_ref, offset_ref, frac_ref, rows_ref, head_ref, target_ref, copy_ref, out_ref
):
    groups, depth, _ = out_ref.shape
    pairs = owner_ref.shape[1]
    tiles = rows_ref.shape[2] // LANES
    capacity = (depth - EXTRA) // (2 * tiles)
    copy_ref[...] = head_ref[...]
    owner = owner_ref[...]
    named = (iota((groups, pairs), 0) == owner).astype(F32)
    before = (iota((pairs, pairs), 0) < iota((pairs, pairs), 1)).astype(F32).astype(BF16)
    rank = jnp.sum(dot(named.astype(BF16), before) * named, axis=0, keepdims=True)
    target = owner * capacity + rank.astype(jnp.int32)
    target_ref[...] = target
    onehot = slot_onehot(target, groups * capacity)
    for c in range(2):
        packed = dot(onehot, rows_ref[c]).astype(BF16)
        for tile in range(tiles):
            part = packed[:, tile * LANES : (tile + 1) * LANES]
            out_ref[:, tile_rows(tile, c, capacity)] = part.reshape(groups, capacity, LANES)

    frac = frac_ref[...]
    place = iota((EXTRA, pairs), 0)
    weight = jnp.where(place == offset_ref[...], (1.0 - frac).astype(BF16).astype(F32), 0.0)
    weight += jnp.where(place == offset_ref[...] + 1, frac.astype(BF16).astype(F32), 0.0)
    weight = lax.dot_general(
        weight.astype(BF16), onehot, (((1,), (1,)), ((), ())), preferred_element_type=F32
    )
    share = LANES // capacity
    quarter = quarter_ref[0]
    mine = iota((EXTRA, LANES), 1) // capacity == quarter
    for group in range(groups):
        tile = weight[:, group // share * LANES : (group // share + 1) * LANES]
        turn = (quarter + share - group % share) % share * capacity
        tile = jnp.where(mine, pltpu.roll(tile, turn, 1), 0.0)
        out_ref[group, depth - EXTRA :] = tile.astype(BF16)


def pack_heads_kernel(target_ref, head_ref, arrived_ref, out_ref):
    groups, double, lanes = out_ref.shape
    capacity = double // 2
    onehot = slot_onehot(target_ref[...], groups * capacity)
    packed = dot(onehot, head_ref[...]).astype(BF16)
    for c in range(2):
        part = packed[:, c * lanes : (c + 1) * lanes]
        out_ref[:, c * capacity : (c + 1) * capacity] = part.reshape(groups, capacity, lanes)


def prepare_kernel(own_bins, got_ref, got_head_ref, head_ref, weight_ref, rows_ref, upper_ref):
    groups, double, lanes = got_head_ref.shape
    capacity = double // 2
    slots = groups * capacity
    share = LANES // capacity
    extra = got_ref.shape[1] - EXTRA
    for c in range(2):
        for tile in range(rows_ref.shape[2] // LANES):
            part = got_ref[:, tile_rows(tile, c, capacity)].reshape(slots, LANES)
            rows_ref[c, :, tile * LANES : (tile + 1) * LANES] = part
        head = got_head_ref[:, c * capacity : (c + 1) * capacity].reshape(slots, lanes)
        head_ref[c * lanes : (c + 1) * lanes] = head.astype(F32).T.astype(BF16)
    for at in range(groups // share):
        tile = got_ref[share * at, extra:].astype(F32)
        for k in range(1, share):
            tile += got_ref[share * at + k, extra:].astype(F32)
        weight_ref[:, at * LANES : (at + 1) * LANES] = tile
    weight = weight_ref[own_bins : own_bins + 1]
    scaled = [
        (head_ref[c * GW : (c + 1) * GW].astype(F32) * weight).astype(BF16) for c in range(2)
    ]
    for c, part in enumerate(complex_dot(scaled, rows_ref)):
        upper_ref[c] = part.astype(BF16)


def complex_dot(left, right):
    real = dot(left[0], right[0]) + dot(left[1], right[1])
    imag = dot(left[0], right[1]) - dot(left[1], right[0])
    return real, imag


def spectral_kernel(own_bins, head_ref, weight_ref, rows_ref, out_ref):
    chunk, per, bins, width = out_ref.shape
    window = chunk * per
    slots = weight_ref.shape[1]
    at = pl.program_id(0) * window
    scaled = []
    for c in range(2):
        head = head_ref[pl.ds(pl.multiple_of(c * GW + at, window), window)].astype(F32)
        part = (head[:, None, :] * weight_ref[:own_bins][None]).astype(BF16)
        scaled.append(part.reshape(window * own_bins, slots))
    result = [part.reshape(window, own_bins, width) for part in complex_dot(scaled, rows_ref)]
    result = jnp.concatenate(result, axis=1).reshape(chunk, per, bins, width)
    out_ref[...] = result.astype(BF16)


def carry_kernel(spectral_ref, upper_ref, out_ref):
    groups, per, bins, width = out_ref.shape
    place = iota((groups * per, bins, width), 1)
    values = spectral_ref[...].astype(F32).reshape(groups * per, bins, width)
    for c in range(2):
        upper = upper_ref[c].astype(F32).reshape(groups * per, 1, width)
        values = values + jnp.where(place == c * (bins // 2), upper, 0.0)
    out_ref[...] = values.astype(BF16).reshape(groups, per, bins, width)


def table_kernel(own_bins, high_ref, low_ref):
    shape = high_ref.shape
    row = iota(shape, 0)
    column = iota(shape, 1)
    group = 2 * own_bins
    frequency = (row // group * own_bins + row % own_bins).astype(F32)
    bin_at = (column // group * own_bins + column % own_bins).astype(F32)
    row_imag = row // own_bins % 2 == 1
    column_imag = column // own_bins % 2 == 1
    difference = frequency - bin_at
    second = frequency + bin_at + 1.0
    first_scale = 1.0 / (difference * difference + 1.0)
    second_scale = 1.0 / (second * second + 1.0)
    real_part = difference * first_scale - second * second_scale
    imag_part = second_scale - first_scale
    crossed = jnp.where(row_imag, imag_part, -imag_part)
    table = jnp.where(row_imag == column_imag, real_part, crossed)
    high = table.astype(BF16)
    high_ref[...] = high
    low_ref[...] = (table - high.astype(F32)).astype(BF16)


def hilbert_kernel(own_bins, in_ref, out_ref, high, low):
    groups, per, bins, width = out_ref.shape
    table_kernel(own_bins, high, low)
    for g in range(per):
        values = in_ref[:, g].reshape(groups * bins, width)
        result = dot(high[...], values) + dot(low[...], values)
        out_ref[:, g] = result.astype(BF16).reshape(groups, bins, width)


def final_kernel(in_ref, out_ref, wide):
    groups, per, depth, lanes = in_ref.shape
    wide[...] = in_ref[...].astype(F32).reshape(groups * per * depth, lanes)
    for c in range(2):
        for step in range(depth // 2):
            out_ref[step, c] = wide[
                pl.ds(c * (depth // 2) + step, groups * per, stride=depth), :
            ]


def from_first(block, axis):
    place = lax.axis_index(axis)
    ahead = lax.ppermute(block, axis, [(0, 3)])
    behind = lax.ppermute(block, axis, [(0, 5)])
    block = jnp.where(place == 3, ahead, jnp.where(place == 5, behind, block))
    ahead = lax.ppermute(block, axis, [(0, 1), (3, 4), (5, 6)])
    behind = lax.ppermute(block, axis, [(0, 7), (3, 2)])
    use_ahead = (place == 1) | (place == 4) | (place == 6)
    use_behind = (place == 7) | (place == 2)
    return jnp.where(use_ahead, ahead, jnp.where(use_behind, behind, block))


def exchange(block):
    return lax.all_to_all(block, "bin", split_axis=0, concat_axis=0, tiled=True)


def on_device(pair_rows, pair_owner, pair_offset, pair_frac):
    groups = lax.axis_size("bin")
    pairs, _, columns = pair_rows.shape
    capacity = 2 * pairs // groups
    slots = groups * capacity
    own_bins = NB // groups
    per = GW // groups
    blocks = 4
    shape = jax.ShapeDtypeStruct
    scalar = pl.BlockSpec(memory_space=pltpu.SMEM)
    here = pl.BlockSpec(memory_space=pltpu.VMEM)

    quarter = lax.axis_index("bin") % (LANES // capacity)
    by_part = jnp.swapaxes(pair_rows, 0, 1)
    target, head, packed = call(
        pack_rows_kernel,
        [
            shape((1, pairs), jnp.int32),
            shape((pairs, 2 * GW), BF16),
            shape((groups, 2 * capacity * columns // LANES + EXTRA, LANES), BF16),
        ],
        in_specs=[scalar] + [here] * 5,
    )(
        quarter.reshape(1),
        pair_owner.reshape(1, pairs),
        pair_offset.reshape(1, pairs),
        pair_frac.reshape(1, pairs),
        by_part,
        pair_rows[:, :, :GW].reshape(pairs, 2 * GW),
    )
    got = exchange(packed)
    head = from_first(head, "gcol")
    got_head = exchange(
        call(
            pack_heads_kernel,
            shape((groups, 2 * capacity, GW), BF16),
            in_specs=[here] * 2 + [pl.BlockSpec(memory_space=pl.ANY)],
        )(target, head, got)
    )

    whole = lambda *dims: pl.BlockSpec(dims, lambda i: (0,) * len(dims))
    head, weight, rows, upper = call(
        functools.partial(prepare_kernel, own_bins),
        [
            shape((2 * GW, slots), BF16),
            shape((EXTRA, slots), F32),
            shape((2, slots, columns), BF16),
            shape((2, GW, columns), BF16),
        ],
    )(got, got_head)
    upper = lax.ppermute(upper, "bin", [(i, i + 1) for i in range(groups - 1)])
    spectral = call(
        functools.partial(spectral_kernel, own_bins),
        shape((groups, per, 2 * own_bins, columns), BF16),
        grid=(blocks,),
        in_specs=[whole(2 * GW, slots), whole(EXTRA, slots), whole(2, slots, columns)],
        out_specs=pl.BlockSpec(
            (groups // blocks, per, 2 * own_bins, columns), lambda i: (i, 0, 0, 0)
        ),
    )(head, weight, rows)
    spectral = call(
        carry_kernel, shape(spectral.shape, BF16), input_output_aliases={0: 0}
    )(spectral, upper)
    chi = call(
        functools.partial(hilbert_kernel, own_bins),
        shape(spectral.shape, BF16),
        scratch_shapes=[pltpu.VMEM((2 * NB, 2 * NB), BF16)] * 2,
    )(exchange(spectral))
    return call(
        final_kernel,
        shape((own_bins, 2, GW, columns), F32),
        grid=(columns // LANES,),
        in_specs=[
            pl.BlockSpec((groups, per, 2 * own_bins, LANES), lambda i: (0, 0, 0, i))
        ],
        out_specs=pl.BlockSpec((own_bins, 2, GW, LANES), lambda i: (0, 0, 0, i)),
        scratch_shapes=[pltpu.VMEM((GW * 2 * own_bins, LANES), F32)],
    )(exchange(chi))


def solution(mesh):
    placed = (P("bin", None, "gcol"), P("bin", None), P("bin"), P("bin"))
    return jax.shard_map(
        on_device,
        mesh=mesh,
        in_specs=placed,
        out_specs=P("bin", None, None, "gcol"),
        check_vma=False,
    )
```

time: 158 us -> 142 us (0.90)
  blocking collectives: 93.5 us -> 82.3 us
  starting transfers between devices: 18.1 us -> 23.4 us
  Pallas kernels: 18.9 us -> 15.6 us
  local copies, waits for them, and re-layouts: 6.08 us -> 2.84 us
  waiting for transfers between devices: 19.7 us -> 16.8 us
    all_to_all x3, blocking collectives: 93.5 us -> 82.3 us  [exchange(): return lax.all_to_all(block, 'bin', split_axis=0, concat_axis=0, tiled=True)]
    all_to_all x1, waiting for transfers between devices: 0.01 us -> 6.56 us  [exchange(): return lax.all_to_all(block, 'bin', split_axis=0, concat_axis=0, tiled=True)]
    ppermute x1, waiting for transfers between devices: 8.82 us -> 4.12 us  [from_first(): behind = lax.ppermute(block, axis, [(0, 5)])]
    ppermute x1, waiting for transfers between devices: 8.19 us -> 3.51 us  [from_first(): behind = lax.ppermute(block, axis, [(0, 7), (3, 2)])]
    all_to_all x1, starting transfers between devices: 4.17 us -> 8.59 us  [exchange(): return lax.all_to_all(block, 'bin', split_axis=0, concat_axis=0, tiled=True)]
    pallas_call x5 -> x7, Pallas kernels: 18.9 us -> 15.6 us  [the longest x1 5.08 us: on_device(): call(functools.partial(spectral_kernel, own_bins), shape((groups, per, 2...]
    unnamed x21 -> x10, local copies, waits for them, and re-layouts: 6.02 us -> 2.84 us
    ppermute x0 -> x1, starting transfers between devices: none -> 2.49 us  [on_device(): upper = lax.ppermute(upper, 'bin', [(i, i + 1) for i in range(groups - 1)])]
  transfers between devices with their start and end apart: 5 -> 6, of which waited for: 4 -> 5; matrix products, arithmetic and copies ran while one was open for 0% -> 0% of each run, Pallas kernels for 1% -> 4%
where the time goes in v3:
time: 142 us; the launch traced here: 141 us
  blocking collectives  82.3 us (58%)
  starting transfers between devices  23.4 us (16%)
  waiting for transfers between devices  16.8 us (12%)
  Pallas kernels  15.6 us (11%)
  local copies, waits for them, and re-layouts  2.84 us (2%)
    all_to_all x3, blocking collectives, exchange(): return lax.all_to_all(block, 'bin', split_axis=0, concat_axis=0, tiled=True)  82.3 us
    all_to_all x1, starting transfers between devices, exchange(): return lax.all_to_all(block, 'bin', split_axis=0, concat_axis=0, tiled=True)  8.59 us
    ppermute x1, starting transfers between devices, from_first(): behind = lax.ppermute(block, axis, [(0, 5)])  8.38 us
    all_to_all x1, waiting for transfers between devices, exchange(): return lax.all_to_all(block, 'bin', split_axis=0, concat_axis=0, tiled=True)  6.56 us
    pallas_call x1, Pallas kernels, on_device(): call(functools.partial(spectral_kernel, own_bins), shape((groups, per, 2...  5.08 us
    ppermute x1, waiting for transfers between devices, from_first(): behind = lax.ppermute(block, axis, [(0, 5)])  4.12 us
    ppermute x1, waiting for transfers between devices, from_first(): behind = lax.ppermute(block, axis, [(0, 7), (3, 2)])  3.51 us
    pallas_call x1, Pallas kernels, on_device(): call(final_kernel, shape((own_bins, 2, GW, columns), F32), grid=(columns...  3.43 us
  transfers between devices with their start and end apart: 6, of which 5 were waited for; matrix products, arithmetic and copies ran while one was open for 0% of the time, Pallas kernels for 4%

profile of v3, /device:TPU:1, one launch (start us, length us, event | category | flops | bytes accessed | tf_op | source)
XLA Modules:
  0.0 141.2 jit_solution(8058157840477658230)
XLA Ops:
  0.0 0.0 slice-start
  0.0 0.0 copy-start.1
  0.0 1.4 %copy.10 = bf16[512,2,512]{2,0,1:T(8,128)(2,1)S(1)} copy(bf16[512,2,512]{2,1,0:T(2,128)(2,1)} %param.4) | data formatting | bytes 2097152 | tf_op args[0]
  1.5 0.0 slice-done
  1.5 0.0 copy-done.3
  1.5 0.0 copy-done.2
  1.6 0.0 copy-done.1
  1.6 1.7 %shard_map.46 = (s32[1,512]{1,0:T(1,128)S(1)}, bf16[512,256]{1,0:T(8,128)(2,1)S(1)}, bf16[32,272,128]{2,1,0:T(8,128)(2,1)S(1)}) custom-call(s32[1]{0:T(128)} %bitcast.quarter_ref, s32[1,512]{1,0:T(1,128)S(1)} %bitcast.13, s32[1,512]{1,0:T(1,128)S(1)} %bitcast.14, f32[1,512]{1,0:T(1,128)S(1)} %bitcast.15, bf16[2,512,512]{2,1,0:T(8,128)(2,1)S(1)} %bitcast.11, ...), custom_call_target="tpu_custom_call" | custom-call | tf_op jit(solution)/shard_map/pallas_call | solution.py:220
  3.3 0.0 copy-start
  3.3 1.4 copy-done
  4.7 8.6 %all-to-all-start = ((bf16[32,272,128]{2,1,0:T(8,128)(2,1)}), bf16[32,272,128]{2,1,0:T(8,128)(2,1)S(1)}, u32[]{:S(2)}, u32[]{:S(2)}) async-start(bf16[32,272,128]{2,1,0:T(8,128)(2,1)} %copy-done), calls=%async_computation | async-start | bytes 4456448 | tf_op jit(solution)/shard_map/all_to_all | solution.py:203
  13.3 8.4 %collective-permute-start.1 = (bf16[512,256]{1,0:T(8,128)(2,1)S(1)}, bf16[512,256]{1,0:T(8,128)(2,1)S(1)}, u32[]{:S(2)}, u32[]{:S(2)}) collective-permute-start(bf16[512,256]{1,0:T(8,128)(2,1)S(1)} %get-tuple-element.14), channel_id=1, source_target_pairs={{0,5},{8,13},{16,21},{24,29},{32,37},{40,45},{48,53},{56,61},{64,6... | collective-permute-start | bytes 786440 | tf_op jit(solution)/shard_map/ppermute | solution.py:193
  21.6 1.3 collective-permute-start
  23.0 4.1 %collective-permute-done.1 = bf16[512,256]{1,0:T(8,128)(2,1)S(1)} collective-permute-done((bf16[512,256]{1,0:T(8,128)(2,1)S(1)}, bf16[512,256]{1,0:T(8,128)(2,1)S(1)}, u32[]{:S(2)}, u32[]{:S(2)}) %collective-permute-start.1) | collective-permute-done | bytes 262176 | tf_op jit(solution)/shard_map/ppermute | solution.py:193
  27.1 1.3 collective-permute-done
  28.4 0.1 select_select_fusion.1
  28.5 1.3 collective-permute-start.3
  29.8 1.3 collective-permute-start.2
  31.1 3.5 %collective-permute-done.3 = bf16[512,256]{1,0:T(8,128)(2,1)S(1)} collective-permute-done((bf16[512,256]{1,0:T(8,128)(2,1)S(1)}, bf16[512,256]{1,0:T(8,128)(2,1)S(1)}, u32[]{:S(2)}, u32[]{:S(2)}) %collective-permute-start.3) | collective-permute-done | bytes 262176 | tf_op jit(solution)/shard_map/ppermute | solution.py:196
  34.6 1.3 collective-permute-done.2
  36.0 6.6 %all-to-all-done.arrived_ref.got_ref = bf16[32,272,128]{2,1,0:T(8,128)(2,1)S(1)} async-done(((bf16[32,272,128]{2,1,0:T(8,128)(2,1)}), bf16[32,272,128]{2,1,0:T(8,128)(2,1)S(1)}, u32[]{:S(2)}, u32[]{:S(2)}) %all-to-all-start) | async-done | bytes 2228256 | tf_op jit(solution)/shard_map/all_to_all | solution.py:203
  42.5 0.4 shard_map.47
  43.0 16.8 %all_to_all.20.got_head_ref = bf16[32,64,128]{2,1,0:T(8,128)(2,1)S(1)} all-to-all(bf16[32,64,128]{2,1,0:T(8,128)(2,1)S(1)} %shard_map.47), channel_id=1, replica_groups=mesh['bin'=32,'gcol'=8] {'bin'}, dimensions={0} | all-to-all | bytes 1048576 | tf_op jit(solution)/shard_map/all_to_all | solution.py:203
  59.8 1.1 shard_map.48
  60.9 2.5 %collective-permute-start.4 = (bf16[2,128,512]{2,1,0:T(8,128)(2,1)S(1)}, bf16[2,128,512]{2,1,0:T(8,128)(2,1)S(1)}, u32[]{:S(2)}, u32[]{:S(2)}) collective-permute-start(bf16[2,128,512]{2,1,0:T(8,128)(2,1)S(1)} %get-tuple-element.18), channel_id=1, source_target_pairs={{0,8},{8,16},{16,24},{24,32},{32,40},{40,48},{48,56},{56,64},{64,7... | collective-permute-start | bytes 786440 | tf_op jit(solution)/shard_map/ppermute | solution.py:256
  63.4 5.1 %shard_map.49.spectral_ref = bf16[32,4,16,512]{3,2,1,0:T(8,128)(2,1)S(1)} custom-call(bf16[256,1024]{1,0:T(8,128)(2,1)S(1)} %get-tuple-element.15.head_ref, f32[16,1024]{1,0:T(8,128)S(1)} %get-tuple-element.16.weight_ref, bf16[2,1024,512]{2,1,0:T(8,128)(2,1)S(1)} %get-tuple-element.17.rows_ref), custom_call_target="tpu_custom_call" | custom-call | tf_op jit(solution)/shard_map/pallas_call | solution.py:257
  68.5 0.0 collective-permute-done.4.upper_ref
  68.5 1.1 shard_map.50
  69.6 33.5 %all_to_all.21.in_ref = bf16[32,4,16,512]{3,2,1,0:T(8,128)(2,1)S(1)} all-to-all(bf16[32,4,16,512]{3,2,1,0:T(8,128)(2,1)S(1)} %shard_map.50), channel_id=1, replica_groups=mesh['bin'=32,'gcol'=8] {'bin'}, dimensions={0} | all-to-all | bytes 4194304 | tf_op jit(solution)/shard_map/all_to_all | solution.py:203
  103.1 2.7 %shard_map.51 = bf16[32,4,16,512]{3,2,1,0:T(8,128)(2,1)S(1)} custom-call(bf16[32,4,16,512]{3,2,1,0:T(8,128)(2,1)S(1)} %all_to_all.21.in_ref), custom_call_target="tpu_custom_call" | custom-call | tf_op jit(solution)/shard_map/pallas_call | solution.py:269
  105.9 31.9 %all_to_all.22.in_ref = bf16[32,4,16,512]{3,2,1,0:T(8,128)(2,1)S(1)} all-to-all(bf16[32,4,16,512]{3,2,1,0:T(8,128)(2,1)S(1)} %shard_map.51), channel_id=1, replica_groups=mesh['bin'=32,'gcol'=8] {'bin'}, dimensions={0} | all-to-all | bytes 4194304 | tf_op jit(solution)/shard_map/all_to_all | solution.py:203
  137.8 3.4 %shard_map.52 = f32[8,2,128,512]{3,2,1,0:T(8,128)} custom-call(bf16[32,4,16,512]{3,2,1,0:T(8,128)(2,1)S(1)} %all_to_all.22.in_ref), custom_call_target="tpu_custom_call" | custom-call | tf_op jit(solution)/shard_map/pallas_call | solution.py:274
  (4 shorter events, 0.1 us)
Async XLA Ops:
  0.0 1.5 %slice-start = ((bf16[512,2,512]{2,1,0:T(2,128)(2,1)}), bf16[512,2,128]{2,1,0:T(2,128)(2,1)S(1)}, s32[]{:S(2)}) async-start(bf16[512,2,512]{2,1,0:T(2,128)(2,1)} %param.4), calls=%async_computation.4 | async-start | bytes 524288 | tf_op jit(solution)/shard_map/slice | solution.py:234
  0.0 1.5 %copy-start.3 = (f32[512]{0:T(512)S(1)}, f32[512]{0:T(512)}, u32[]{:S(2)}) copy-start(f32[512]{0:T(512)} %param.7) | copy-start | bytes 6148
  0.0 1.5 %copy-start.2 = (s32[512]{0:T(512)S(1)}, s32[512]{0:T(512)}, u32[]{:S(2)}) copy-start(s32[512]{0:T(512)} %param.6) | copy-start | bytes 6148
  0.0 1.5 %copy-start.1 = (s32[512,1]{0,1:T(1,128)S(1)}, s32[512,1]{0,1:T(1,128)}, u32[]{:S(2)}) copy-start(s32[512,1]{0,1:T(1,128)} %param.5) | copy-start | bytes 6148
  3.3 1.4 copy-start
  4.7 37.9 %all-to-all-start = ((bf16[32,272,128]{2,1,0:T(8,128)(2,1)}), bf16[32,272,128]{2,1,0:T(8,128)(2,1)S(1)}, u32[]{:S(2)}, u32[]{:S(2)}) async-start(bf16[32,272,128]{2,1,0:T(8,128)(2,1)} %copy-done), calls=%async_computation | async-start | bytes 4456448 | tf_op jit(solution)/shard_map/all_to_all | solution.py:203
  13.3 13.8 %collective-permute-start.1 = (bf16[512,256]{1,0:T(8,128)(2,1)S(1)}, bf16[512,256]{1,0:T(8,128)(2,1)S(1)}, u32[]{:S(2)}, u32[]{:S(2)}) collective-permute-start(bf16[512,256]{1,0:T(8,128)(2,1)S(1)} %get-tuple-element.14), channel_id=1, source_target_pairs={{0,5},{8,13},{16,21},{24,29},{32,37},{40,45},{48,53},{56,61},{64,6... | collective-permute-start | bytes 786440 | tf_op jit(solution)/shard_map/ppermute | solution.py:193
  21.6 6.8 %collective-permute-start = (bf16[512,256]{1,0:T(8,128)(2,1)S(1)}, bf16[512,256]{1,0:T(8,128)(2,1)S(1)}, u32[]{:S(2)}, u32[]{:S(2)}) collective-permute-start(bf16[512,256]{1,0:T(8,128)(2,1)S(1)} %get-tuple-element.14), channel_id=1, source_target_pairs={{0,3},{8,11},{16,19},{24,27},{32,35},{40,43},{48,51},{56,59},{64,6... | collective-permute-start | bytes 786440 | tf_op jit(solution)/shard_map/ppermute | solution.py:192
  28.5 6.1 %collective-permute-start.3 = (bf16[512,256]{1,0:T(8,128)(2,1)S(1)}, bf16[512,256]{1,0:T(8,128)(2,1)S(1)}, u32[]{:S(2)}, u32[]{:S(2)}) collective-permute-start(bf16[512,256]{1,0:T(8,128)(2,1)S(1)} %select_select_fusion.1), channel_id=1, source_target_pairs={{0,7},{3,2},{8,15},{11,10},{16,23},{19,18},{24,31},{27,26},{32,39}... | collective-permute-start | bytes 786440 | tf_op jit(solution)/shard_map/ppermute | solution.py:196
  29.8 6.1 %collective-permute-start.2 = (bf16[512,256]{1,0:T(8,128)(2,1)S(1)}, bf16[512,256]{1,0:T(8,128)(2,1)S(1)}, u32[]{:S(2)}, u32[]{:S(2)}) collective-permute-start(bf16[512,256]{1,0:T(8,128)(2,1)S(1)} %select_select_fusion.1), channel_id=1, source_target_pairs={{0,1},{3,4},{5,6},{8,9},{11,12},{13,14},{16,17},{19,20},{21,22},{2... | collective-permute-start | bytes 786440 | tf_op jit(solution)/shard_map/ppermute | solution.py:195
  60.9 7.6 %collective-permute-start.4 = (bf16[2,128,512]{2,1,0:T(8,128)(2,1)S(1)}, bf16[2,128,512]{2,1,0:T(8,128)(2,1)S(1)}, u32[]{:S(2)}, u32[]{:S(2)}) collective-permute-start(bf16[2,128,512]{2,1,0:T(8,128)(2,1)S(1)} %get-tuple-element.18), channel_id=1, source_target_pairs={{0,8},{8,16},{16,24},{24,32},{32,40},{40,48},{48,56},{56,64},{64,7... | collective-permute-start | bytes 786440 | tf_op jit(solution)/shard_map/ppermute | solution.py:256

commit v4 on v3

--- a/solution.py
+++ b/solution.py
@@ -5,12 +5,16 @@
 from jax import lax
 from jax.experimental import pallas as pl
 from jax.experimental.pallas import tpu as pltpu
+from jax.sharding import Mesh
 from jax.sharding import PartitionSpec as P
 
 NB = 256
 GW = 128
 LANES = 128
 EXTRA = 16
+ROW = 8
+BIN = ("y", "x", "core")
+ORDER = ("x", "y", "core")
 BF16 = jnp.bfloat16
 F32 = jnp.float32
 VMEM_BYTES = 24 * 1024 * 1024
@@ -31,6 +35,15 @@
         compiler_params=pltpu.CompilerParams(vmem_limit_bytes=VMEM_BYTES),
         **options,
     )
+
+
+def along_path(index):
+    row, at = index // ROW, index % ROW
+    return row * ROW + at + (row % 2) * (ROW - 1 - 2 * at)
+
+
+def block_at(place):
+    return place % ROW // 2 * ROW + place // ROW * 2 + place % 2
 
 
 def slot_onehot(target, slots):
@@ -54,7 +67,7 @@
     named = (iota((groups, pairs), 0) == owner).astype(F32)
     before = (iota((pairs, pairs), 0) < iota((pairs, pairs), 1)).astype(F32).astype(BF16)
     rank = jnp.sum(dot(named.astype(BF16), before) * named, axis=0, keepdims=True)
-    target = owner * capacity + rank.astype(jnp.int32)
+    target = along_path(owner) * capacity + rank.astype(jnp.int32)
     target_ref[...] = target
     onehot = slot_onehot(target, groups * capacity)
     for c in range(2):
@@ -80,7 +93,7 @@
         out_ref[group, depth - EXTRA :] = tile.astype(BF16)
 
 
-def pack_heads_kernel(target_ref, head_ref, arrived_ref, out_ref):
+def pack_heads_kernel(target_ref, head_ref, arrived_ref, high_ref, low_ref, out_ref):
     groups, double, lanes = out_ref.shape
     capacity = double // 2
     onehot = slot_onehot(target_ref[...], groups * capacity)
@@ -97,9 +110,12 @@
     share = LANES // capacity
     extra = got_ref.shape[1] - EXTRA
     for c in range(2):
-        for tile in range(rows_ref.shape[2] // LANES):
+        for tile in range(rows_ref.shape[1] // LANES):
             part = got_ref[:, tile_rows(tile, c, capacity)].reshape(slots, LANES)
-            rows_ref[c, :, tile * LANES : (tile + 1) * LANES] = part
+            for at in range(c, 3, 2):
+                rows_ref[
+                    at * slots : (at + 1) * slots, tile * LANES : (tile + 1) * LANES
+                ] = part
         head = got_head_ref[:, c * capacity : (c + 1) * capacity].reshape(slots, lanes)
         head_ref[c * lanes : (c + 1) * lanes] = head.astype(F32).T.astype(BF16)
     for at in range(groups // share):
@@ -115,9 +131,10 @@
         upper_ref[c] = part.astype(BF16)
 
 
-def complex_dot(left, right):
-    real = dot(left[0], right[0]) + dot(left[1], right[1])
-    imag = dot(left[0], right[1]) - dot(left[1], right[0])
+def complex_dot(left, rows_ref):
+    slots = rows_ref.shape[0] // 3
+    real = dot(jnp.concatenate(left, axis=1), rows_ref[: 2 * slots])
+    imag = dot(jnp.concatenate([left[0], -left[1]], axis=1), rows_ref[slots:])
     return real, imag
 
 
@@ -151,8 +168,8 @@
     row = iota(shape, 0)
     column = iota(shape, 1)
     group = 2 * own_bins
-    frequency = (row // group * own_bins + row % own_bins).astype(F32)
-    bin_at = (column // group * own_bins + column % own_bins).astype(F32)
+    frequency = (block_at(row // group) * own_bins + row % own_bins).astype(F32)
+    bin_at = (along_path(column // group) * own_bins + column % own_bins).astype(F32)
     row_imag = row // own_bins % 2 == 1
     column_imag = column // own_bins % 2 == 1
     difference = frequency - bin_at
@@ -168,9 +185,8 @@
     low_ref[...] = (table - high.astype(F32)).astype(BF16)
 
 
-def hilbert_kernel(own_bins, in_ref, out_ref, high, low):
+def hilbert_kernel(high, low, in_ref, out_ref):
     groups, per, bins, width = out_ref.shape
-    table_kernel(own_bins, high, low)
     for g in range(per):
         values = in_ref[:, g].reshape(groups * bins, width)
         result = dot(high[...], values) + dot(low[...], values)
@@ -200,22 +216,22 @@
 
 
 def exchange(block):
-    return lax.all_to_all(block, "bin", split_axis=0, concat_axis=0, tiled=True)
+    return lax.all_to_all(block, ORDER, split_axis=0, concat_axis=0, tiled=True)
 
 
 def on_device(pair_rows, pair_owner, pair_offset, pair_frac):
-    groups = lax.axis_size("bin")
+    groups = lax.axis_size(BIN)
     pairs, _, columns = pair_rows.shape
     capacity = 2 * pairs // groups
     slots = groups * capacity
     own_bins = NB // groups
     per = GW // groups
-    blocks = 4
+    blocks = 2
     shape = jax.ShapeDtypeStruct
     scalar = pl.BlockSpec(memory_space=pltpu.SMEM)
     here = pl.BlockSpec(memory_space=pltpu.VMEM)
 
-    quarter = lax.axis_index("bin") % (LANES // capacity)
+    quarter = lax.axis_index(ORDER) % (LANES // capacity)
     by_part = jnp.swapaxes(pair_rows, 0, 1)
     target, head, packed = call(
         pack_rows_kernel,
@@ -235,12 +251,15 @@
     )
     got = exchange(packed)
     head = from_first(head, "gcol")
+    high, low = call(
+        functools.partial(table_kernel, own_bins), [shape((2 * NB, 2 * NB), BF16)] * 2
+    )()
     got_head = exchange(
         call(
             pack_heads_kernel,
             shape((groups, 2 * capacity, GW), BF16),
-            in_specs=[here] * 2 + [pl.BlockSpec(memory_space=pl.ANY)],
-        )(target, head, got)
+            in_specs=[here] * 2 + [pl.BlockSpec(memory_space=pl.ANY)] * 3,
+        )(target, head, got, high, low)
     )
 
     whole = lambda *dims: pl.BlockSpec(dims, lambda i: (0,) * len(dims))
@@ -249,16 +268,17 @@
         [
             shape((2 * GW, slots), BF16),
             shape((EXTRA, slots), F32),
-            shape((2, slots, columns), BF16),
+            shape((3 * slots, columns), BF16),
             shape((2, GW, columns), BF16),
         ],
     )(got, got_head)
-    upper = lax.ppermute(upper, "bin", [(i, i + 1) for i in range(groups - 1)])
+    path = [block_at(along_path(i)) for i in range(groups)]
+    upper = lax.ppermute(upper, BIN, list(zip(path[:-1], path[1:])))
     spectral = call(
         functools.partial(spectral_kernel, own_bins),
         shape((groups, per, 2 * own_bins, columns), BF16),
         grid=(blocks,),
-        in_specs=[whole(2 * GW, slots), whole(EXTRA, slots), whole(2, slots, columns)],
+        in_specs=[whole(2 * GW, slots), whole(EXTRA, slots), whole(3 * slots, columns)],
         out_specs=pl.BlockSpec(
             (groups // blocks, per, 2 * own_bins, columns), lambda i: (i, 0, 0, 0)
         ),
@@ -266,11 +286,7 @@
     spectral = call(
         carry_kernel, shape(spectral.shape, BF16), input_output_aliases={0: 0}
     )(spectral, upper)
-    chi = call(
-        functools.partial(hilbert_kernel, own_bins),
-        shape(spectral.shape, BF16),
-        scratch_shapes=[pltpu.VMEM((2 * NB, 2 * NB), BF16)] * 2,
-    )(exchange(spectral))
+    chi = call(hilbert_kernel, shape(spectral.shape, BF16))(high, low, exchange(spectral))
     return call(
         final_kernel,
         shape((own_bins, 2, GW, columns), F32),
@@ -284,11 +300,13 @@
 
 
 def solution(mesh):
-    placed = (P("bin", None, "gcol"), P("bin", None), P("bin"), P("bin"))
+    bins, columns = mesh.devices.shape
+    devices = mesh.devices.reshape(bins // ROW, ROW // 2, 2, columns)
+    placed = (P(BIN, None, "gcol"), P(BIN, None), P(BIN), P(BIN))
     return jax.shard_map(
         on_device,
-        mesh=mesh,
+        mesh=Mesh(devices, (*BIN, "gcol")),
         in_specs=placed,
-        out_specs=P("bin", None, None, "gcol"),
+        out_specs=P(BIN, None, None, "gcol"),
         check_vma=False,
     )

time: 142 us -> 138 us (0.972)
  waiting for transfers between devices: 16.8 us -> 14.1 us
  blocking collectives: 82.3 us -> 79.7 us
    all_to_all x3, blocking collectives: 82.3 us -> 79.7 us  [exchange(): return lax.all_to_all(block, ORDER, split_axis=0, concat_axis=0, tiled=True)]
    ppermute x1, waiting for transfers between devices: 3.51 us -> 1.35 us  [from_first(): behind = lax.ppermute(block, axis, [(0, 7), (3, 2)])]
    pallas_call x1 -> x2, Pallas kernels: 2.73 us -> 3.13 us  [the longest x1 2.33 us: on_device(): call(hilbert_kernel, shape(spectral.shape, BF16))]
  transfers between devices with their start and end apart: 6 -> 6, of which waited for: 5 -> 5; matrix products, arithmetic and copies ran while one was open for 0% -> 1% of each run, Pallas kernels for 4% -> 4%
where the time goes in v4:
time: 138 us
  blocking collectives  79.7 us (58%)
  starting transfers between devices  24.3 us (18%)
  Pallas kernels  15.7 us (11%)
  waiting for transfers between devices  14.1 us (10%)
  local copies, waits for them, and re-layouts  2.84 us (2%)
    all_to_all x3, blocking collectives, exchange(): return lax.all_to_all(block, ORDER, split_axis=0, concat_axis=0, tiled=True)  79.7 us
    all_to_all x1, starting transfers between devices, exchange(): return lax.all_to_all(block, ORDER, split_axis=0, concat_axis=0, tiled=True)  8.59 us
    ppermute x1, starting transfers between devices, from_first(): behind = lax.ppermute(block, axis, [(0, 5)])  8.38 us
    all_to_all x1, waiting for transfers between devices, exchange(): return lax.all_to_all(block, ORDER, split_axis=0, concat_axis=0, tiled=True)  5.38 us
    pallas_call x1, Pallas kernels, on_device(): call(functools.partial(spectral_kernel, own_bins), shape((groups, per, 2...  4.72 us
    ppermute x1, waiting for transfers between devices, from_first(): behind = lax.ppermute(block, axis, [(0, 5)])  4.12 us
    pallas_call x1, Pallas kernels, on_device(): call(final_kernel, shape((own_bins, 2, GW, columns), F32), grid=(columns...  3.43 us
    unnamed x12, local copies, waits for them, and re-layouts  2.84 us
  transfers between devices with their start and end apart: 6, of which 5 were waited for; matrix products, arithmetic and copies ran while one was open for 1% of the time, Pallas kernels for 4%

profile of v4, /device:TPU:1, one launch (start us, length us, event | category | flops | bytes accessed | tf_op | source)
XLA Modules:
  0.0 138.0 jit_solution(813961007830821665)
XLA Ops:
  0.0 0.0 copy-start.1
  0.0 1.4 %copy.10 = bf16[512,2,512]{2,0,1:T(8,128)(2,1)S(1)} copy(bf16[512,2,512]{2,1,0:T(2,128)(2,1)} %param.4) | data formatting | bytes 2097152 | tf_op args[0]
  1.5 0.0 slice-done
  1.5 0.0 copy-done.3
  1.5 0.0 copy-done.2
  1.6 1.7 %shard_map.47 = (s32[1,512]{1,0:T(1,128)S(1)}, bf16[512,256]{1,0:T(8,128)(2,1)S(1)}, bf16[32,272,128]{2,1,0:T(8,128)(2,1)S(1)}) custom-call(s32[1]{0:T(128)} %bitcast.quarter_ref, s32[1,512]{1,0:T(1,128)S(1)} %bitcast.13, s32[1,512]{1,0:T(1,128)S(1)} %bitcast.14, f32[1,512]{1,0:T(1,128)S(1)} %bitcast.15, bf16[2,512,512]{2,1,0:T(8,128)(2,1)S(1)} %bitcast.11, ...), custom_call_target="tpu_custom_call" | custom-call | tf_op jit(solution)/shard_map/pallas_call | solution.py:236
  3.3 0.0 copy-start
  3.3 1.4 copy-done
  4.7 8.6 %all-to-all-start = ((bf16[32,272,128]{2,1,0:T(8,128)(2,1)}), bf16[32,272,128]{2,1,0:T(8,128)(2,1)S(1)}, u32[]{:S(2)}, u32[]{:S(2)}) async-start(bf16[32,272,128]{2,1,0:T(8,128)(2,1)} %copy-done), calls=%async_computation | async-start | bytes 4456448 | tf_op jit(solution)/shard_map/all_to_all | solution.py:219
  13.3 8.4 %collective-permute-start.1 = (bf16[512,256]{1,0:T(8,128)(2,1)S(1)}, bf16[512,256]{1,0:T(8,128)(2,1)S(1)}, u32[]{:S(2)}, u32[]{:S(2)}) collective-permute-start(bf16[512,256]{1,0:T(8,128)(2,1)S(1)} %get-tuple-element.18), channel_id=1, source_target_pairs={{0,5},{8,13},{16,21},{24,29},{32,37},{40,45},{48,53},{56,61},{64,6... | collective-permute-start | bytes 786440 | tf_op jit(solution)/shard_map/ppermute | solution.py:209
  21.6 1.3 collective-permute-start
  23.0 4.1 %collective-permute-done.1 = bf16[512,256]{1,0:T(8,128)(2,1)S(1)} collective-permute-done((bf16[512,256]{1,0:T(8,128)(2,1)S(1)}, bf16[512,256]{1,0:T(8,128)(2,1)S(1)}, u32[]{:S(2)}, u32[]{:S(2)}) %collective-permute-start.1) | collective-permute-done | bytes 262176 | tf_op jit(solution)/shard_map/ppermute | solution.py:209
  27.1 1.3 collective-permute-done
  28.5 2.0 %collective-permute-start.3 = (bf16[512,256]{1,0:T(8,128)(2,1)S(1)}, bf16[512,256]{1,0:T(8,128)(2,1)}, u32[]{:S(2)}, u32[]{:S(2)}) collective-permute-start(bf16[512,256]{1,0:T(8,128)(2,1)S(1)} %select_select_fusion.1), channel_id=1, source_target_pairs={{0,7},{3,2},{8,15},{11,10},{16,23},{19,18},{24,31},{27,26},{32,39}... | collective-permute-start | bytes 786440 | tf_op jit(solution)/shard_map/ppermute | solution.py:212
  30.4 2.0 %collective-permute-start.2 = (bf16[512,256]{1,0:T(8,128)(2,1)S(1)}, bf16[512,256]{1,0:T(8,128)(2,1)}, u32[]{:S(2)}, u32[]{:S(2)}) collective-permute-start(bf16[512,256]{1,0:T(8,128)(2,1)S(1)} %select_select_fusion.1), channel_id=1, source_target_pairs={{0,1},{3,4},{5,6},{8,9},{11,12},{13,14},{16,17},{19,20},{21,22},{2... | collective-permute-start | bytes 786440 | tf_op jit(solution)/shard_map/ppermute | solution.py:211
  32.4 0.8 shard_map.46
  33.3 1.3 collective-permute-done.3
  34.6 0.0 copy-done.4
  34.6 2.0 %collective-permute-done.2 = bf16[512,256]{1,0:T(8,128)(2,1)} collective-permute-done((bf16[512,256]{1,0:T(8,128)(2,1)S(1)}, bf16[512,256]{1,0:T(8,128)(2,1)}, u32[]{:S(2)}, u32[]{:S(2)}) %collective-permute-start.2) | collective-permute-done | bytes 262176 | tf_op jit(solution)/shard_map/ppermute | solution.py:211
  36.6 1.0 select_select_fusion.head_ref
  37.6 5.4 %all-to-all-done.arrived_ref.got_ref = bf16[32,272,128]{2,1,0:T(8,128)(2,1)S(1)} async-done(((bf16[32,272,128]{2,1,0:T(8,128)(2,1)}), bf16[32,272,128]{2,1,0:T(8,128)(2,1)S(1)}, u32[]{:S(2)}, u32[]{:S(2)}) %all-to-all-start) | async-done | bytes 2228256 | tf_op jit(solution)/shard_map/all_to_all | solution.py:219
  43.0 0.4 shard_map.48
  43.4 15.3 %all_to_all.20.got_head_ref = bf16[32,64,128]{2,1,0:T(8,128)(2,1)S(1)} all-to-all(bf16[32,64,128]{2,1,0:T(8,128)(2,1)S(1)} %shard_map.48), channel_id=1, replica_groups=mesh['y'=4,'x'=4,'core'=2,'gcol'=8] {'x','y','core'}, dimensions={0} | all-to-all | bytes 1048576 | tf_op jit(solution)/shard_map/all_to_all | solution.py:219
  58.7 1.2 shard_map.49
  59.9 2.1 %collective-permute-start.4 = (bf16[2,128,512]{2,1,0:T(8,128)(2,1)S(1)}, bf16[2,128,512]{2,1,0:T(8,128)(2,1)S(1)}, u32[]{:S(2)}, u32[]{:S(2)}) collective-permute-start(bf16[2,128,512]{2,1,0:T(8,128)(2,1)S(1)} %get-tuple-element.22), channel_id=1, source_target_pairs={{0,8},{8,64},{64,72},{72,128},{128,136},{136,192},{192,200},{200,2... | collective-permute-start | bytes 786440 | tf_op jit(solution)/shard_map/ppermute | solution.py:276
  61.9 4.7 %shard_map.50.spectral_ref = bf16[32,4,16,512]{3,2,1,0:T(8,128)(2,1)S(1)} custom-call(bf16[256,1024]{1,0:T(8,128)(2,1)S(1)} %get-tuple-element.19.head_ref, f32[16,1024]{1,0:T(8,128)S(1)} %get-tuple-element.20.weight_ref, bf16[3072,512]{1,0:T(8,128)(2,1)S(1)} %get-tuple-element.21.rows_ref), custom_call_target="tpu_custom_call" | custom-call | tf_op jit(solution)/shard_map/pallas_call | solution.py:277
  66.7 0.0 collective-permute-done.4.upper_ref
  66.7 1.1 shard_map.51
  67.8 32.6 %all_to_all.21.in_ref = bf16[32,4,16,512]{3,2,1,0:T(8,128)(2,1)S(1)} all-to-all(bf16[32,4,16,512]{3,2,1,0:T(8,128)(2,1)S(1)} %shard_map.51), channel_id=1, replica_groups=mesh['y'=4,'x'=4,'core'=2,'gcol'=8] {'x','y','core'}, dimensions={0} | all-to-all | bytes 4194304 | tf_op jit(solution)/shard_map/all_to_all | solution.py:219
  100.3 2.3 %shard_map.52 = bf16[32,4,16,512]{3,2,1,0:T(8,128)(2,1)S(1)} custom-call(bf16[512,512]{1,0:T(8,128)(2,1)S(1)} %get-tuple-element.14.high_ref.high, bf16[512,512]{1,0:T(8,128)(2,1)S(1)} %get-tuple-element.15.low_ref.low, bf16[32,4,16,512]{3,2,1,0:T(8,128)(2,1)S(1)} %all_to_all.21.in_ref), custom_call_target="tpu_custom_call" | custom-call | tf_op jit(solution)/shard_map/pallas_call | solution.py:289
  102.6 31.9 %all_to_all.22.in_ref = bf16[32,4,16,512]{3,2,1,0:T(8,128)(2,1)S(1)} all-to-all(bf16[32,4,16,512]{3,2,1,0:T(8,128)(2,1)S(1)} %shard_map.52), channel_id=1, replica_groups=mesh['y'=4,'x'=4,'core'=2,'gcol'=8] {'x','y','core'}, dimensions={0} | all-to-all | bytes 4194304 | tf_op jit(solution)/shard_map/all_to_all | solution.py:219
  134.6 3.4 %shard_map.53 = f32[8,2,128,512]{3,2,1,0:T(8,128)} custom-call(bf16[32,4,16,512]{3,2,1,0:T(8,128)(2,1)S(1)} %all_to_all.22.in_ref), custom_call_target="tpu_custom_call" | custom-call | tf_op jit(solution)/shard_map/pallas_call | solution.py:290
  (7 shorter events, 0.1 us)
Async XLA Ops:
  0.0 1.5 %slice-start = ((bf16[512,2,512]{2,1,0:T(2,128)(2,1)}), bf16[512,2,128]{2,1,0:T(2,128)(2,1)S(1)}, s32[]{:S(2)}) async-start(bf16[512,2,512]{2,1,0:T(2,128)(2,1)} %param.4), calls=%async_computation.4 | async-start | bytes 524288 | tf_op jit(solution)/shard_map/slice | solution.py:250
  0.0 1.5 %copy-start.3 = (f32[512]{0:T(512)S(1)}, f32[512]{0:T(512)}, u32[]{:S(2)}) copy-start(f32[512]{0:T(512)} %param.7) | copy-start | bytes 6148
  0.0 1.5 %copy-start.2 = (s32[512]{0:T(512)S(1)}, s32[512]{0:T(512)}, u32[]{:S(2)}) copy-start(s32[512]{0:T(512)} %param.6) | copy-start | bytes 6148
  0.0 1.5 %copy-start.1 = (s32[512,1]{0,1:T(1,128)S(1)}, s32[512,1]{0,1:T(1,128)}, u32[]{:S(2)}) copy-start(s32[512,1]{0,1:T(1,128)} %param.5) | copy-start | bytes 6148
  3.3 1.4 copy-start
  4.7 38.3 %all-to-all-start = ((bf16[32,272,128]{2,1,0:T(8,128)(2,1)}), bf16[32,272,128]{2,1,0:T(8,128)(2,1)S(1)}, u32[]{:S(2)}, u32[]{:S(2)}) async-start(bf16[32,272,128]{2,1,0:T(8,128)(2,1)} %copy-done), calls=%async_computation | async-start | bytes 4456448 | tf_op jit(solution)/shard_map/all_to_all | solution.py:219
  13.3 13.8 %collective-permute-start.1 = (bf16[512,256]{1,0:T(8,128)(2,1)S(1)}, bf16[512,256]{1,0:T(8,128)(2,1)S(1)}, u32[]{:S(2)}, u32[]{:S(2)}) collective-permute-start(bf16[512,256]{1,0:T(8,128)(2,1)S(1)} %get-tuple-element.18), channel_id=1, source_target_pairs={{0,5},{8,13},{16,21},{24,29},{32,37},{40,45},{48,53},{56,61},{64,6... | collective-permute-start | bytes 786440 | tf_op jit(solution)/shard_map/ppermute | solution.py:209
  21.6 6.8 %collective-permute-start = (bf16[512,256]{1,0:T(8,128)(2,1)S(1)}, bf16[512,256]{1,0:T(8,128)(2,1)S(1)}, u32[]{:S(2)}, u32[]{:S(2)}) collective-permute-start(bf16[512,256]{1,0:T(8,128)(2,1)S(1)} %get-tuple-element.18), channel_id=1, source_target_pairs={{0,3},{8,11},{16,19},{24,27},{32,35},{40,43},{48,51},{56,59},{64,6... | collective-permute-start | bytes 786440 | tf_op jit(solution)/shard_map/ppermute | solution.py:208
  28.4 6.2 %copy-start.4 = (bf16[512,256]{1,0:T(8,128)(2,1)}, bf16[512,256]{1,0:T(8,128)(2,1)S(1)}, u32[]{:S(2)}) copy-start(bf16[512,256]{1,0:T(8,128)(2,1)S(1)} %select_select_fusion.1) | copy-start | bytes 786436
  28.5 6.2 %collective-permute-start.3 = (bf16[512,256]{1,0:T(8,128)(2,1)S(1)}, bf16[512,256]{1,0:T(8,128)(2,1)}, u32[]{:S(2)}, u32[]{:S(2)}) collective-permute-start(bf16[512,256]{1,0:T(8,128)(2,1)S(1)} %select_select_fusion.1), channel_id=1, source_target_pairs={{0,7},{3,2},{8,15},{11,10},{16,23},{19,18},{24,31},{27,26},{32,39}... | collective-permute-start | bytes 786440 | tf_op jit(solution)/shard_map/ppermute | solution.py:212
  30.4 6.1 %collective-permute-start.2 = (bf16[512,256]{1,0:T(8,128)(2,1)S(1)}, bf16[512,256]{1,0:T(8,128)(2,1)}, u32[]{:S(2)}, u32[]{:S(2)}) collective-permute-start(bf16[512,256]{1,0:T(8,128)(2,1)S(1)} %select_select_fusion.1), channel_id=1, source_target_pairs={{0,1},{3,4},{5,6},{8,9},{11,12},{13,14},{16,17},{19,20},{21,22},{2... | collective-permute-start | bytes 786440 | tf_op jit(solution)/shard_map/ppermute | solution.py:211
  59.9 6.8 %collective-permute-start.4 = (bf16[2,128,512]{2,1,0:T(8,128)(2,1)S(1)}, bf16[2,128,512]{2,1,0:T(8,128)(2,1)S(1)}, u32[]{:S(2)}, u32[]{:S(2)}) collective-permute-start(bf16[2,128,512]{2,1,0:T(8,128)(2,1)S(1)} %get-tuple-element.22), channel_id=1, source_target_pairs={{0,8},{8,64},{64,72},{72,128},{128,136},{136,192},{192,200},{200,2... | collective-permute-start | bytes 786440 | tf_op jit(solution)/shard_map/ppermute | solution.py:276

commit v5 on v4

--- a/solution.py
+++ b/solution.py
@@ -11,7 +11,8 @@
 NB = 256
 GW = 128
 LANES = 128
-EXTRA = 16
+EXTRA = 8
+WEIGHT_ROWS = 16
 ROW = 8
 BIN = ("y", "x", "core")
 ORDER = ("x", "y", "core")
@@ -78,8 +79,9 @@
 
     frac = frac_ref[...]
     place = iota((EXTRA, pairs), 0)
-    weight = jnp.where(place == offset_ref[...], (1.0 - frac).astype(BF16).astype(F32), 0.0)
-    weight += jnp.where(place == offset_ref[...] + 1, frac.astype(BF16).astype(F32), 0.0)
+    weight = jnp.where(place == 0, (1.0 - frac).astype(BF16).astype(F32), 0.0)
+    weight = jnp.where(place == 1, frac.astype(BF16).astype(F32), weight)
+    weight = jnp.where(place == 2, offset_ref[...].astype(F32), weight)
     weight = lax.dot_general(
         weight.astype(BF16), onehot, (((1,), (1,)), ((), ())), preferred_element_type=F32
     )
@@ -122,7 +124,10 @@
         tile = got_ref[share * at, extra:].astype(F32)
         for k in range(1, share):
             tile += got_ref[share * at + k, extra:].astype(F32)
-        weight_ref[:, at * LANES : (at + 1) * LANES] = tile
+        low, high, offset = (tile[n : n + 1] for n in range(3))
+        place = iota((WEIGHT_ROWS, LANES), 0).astype(F32)
+        weight = jnp.where(place == offset, low, 0.0) + jnp.where(place == offset + 1.0, high, 0.0)
+        weight_ref[:, at * LANES : (at + 1) * LANES] = weight
     weight = weight_ref[own_bins : own_bins + 1]
     scaled = [
         (head_ref[c * GW : (c + 1) * GW].astype(F32) * weight).astype(BF16) for c in range(2)
@@ -195,12 +200,14 @@
 
 def final_kernel(in_ref, out_ref, wide):
     groups, per, depth, lanes = in_ref.shape
-    wide[...] = in_ref[...].astype(F32).reshape(groups * per * depth, lanes)
-    for c in range(2):
-        for step in range(depth // 2):
-            out_ref[step, c] = wide[
-                pl.ds(c * (depth // 2) + step, groups * per, stride=depth), :
-            ]
+    for k in range(lanes // LANES):
+        at = slice(k * LANES, (k + 1) * LANES)
+        wide[k] = in_ref[:, :, :, at].astype(F32).reshape(groups * per * depth, LANES)
+        for c in range(2):
+            for step in range(depth // 2):
+                out_ref[step, c, :, at] = wide[
+                    k, pl.ds(c * (depth // 2) + step, groups * per, stride=depth), :
+                ]
 
 
 def from_first(block, axis):
@@ -226,7 +233,7 @@
     slots = groups * capacity
     own_bins = NB // groups
     per = GW // groups
-    blocks = 2
+    blocks = 1
     shape = jax.ShapeDtypeStruct
     scalar = pl.BlockSpec(memory_space=pltpu.SMEM)
     here = pl.BlockSpec(memory_space=pltpu.VMEM)
@@ -267,7 +274,7 @@
         functools.partial(prepare_kernel, own_bins),
         [
             shape((2 * GW, slots), BF16),
-            shape((EXTRA, slots), F32),
+            shape((WEIGHT_ROWS, slots), F32),
             shape((3 * slots, columns), BF16),
             shape((2, GW, columns), BF16),
         ],
@@ -278,7 +285,7 @@
         functools.partial(spectral_kernel, own_bins),
         shape((groups, per, 2 * own_bins, columns), BF16),
         grid=(blocks,),
-        in_specs=[whole(2 * GW, slots), whole(EXTRA, slots), whole(3 * slots, columns)],
+        in_specs=[whole(2 * GW, slots), whole(WEIGHT_ROWS, slots), whole(3 * slots, columns)],
         out_specs=pl.BlockSpec(
             (groups // blocks, per, 2 * own_bins, columns), lambda i: (i, 0, 0, 0)
         ),
@@ -290,12 +297,12 @@
     return call(
         final_kernel,
         shape((own_bins, 2, GW, columns), F32),
-        grid=(columns // LANES,),
+        grid=(2,),
         in_specs=[
-            pl.BlockSpec((groups, per, 2 * own_bins, LANES), lambda i: (0, 0, 0, i))
+            pl.BlockSpec((groups, per, 2 * own_bins, columns // 2), lambda i: (0, 0, 0, i))
         ],
-        out_specs=pl.BlockSpec((own_bins, 2, GW, LANES), lambda i: (0, 0, 0, i)),
-        scratch_shapes=[pltpu.VMEM((GW * 2 * own_bins, LANES), F32)],
+        out_specs=pl.BlockSpec((own_bins, 2, GW, columns // 2), lambda i: (0, 0, 0, i)),
+        scratch_shapes=[pltpu.VMEM((columns // LANES // 2, GW * 2 * own_bins, LANES), F32)],
     )(exchange(chi))
 
 

time: 138 us -> 137 us (level)
  no operation moved by 1% of the time
where the time goes in v5:
time: 137 us
  blocking collectives  79.8 us (58%)
  starting transfers between devices  24.3 us (18%)
  Pallas kernels  15.1 us (11%)
  waiting for transfers between devices  13.4 us (10%)
  local copies, waits for them, and re-layouts  2.82 us (2%)
    all_to_all x3, blocking collectives, exchange(): return lax.all_to_all(block, ORDER, split_axis=0, concat_axis=0, tiled=True)  79.8 us
    all_to_all x1, starting transfers between devices, exchange(): return lax.all_to_all(block, ORDER, split_axis=0, concat_axis=0, tiled=True)  8.59 us
    ppermute x1, starting transfers between devices, from_first(): behind = lax.ppermute(block, axis, [(0, 5)])  8.38 us
    all_to_all x1, waiting for transfers between devices, exchange(): return lax.all_to_all(block, ORDER, split_axis=0, concat_axis=0, tiled=True)  4.68 us
    pallas_call x1, Pallas kernels, on_device(): call(functools.partial(spectral_kernel, own_bins), shape((groups, per, 2...  4.5 us
    ppermute x1, waiting for transfers between devices, from_first(): behind = lax.ppermute(block, axis, [(0, 5)])  4.12 us
    pallas_call x1, Pallas kernels, on_device(): call(final_kernel, shape((own_bins, 2, GW, columns), F32), grid=(2,), in_...  3.07 us
    unnamed x12, local copies, waits for them, and re-layouts  2.82 us
  transfers between devices with their start and end apart: 6, of which 5 were waited for; matrix products, arithmetic and copies ran while one was open for 1% of the time, Pallas kernels for 4%

profile of v5, /device:TPU:1, one launch (start us, length us, event | category | flops | bytes accessed | tf_op | source)
XLA Modules:
  0.0 136.7 jit_solution(7571602674610055305)
XLA Ops:
  0.0 0.0 copy-start.1
  0.0 1.4 %copy.10 = bf16[512,2,512]{2,0,1:T(8,128)(2,1)S(1)} copy(bf16[512,2,512]{2,1,0:T(2,128)(2,1)} %param.4) | data formatting | bytes 2097152 | tf_op args[0]
  1.5 0.0 slice-done
  1.5 0.0 copy-done.3
  1.5 0.0 copy-done.2
  1.6 0.0 copy-done.1
  1.6 1.7 %shard_map.47 = (s32[1,512]{1,0:T(1,128)S(1)}, bf16[512,256]{1,0:T(8,128)(2,1)S(1)}, bf16[32,264,128]{2,1,0:T(8,128)(2,1)S(1)}) custom-call(s32[1]{0:T(128)} %bitcast.quarter_ref, s32[1,512]{1,0:T(1,128)S(1)} %bitcast.13, s32[1,512]{1,0:T(1,128)S(1)} %bitcast.14, f32[1,512]{1,0:T(1,128)S(1)} %bitcast.15, bf16[2,512,512]{2,1,0:T(8,128)(2,1)S(1)} %bitcast.11, ...), custom_call_target="tpu_custom_call" | custom-call | tf_op jit(solution)/shard_map/pallas_call | solution.py:243
  3.3 0.0 copy-start
  3.3 1.3 copy-done
  4.6 8.6 %all-to-all-start = ((bf16[32,264,128]{2,1,0:T(8,128)(2,1)}), bf16[32,264,128]{2,1,0:T(8,128)(2,1)S(1)}, u32[]{:S(2)}, u32[]{:S(2)}) async-start(bf16[32,264,128]{2,1,0:T(8,128)(2,1)} %copy-done), calls=%async_computation | async-start | bytes 4325376 | tf_op jit(solution)/shard_map/all_to_all | solution.py:226
  13.2 8.4 %collective-permute-start.1 = (bf16[512,256]{1,0:T(8,128)(2,1)S(1)}, bf16[512,256]{1,0:T(8,128)(2,1)S(1)}, u32[]{:S(2)}, u32[]{:S(2)}) collective-permute-start(bf16[512,256]{1,0:T(8,128)(2,1)S(1)} %get-tuple-element.18), channel_id=1, source_target_pairs={{0,5},{8,13},{16,21},{24,29},{32,37},{40,45},{48,53},{56,61},{64,6... | collective-permute-start | bytes 786440 | tf_op jit(solution)/shard_map/ppermute | solution.py:216
  21.6 1.3 collective-permute-start
  22.9 4.1 %collective-permute-done.1 = bf16[512,256]{1,0:T(8,128)(2,1)S(1)} collective-permute-done((bf16[512,256]{1,0:T(8,128)(2,1)S(1)}, bf16[512,256]{1,0:T(8,128)(2,1)S(1)}, u32[]{:S(2)}, u32[]{:S(2)}) %collective-permute-start.1) | collective-permute-done | bytes 262176 | tf_op jit(solution)/shard_map/ppermute | solution.py:216
  27.1 1.3 collective-permute-done
  28.4 2.0 %collective-permute-start.3 = (bf16[512,256]{1,0:T(8,128)(2,1)S(1)}, bf16[512,256]{1,0:T(8,128)(2,1)}, u32[]{:S(2)}, u32[]{:S(2)}) collective-permute-start(bf16[512,256]{1,0:T(8,128)(2,1)S(1)} %select_select_fusion.1), channel_id=1, source_target_pairs={{0,7},{3,2},{8,15},{11,10},{16,23},{19,18},{24,31},{27,26},{32,39}... | collective-permute-start | bytes 786440 | tf_op jit(solution)/shard_map/ppermute | solution.py:219
  30.4 2.0 %collective-permute-start.2 = (bf16[512,256]{1,0:T(8,128)(2,1)S(1)}, bf16[512,256]{1,0:T(8,128)(2,1)}, u32[]{:S(2)}, u32[]{:S(2)}) collective-permute-start(bf16[512,256]{1,0:T(8,128)(2,1)S(1)} %select_select_fusion.1), channel_id=1, source_target_pairs={{0,1},{3,4},{5,6},{8,9},{11,12},{13,14},{16,17},{19,20},{21,22},{2... | collective-permute-start | bytes 786440 | tf_op jit(solution)/shard_map/ppermute | solution.py:218
  32.4 0.8 shard_map.46
  33.2 1.3 collective-permute-done.3
  34.6 2.0 %collective-permute-done.2 = bf16[512,256]{1,0:T(8,128)(2,1)} collective-permute-done((bf16[512,256]{1,0:T(8,128)(2,1)S(1)}, bf16[512,256]{1,0:T(8,128)(2,1)}, u32[]{:S(2)}, u32[]{:S(2)}) %collective-permute-start.2) | collective-permute-done | bytes 262176 | tf_op jit(solution)/shard_map/ppermute | solution.py:218
  36.6 1.0 select_select_fusion.head_ref
  37.5 4.7 %all-to-all-done.arrived_ref.got_ref = bf16[32,264,128]{2,1,0:T(8,128)(2,1)S(1)} async-done(((bf16[32,264,128]{2,1,0:T(8,128)(2,1)}), bf16[32,264,128]{2,1,0:T(8,128)(2,1)S(1)}, u32[]{:S(2)}, u32[]{:S(2)}) %all-to-all-start) | async-done | bytes 2162720 | tf_op jit(solution)/shard_map/all_to_all | solution.py:226
  42.2 0.4 shard_map.48
  42.7 15.3 %all_to_all.20.got_head_ref = bf16[32,64,128]{2,1,0:T(8,128)(2,1)S(1)} all-to-all(bf16[32,64,128]{2,1,0:T(8,128)(2,1)S(1)} %shard_map.48), channel_id=1, replica_groups=mesh['y'=4,'x'=4,'core'=2,'gcol'=8] {'x','y','core'}, dimensions={0} | all-to-all | bytes 1048576 | tf_op jit(solution)/shard_map/all_to_all | solution.py:226
  57.9 1.2 shard_map.49
  59.1 2.1 %collective-permute-start.4 = (bf16[2,128,512]{2,1,0:T(8,128)(2,1)S(1)}, bf16[2,128,512]{2,1,0:T(8,128)(2,1)S(1)}, u32[]{:S(2)}, u32[]{:S(2)}) collective-permute-start(bf16[2,128,512]{2,1,0:T(8,128)(2,1)S(1)} %get-tuple-element.22), channel_id=1, source_target_pairs={{0,8},{8,64},{64,72},{72,128},{128,136},{136,192},{192,200},{200,2... | collective-permute-start | bytes 786440 | tf_op jit(solution)/shard_map/ppermute | solution.py:283
  61.2 4.5 %shard_map.50.spectral_ref = bf16[32,4,16,512]{3,2,1,0:T(8,128)(2,1)S(1)} custom-call(bf16[256,1024]{1,0:T(8,128)(2,1)S(1)} %get-tuple-element.19.head_ref, f32[16,1024]{1,0:T(8,128)S(1)} %get-tuple-element.20.weight_ref, bf16[3072,512]{1,0:T(8,128)(2,1)S(1)} %get-tuple-element.21.rows_ref), custom_call_target="tpu_custom_call" | custom-call | tf_op jit(solution)/shard_map/pallas_call | solution.py:284
  65.7 0.0 collective-permute-done.4.upper_ref
  65.7 1.1 shard_map.51
  66.8 32.6 %all_to_all.21.in_ref = bf16[32,4,16,512]{3,2,1,0:T(8,128)(2,1)S(1)} all-to-all(bf16[32,4,16,512]{3,2,1,0:T(8,128)(2,1)S(1)} %shard_map.51), channel_id=1, replica_groups=mesh['y'=4,'x'=4,'core'=2,'gcol'=8] {'x','y','core'}, dimensions={0} | all-to-all | bytes 4194304 | tf_op jit(solution)/shard_map/all_to_all | solution.py:226
  99.4 2.3 %shard_map.52 = bf16[32,4,16,512]{3,2,1,0:T(8,128)(2,1)S(1)} custom-call(bf16[512,512]{1,0:T(8,128)(2,1)S(1)} %get-tuple-element.14.high_ref.high, bf16[512,512]{1,0:T(8,128)(2,1)S(1)} %get-tuple-element.15.low_ref.low, bf16[32,4,16,512]{3,2,1,0:T(8,128)(2,1)S(1)} %all_to_all.21.in_ref), custom_call_target="tpu_custom_call" | custom-call | tf_op jit(solution)/shard_map/pallas_call | solution.py:296
  101.7 31.9 %all_to_all.22.in_ref = bf16[32,4,16,512]{3,2,1,0:T(8,128)(2,1)S(1)} all-to-all(bf16[32,4,16,512]{3,2,1,0:T(8,128)(2,1)S(1)} %shard_map.52), channel_id=1, replica_groups=mesh['y'=4,'x'=4,'core'=2,'gcol'=8] {'x','y','core'}, dimensions={0} | all-to-all | bytes 4194304 | tf_op jit(solution)/shard_map/all_to_all | solution.py:226
  133.6 3.1 %shard_map.53 = f32[8,2,128,512]{3,2,1,0:T(8,128)} custom-call(bf16[32,4,16,512]{3,2,1,0:T(8,128)(2,1)S(1)} %all_to_all.22.in_ref), custom_call_target="tpu_custom_call" | custom-call | tf_op jit(solution)/shard_map/pallas_call | solution.py:297
  (7 shorter events, 0.1 us)
Async XLA Ops:
  0.0 1.5 %slice-start = ((bf16[512,2,512]{2,1,0:T(2,128)(2,1)}), bf16[512,2,128]{2,1,0:T(2,128)(2,1)S(1)}, s32[]{:S(2)}) async-start(bf16[512,2,512]{2,1,0:T(2,128)(2,1)} %param.4), calls=%async_computation.4 | async-start | bytes 524288 | tf_op jit(solution)/shard_map/slice | solution.py:257
  0.0 1.5 %copy-start.3 = (f32[512]{0:T(512)S(1)}, f32[512]{0:T(512)}, u32[]{:S(2)}) copy-start(f32[512]{0:T(512)} %param.7) | copy-start | bytes 6148
  0.0 1.5 %copy-start.2 = (s32[512]{0:T(512)S(1)}, s32[512]{0:T(512)}, u32[]{:S(2)}) copy-start(s32[512]{0:T(512)} %param.6) | copy-start | bytes 6148
  0.0 1.5 %copy-start.1 = (s32[512,1]{0,1:T(1,128)S(1)}, s32[512,1]{0,1:T(1,128)}, u32[]{:S(2)}) copy-start(s32[512,1]{0,1:T(1,128)} %param.5) | copy-start | bytes 6148
  3.3 1.3 copy-start
  4.6 37.6 %all-to-all-start = ((bf16[32,264,128]{2,1,0:T(8,128)(2,1)}), bf16[32,264,128]{2,1,0:T(8,128)(2,1)S(1)}, u32[]{:S(2)}, u32[]{:S(2)}) async-start(bf16[32,264,128]{2,1,0:T(8,128)(2,1)} %copy-done), calls=%async_computation | async-start | bytes 4325376 | tf_op jit(solution)/shard_map/all_to_all | solution.py:226
  13.2 13.8 %collective-permute-start.1 = (bf16[512,256]{1,0:T(8,128)(2,1)S(1)}, bf16[512,256]{1,0:T(8,128)(2,1)S(1)}, u32[]{:S(2)}, u32[]{:S(2)}) collective-permute-start(bf16[512,256]{1,0:T(8,128)(2,1)S(1)} %get-tuple-element.18), channel_id=1, source_target_pairs={{0,5},{8,13},{16,21},{24,29},{32,37},{40,45},{48,53},{56,61},{64,6... | collective-permute-start | bytes 786440 | tf_op jit(solution)/shard_map/ppermute | solution.py:216
  21.6 6.8 %collective-permute-start = (bf16[512,256]{1,0:T(8,128)(2,1)S(1)}, bf16[512,256]{1,0:T(8,128)(2,1)S(1)}, u32[]{:S(2)}, u32[]{:S(2)}) collective-permute-start(bf16[512,256]{1,0:T(8,128)(2,1)S(1)} %get-tuple-element.18), channel_id=1, source_target_pairs={{0,3},{8,11},{16,19},{24,27},{32,35},{40,43},{48,51},{56,59},{64,6... | collective-permute-start | bytes 786440 | tf_op jit(solution)/shard_map/ppermute | solution.py:215
  28.4 6.2 %copy-start.4 = (bf16[512,256]{1,0:T(8,128)(2,1)}, bf16[512,256]{1,0:T(8,128)(2,1)S(1)}, u32[]{:S(2)}) copy-start(bf16[512,256]{1,0:T(8,128)(2,1)S(1)} %select_select_fusion.1) | copy-start | bytes 786436
  28.4 6.2 %collective-permute-start.3 = (bf16[512,256]{1,0:T(8,128)(2,1)S(1)}, bf16[512,256]{1,0:T(8,128)(2,1)}, u32[]{:S(2)}, u32[]{:S(2)}) collective-permute-start(bf16[512,256]{1,0:T(8,128)(2,1)S(1)} %select_select_fusion.1), channel_id=1, source_target_pairs={{0,7},{3,2},{8,15},{11,10},{16,23},{19,18},{24,31},{27,26},{32,39}... | collective-permute-start | bytes 786440 | tf_op jit(solution)/shard_map/ppermute | solution.py:219
  30.4 6.1 %collective-permute-start.2 = (bf16[512,256]{1,0:T(8,128)(2,1)S(1)}, bf16[512,256]{1,0:T(8,128)(2,1)}, u32[]{:S(2)}, u32[]{:S(2)}) collective-permute-start(bf16[512,256]{1,0:T(8,128)(2,1)S(1)} %select_select_fusion.1), channel_id=1, source_target_pairs={{0,1},{3,4},{5,6},{8,9},{11,12},{13,14},{16,17},{19,20},{21,22},{2... | collective-permute-start | bytes 786440 | tf_op jit(solution)/shard_map/ppermute | solution.py:218
  59.1 6.6 %collective-permute-start.4 = (bf16[2,128,512]{2,1,0:T(8,128)(2,1)S(1)}, bf16[2,128,512]{2,1,0:T(8,128)(2,1)S(1)}, u32[]{:S(2)}, u32[]{:S(2)}) collective-permute-start(bf16[2,128,512]{2,1,0:T(8,128)(2,1)S(1)} %get-tuple-element.22), channel_id=1, source_target_pairs={{0,8},{8,64},{64,72},{72,128},{128,136},{136,192},{192,200},{200,2... | collective-permute-start | bytes 786440 | tf_op jit(solution)/shard_map/ppermute | solution.py:283

commit v6 on v5

--- a/solution.py
+++ b/solution.py
@@ -80,7 +80,8 @@
     frac = frac_ref[...]
     place = iota((EXTRA, pairs), 0)
     weight = jnp.where(place == 0, (1.0 - frac).astype(BF16).astype(F32), 0.0)
-    weight = jnp.where(place == 1, frac.astype(BF16).astype(F32), weight)
+    inside = owner * (NB // groups) + offset_ref[...] < NB - 1
+    weight = jnp.where((place == 1) & inside, frac.astype(BF16).astype(F32), weight)
     weight = jnp.where(place == 2, offset_ref[...].astype(F32), weight)
     weight = lax.dot_general(
         weight.astype(BF16), onehot, (((1,), (1,)), ((), ())), preferred_element_type=F32
@@ -280,7 +281,7 @@
         ],
     )(got, got_head)
     path = [block_at(along_path(i)) for i in range(groups)]
-    upper = lax.ppermute(upper, BIN, list(zip(path[:-1], path[1:])))
+    upper = lax.ppermute(upper, BIN, list(zip(path, path[1:] + path[:1])))
     spectral = call(
         functools.partial(spectral_kernel, own_bins),
         shape((groups, per, 2 * own_bins, columns), BF16),

time: 137 us -> 136 us (level)
  starting transfers between devices: 24.3 us -> 22.5 us
    ppermute x1, starting transfers between devices: 2.06 us -> 0.24 us  [on_device(): upper = lax.ppermute(upper, BIN, list(zip(path, path[1:] + path[:1])))]
where the time goes in v6:
time: 136 us
  blocking collectives  80.8 us (59%)
  starting transfers between devices  22.5 us (17%)
  Pallas kernels  15.1 us (11%)
  waiting for transfers between devices  13.4 us (10%)
  local copies, waits for them, and re-layouts  2.82 us (2%)
    all_to_all x3, blocking collectives, exchange(): return lax.all_to_all(block, ORDER, split_axis=0, concat_axis=0, tiled=True)  80.8 us
    all_to_all x1, starting transfers between devices, exchange(): return lax.all_to_all(block, ORDER, split_axis=0, concat_axis=0, tiled=True)  8.59 us
    ppermute x1, starting transfers between devices, from_first(): behind = lax.ppermute(block, axis, [(0, 5)])  8.38 us
    all_to_all x1, waiting for transfers between devices, exchange(): return lax.all_to_all(block, ORDER, split_axis=0, concat_axis=0, tiled=True)  4.68 us
    pallas_call x1, Pallas kernels, on_device(): call(functools.partial(spectral_kernel, own_bins), shape((groups, per, 2...  4.5 us
    ppermute x1, waiting for transfers between devices, from_first(): behind = lax.ppermute(block, axis, [(0, 5)])  4.12 us
    pallas_call x1, Pallas kernels, on_device(): call(final_kernel, shape((own_bins, 2, GW, columns), F32), grid=(2,), in_...  3.07 us
    unnamed x12, local copies, waits for them, and re-layouts  2.82 us
  transfers between devices with their start and end apart: 6, of which 5 were waited for; matrix products, arithmetic and copies ran while one was open for 1% of the time, Pallas kernels for 4%

profile of v6, /device:TPU:1, one launch (start us, length us, event | category | flops | bytes accessed | tf_op | source)
XLA Modules:
  0.0 135.9 jit_solution(171184517456588302)
XLA Ops:
  0.0 0.0 copy-start.1
  0.0 1.4 %copy.10 = bf16[512,2,512]{2,0,1:T(8,128)(2,1)S(1)} copy(bf16[512,2,512]{2,1,0:T(2,128)(2,1)} %param.4) | data formatting | bytes 2097152 | tf_op args[0]
  1.5 0.0 slice-done
  1.5 0.0 copy-done.3
  1.5 0.0 copy-done.2
  1.6 1.7 %shard_map.47 = (s32[1,512]{1,0:T(1,128)S(1)}, bf16[512,256]{1,0:T(8,128)(2,1)S(1)}, bf16[32,264,128]{2,1,0:T(8,128)(2,1)S(1)}) custom-call(s32[1]{0:T(128)} %bitcast.quarter_ref, s32[1,512]{1,0:T(1,128)S(1)} %bitcast.13, s32[1,512]{1,0:T(1,128)S(1)} %bitcast.14, f32[1,512]{1,0:T(1,128)S(1)} %bitcast.15, bf16[2,512,512]{2,1,0:T(8,128)(2,1)S(1)} %bitcast.11, ...), custom_call_target="tpu_custom_call" | custom-call | tf_op jit(solution)/shard_map/pallas_call | solution.py:244
  3.3 0.0 copy-start
  3.3 1.3 copy-done
  4.6 8.6 %all-to-all-start = ((bf16[32,264,128]{2,1,0:T(8,128)(2,1)}), bf16[32,264,128]{2,1,0:T(8,128)(2,1)S(1)}, u32[]{:S(2)}, u32[]{:S(2)}) async-start(bf16[32,264,128]{2,1,0:T(8,128)(2,1)} %copy-done), calls=%async_computation | async-start | bytes 4325376 | tf_op jit(solution)/shard_map/all_to_all | solution.py:227
  13.2 8.4 %collective-permute-start.1 = (bf16[512,256]{1,0:T(8,128)(2,1)S(1)}, bf16[512,256]{1,0:T(8,128)(2,1)S(1)}, u32[]{:S(2)}, u32[]{:S(2)}) collective-permute-start(bf16[512,256]{1,0:T(8,128)(2,1)S(1)} %get-tuple-element.18), channel_id=1, source_target_pairs={{0,5},{8,13},{16,21},{24,29},{32,37},{40,45},{48,53},{56,61},{64,6... | collective-permute-start | bytes 786440 | tf_op jit(solution)/shard_map/ppermute | solution.py:217
  21.6 1.3 collective-permute-start
  22.9 4.1 %collective-permute-done.1 = bf16[512,256]{1,0:T(8,128)(2,1)S(1)} collective-permute-done((bf16[512,256]{1,0:T(8,128)(2,1)S(1)}, bf16[512,256]{1,0:T(8,128)(2,1)S(1)}, u32[]{:S(2)}, u32[]{:S(2)}) %collective-permute-start.1) | collective-permute-done | bytes 262176 | tf_op jit(solution)/shard_map/ppermute | solution.py:217
  27.1 1.3 collective-permute-done
  28.4 0.0 copy-start.4
  28.4 2.0 %collective-permute-start.3 = (bf16[512,256]{1,0:T(8,128)(2,1)S(1)}, bf16[512,256]{1,0:T(8,128)(2,1)}, u32[]{:S(2)}, u32[]{:S(2)}) collective-permute-start(bf16[512,256]{1,0:T(8,128)(2,1)S(1)} %select_select_fusion.1), channel_id=1, source_target_pairs={{0,7},{3,2},{8,15},{11,10},{16,23},{19,18},{24,31},{27,26},{32,39}... | collective-permute-start | bytes 786440 | tf_op jit(solution)/shard_map/ppermute | solution.py:220
  30.4 2.0 %collective-permute-start.2 = (bf16[512,256]{1,0:T(8,128)(2,1)S(1)}, bf16[512,256]{1,0:T(8,128)(2,1)}, u32[]{:S(2)}, u32[]{:S(2)}) collective-permute-start(bf16[512,256]{1,0:T(8,128)(2,1)S(1)} %select_select_fusion.1), channel_id=1, source_target_pairs={{0,1},{3,4},{5,6},{8,9},{11,12},{13,14},{16,17},{19,20},{21,22},{2... | collective-permute-start | bytes 786440 | tf_op jit(solution)/shard_map/ppermute | solution.py:219
  32.4 0.8 shard_map.46
  33.2 1.3 collective-permute-done.3
  34.6 2.0 %collective-permute-done.2 = bf16[512,256]{1,0:T(8,128)(2,1)} collective-permute-done((bf16[512,256]{1,0:T(8,128)(2,1)S(1)}, bf16[512,256]{1,0:T(8,128)(2,1)}, u32[]{:S(2)}, u32[]{:S(2)}) %collective-permute-start.2) | collective-permute-done | bytes 262176 | tf_op jit(solution)/shard_map/ppermute | solution.py:219
  36.6 1.0 select_select_fusion.head_ref
  37.5 4.7 %all-to-all-done.arrived_ref.got_ref = bf16[32,264,128]{2,1,0:T(8,128)(2,1)S(1)} async-done(((bf16[32,264,128]{2,1,0:T(8,128)(2,1)}), bf16[32,264,128]{2,1,0:T(8,128)(2,1)S(1)}, u32[]{:S(2)}, u32[]{:S(2)}) %all-to-all-start) | async-done | bytes 2162720 | tf_op jit(solution)/shard_map/all_to_all | solution.py:227
  42.2 0.4 shard_map.48
  42.7 15.3 %all_to_all.20.got_head_ref = bf16[32,64,128]{2,1,0:T(8,128)(2,1)S(1)} all-to-all(bf16[32,64,128]{2,1,0:T(8,128)(2,1)S(1)} %shard_map.48), channel_id=1, replica_groups=mesh['y'=4,'x'=4,'core'=2,'gcol'=8] {'x','y','core'}, dimensions={0} | all-to-all | bytes 1048576 | tf_op jit(solution)/shard_map/all_to_all | solution.py:227
  57.9 1.2 shard_map.49
  59.1 0.2 collective-permute-start.4
  59.4 4.5 %shard_map.50.spectral_ref = bf16[32,4,16,512]{3,2,1,0:T(8,128)(2,1)S(1)} custom-call(bf16[256,1024]{1,0:T(8,128)(2,1)S(1)} %get-tuple-element.19.head_ref, f32[16,1024]{1,0:T(8,128)S(1)} %get-tuple-element.20.weight_ref, bf16[3072,512]{1,0:T(8,128)(2,1)S(1)} %get-tuple-element.21.rows_ref), custom_call_target="tpu_custom_call" | custom-call | tf_op jit(solution)/shard_map/pallas_call | solution.py:285
  63.9 0.0 collective-permute-done.4.upper_ref
  63.9 1.1 shard_map.51
  65.0 33.6 %all_to_all.21.in_ref = bf16[32,4,16,512]{3,2,1,0:T(8,128)(2,1)S(1)} all-to-all(bf16[32,4,16,512]{3,2,1,0:T(8,128)(2,1)S(1)} %shard_map.51), channel_id=1, replica_groups=mesh['y'=4,'x'=4,'core'=2,'gcol'=8] {'x','y','core'}, dimensions={0} | all-to-all | bytes 4194304 | tf_op jit(solution)/shard_map/all_to_all | solution.py:227
  98.6 2.3 %shard_map.52 = bf16[32,4,16,512]{3,2,1,0:T(8,128)(2,1)S(1)} custom-call(bf16[512,512]{1,0:T(8,128)(2,1)S(1)} %get-tuple-element.14.high_ref.high, bf16[512,512]{1,0:T(8,128)(2,1)S(1)} %get-tuple-element.15.low_ref.low, bf16[32,4,16,512]{3,2,1,0:T(8,128)(2,1)S(1)} %all_to_all.21.in_ref), custom_call_target="tpu_custom_call" | custom-call | tf_op jit(solution)/shard_map/pallas_call | solution.py:297
  100.9 31.9 %all_to_all.22.in_ref = bf16[32,4,16,512]{3,2,1,0:T(8,128)(2,1)S(1)} all-to-all(bf16[32,4,16,512]{3,2,1,0:T(8,128)(2,1)S(1)} %shard_map.52), channel_id=1, replica_groups=mesh['y'=4,'x'=4,'core'=2,'gcol'=8] {'x','y','core'}, dimensions={0} | all-to-all | bytes 4194304 | tf_op jit(solution)/shard_map/all_to_all | solution.py:227
  132.8 3.1 %shard_map.53 = f32[8,2,128,512]{3,2,1,0:T(8,128)} custom-call(bf16[32,4,16,512]{3,2,1,0:T(8,128)(2,1)S(1)} %all_to_all.22.in_ref), custom_call_target="tpu_custom_call" | custom-call | tf_op jit(solution)/shard_map/pallas_call | solution.py:298
  (7 shorter events, 0.1 us)
Async XLA Ops:
  0.0 1.5 %slice-start = ((bf16[512,2,512]{2,1,0:T(2,128)(2,1)}), bf16[512,2,128]{2,1,0:T(2,128)(2,1)S(1)}, s32[]{:S(2)}) async-start(bf16[512,2,512]{2,1,0:T(2,128)(2,1)} %param.4), calls=%async_computation.4 | async-start | bytes 524288 | tf_op jit(solution)/shard_map/slice | solution.py:258
  0.0 1.5 %copy-start.3 = (f32[512]{0:T(512)S(1)}, f32[512]{0:T(512)}, u32[]{:S(2)}) copy-start(f32[512]{0:T(512)} %param.7) | copy-start | bytes 6148
  0.0 1.5 %copy-start.2 = (s32[512]{0:T(512)S(1)}, s32[512]{0:T(512)}, u32[]{:S(2)}) copy-start(s32[512]{0:T(512)} %param.6) | copy-start | bytes 6148
  0.0 1.5 %copy-start.1 = (s32[512,1]{0,1:T(1,128)S(1)}, s32[512,1]{0,1:T(1,128)}, u32[]{:S(2)}) copy-start(s32[512,1]{0,1:T(1,128)} %param.5) | copy-start | bytes 6148
  3.3 1.3 copy-start
  4.6 37.6 %all-to-all-start = ((bf16[32,264,128]{2,1,0:T(8,128)(2,1)}), bf16[32,264,128]{2,1,0:T(8,128)(2,1)S(1)}, u32[]{:S(2)}, u32[]{:S(2)}) async-start(bf16[32,264,128]{2,1,0:T(8,128)(2,1)} %copy-done), calls=%async_computation | async-start | bytes 4325376 | tf_op jit(solution)/shard_map/all_to_all | solution.py:227
  13.2 13.8 %collective-permute-start.1 = (bf16[512,256]{1,0:T(8,128)(2,1)S(1)}, bf16[512,256]{1,0:T(8,128)(2,1)S(1)}, u32[]{:S(2)}, u32[]{:S(2)}) collective-permute-start(bf16[512,256]{1,0:T(8,128)(2,1)S(1)} %get-tuple-element.18), channel_id=1, source_target_pairs={{0,5},{8,13},{16,21},{24,29},{32,37},{40,45},{48,53},{56,61},{64,6... | collective-permute-start | bytes 786440 | tf_op jit(solution)/shard_map/ppermute | solution.py:217
  21.6 6.8 %collective-permute-start = (bf16[512,256]{1,0:T(8,128)(2,1)S(1)}, bf16[512,256]{1,0:T(8,128)(2,1)S(1)}, u32[]{:S(2)}, u32[]{:S(2)}) collective-permute-start(bf16[512,256]{1,0:T(8,128)(2,1)S(1)} %get-tuple-element.18), channel_id=1, source_target_pairs={{0,3},{8,11},{16,19},{24,27},{32,35},{40,43},{48,51},{56,59},{64,6... | collective-permute-start | bytes 786440 | tf_op jit(solution)/shard_map/ppermute | solution.py:216
  28.4 6.2 %copy-start.4 = (bf16[512,256]{1,0:T(8,128)(2,1)}, bf16[512,256]{1,0:T(8,128)(2,1)S(1)}, u32[]{:S(2)}) copy-start(bf16[512,256]{1,0:T(8,128)(2,1)S(1)} %select_select_fusion.1) | copy-start | bytes 786436
  28.4 6.2 %collective-permute-start.3 = (bf16[512,256]{1,0:T(8,128)(2,1)S(1)}, bf16[512,256]{1,0:T(8,128)(2,1)}, u32[]{:S(2)}, u32[]{:S(2)}) collective-permute-start(bf16[512,256]{1,0:T(8,128)(2,1)S(1)} %select_select_fusion.1), channel_id=1, source_target_pairs={{0,7},{3,2},{8,15},{11,10},{16,23},{19,18},{24,31},{27,26},{32,39}... | collective-permute-start | bytes 786440 | tf_op jit(solution)/shard_map/ppermute | solution.py:220
  30.4 6.1 %collective-permute-start.2 = (bf16[512,256]{1,0:T(8,128)(2,1)S(1)}, bf16[512,256]{1,0:T(8,128)(2,1)}, u32[]{:S(2)}, u32[]{:S(2)}) collective-permute-start(bf16[512,256]{1,0:T(8,128)(2,1)S(1)} %select_select_fusion.1), channel_id=1, source_target_pairs={{0,1},{3,4},{5,6},{8,9},{11,12},{13,14},{16,17},{19,20},{21,22},{2... | collective-permute-start | bytes 786440 | tf_op jit(solution)/shard_map/ppermute | solution.py:219
  59.1 4.7 %collective-permute-start.4 = (bf16[2,128,512]{2,1,0:T(8,128)(2,1)S(1)}, bf16[2,128,512]{2,1,0:T(8,128)(2,1)S(1)}, u32[]{:S(2)}, u32[]{:S(2)}) collective-permute-start(bf16[2,128,512]{2,1,0:T(8,128)(2,1)S(1)} %get-tuple-element.22), channel_id=1, source_target_pairs={{0,8},{8,64},{64,72},{72,128},{128,136},{136,192},{192,200},{200,2... | collective-permute-start | bytes 786440 | tf_op jit(solution)/shard_map/ppermute | solution.py:284

commit v7 on v6

--- a/solution.py
+++ b/solution.py
@@ -57,13 +57,14 @@
 
 
 def pack_rows_kernel(
-    quarter_ref, owner_ref, offset_ref, frac_ref, rows_ref, head_ref, target_ref, copy_ref, out_ref
+    quarter_ref, owner_ref, offset_ref, frac_ref, rows_ref, target_ref, copy_ref, out_ref
 ):
     groups, depth, _ = out_ref.shape
     pairs = owner_ref.shape[1]
     tiles = rows_ref.shape[2] // LANES
     capacity = (depth - EXTRA) // (2 * tiles)
-    copy_ref[...] = head_ref[...]
+    for c in range(2):
+        copy_ref[:, c * GW : (c + 1) * GW] = rows_ref[c, :, :GW]
     owner = owner_ref[...]
     named = (iota((groups, pairs), 0) == owner).astype(F32)
     before = (iota((pairs, pairs), 0) < iota((pairs, pairs), 1)).astype(F32).astype(BF16)
@@ -162,11 +163,12 @@
 def carry_kernel(spectral_ref, upper_ref, out_ref):
     groups, per, bins, width = out_ref.shape
     place = iota((groups * per, bins, width), 1)
-    values = spectral_ref[...].astype(F32).reshape(groups * per, bins, width)
+    added = jnp.zeros((groups * per, bins, width), F32)
     for c in range(2):
         upper = upper_ref[c].astype(F32).reshape(groups * per, 1, width)
-        values = values + jnp.where(place == c * (bins // 2), upper, 0.0)
-    out_ref[...] = values.astype(BF16).reshape(groups, per, bins, width)
+        added = jnp.where(place == c * (bins // 2), upper, added)
+    values = spectral_ref[...].reshape(groups * per, bins, width) + added.astype(BF16)
+    out_ref[...] = values.reshape(groups, per, bins, width)
 
 
 def table_kernel(own_bins, high_ref, low_ref):
@@ -248,14 +250,13 @@
             shape((pairs, 2 * GW), BF16),
             shape((groups, 2 * capacity * columns // LANES + EXTRA, LANES), BF16),
         ],
-        in_specs=[scalar] + [here] * 5,
+        in_specs=[scalar] + [here] * 4,
     )(
         quarter.reshape(1),
         pair_owner.reshape(1, pairs),
         pair_offset.reshape(1, pairs),
         pair_frac.reshape(1, pairs),
         by_part,
-        pair_rows[:, :, :GW].reshape(pairs, 2 * GW),
     )
     got = exchange(packed)
     head = from_first(head, "gcol")

time: 136 us -> 136 us (level)
    unnamed x12 -> x11, local copies, waits for them, and re-layouts: 2.82 us -> 2.76 us
where the time goes in v7:
time: 136 us
  blocking collectives  80.8 us (59%)
  starting transfers between devices  22.5 us (17%)
  Pallas kernels  15 us (11%)
  waiting for transfers between devices  13.4 us (10%)
  local copies, waits for them, and re-layouts  2.76 us (2%)
    all_to_all x3, blocking collectives, exchange(): return lax.all_to_all(block, ORDER, split_axis=0, concat_axis=0, tiled=True)  80.8 us
    all_to_all x1, starting transfers between devices, exchange(): return lax.all_to_all(block, ORDER, split_axis=0, concat_axis=0, tiled=True)  8.59 us
    ppermute x1, starting transfers between devices, from_first(): behind = lax.ppermute(block, axis, [(0, 5)])  8.38 us
    all_to_all x1, waiting for transfers between devices, exchange(): return lax.all_to_all(block, ORDER, split_axis=0, concat_axis=0, tiled=True)  4.67 us
    pallas_call x1, Pallas kernels, on_device(): call(functools.partial(spectral_kernel, own_bins), shape((groups, per, 2...  4.5 us
    ppermute x1, waiting for transfers between devices, from_first(): behind = lax.ppermute(block, axis, [(0, 5)])  4.12 us
    pallas_call x1, Pallas kernels, on_device(): call(final_kernel, shape((own_bins, 2, GW, columns), F32), grid=(2,), in_...  3.07 us
    unnamed x11, local copies, waits for them, and re-layouts  2.76 us
  transfers between devices with their start and end apart: 6, of which 5 were waited for; matrix products, arithmetic and copies ran while one was open for 1% of the time, Pallas kernels for 4%

profile of v7, /device:TPU:1, one launch (start us, length us, event | category | flops | bytes accessed | tf_op | source)
XLA Modules:
  0.0 135.7 jit_solution(3840313033663344380)
XLA Ops:
  0.0 1.4 %copy.8 = bf16[512,2,512]{2,0,1:T(8,128)(2,1)S(1)} copy(bf16[512,2,512]{2,1,0:T(2,128)(2,1)} %param.4) | data formatting | bytes 2097152 | tf_op args[0]
  1.4 0.0 copy-done.3
  1.5 0.0 copy-done.2
  1.5 0.0 copy-done.1
  1.5 1.7 %shard_map.47 = (s32[1,512]{1,0:T(1,128)S(1)}, bf16[512,256]{1,0:T(8,128)(2,1)S(1)}, bf16[32,264,128]{2,1,0:T(8,128)(2,1)S(1)}) custom-call(s32[1]{0:T(128)} %bitcast.quarter_ref, s32[1,512]{1,0:T(1,128)S(1)} %bitcast.8, s32[1,512]{1,0:T(1,128)S(1)} %bitcast.9, f32[1,512]{1,0:T(1,128)S(1)} %bitcast.10, bf16[2,512,512]{2,1,0:T(8,128)(2,1)S(1)} %bitcast.7), custom_call_target="tpu_custom_call" | custom-call | tf_op jit(solution)/shard_map/pallas_call | solution.py:246
  3.2 0.0 copy-start
  3.2 1.3 copy-done
  4.5 8.6 %all-to-all-start = ((bf16[32,264,128]{2,1,0:T(8,128)(2,1)}), bf16[32,264,128]{2,1,0:T(8,128)(2,1)S(1)}, u32[]{:S(2)}, u32[]{:S(2)}) async-start(bf16[32,264,128]{2,1,0:T(8,128)(2,1)} %copy-done), calls=%async_computation | async-start | bytes 4325376 | tf_op jit(solution)/shard_map/all_to_all | solution.py:229
  13.1 8.4 %collective-permute-start.1 = (bf16[512,256]{1,0:T(8,128)(2,1)S(1)}, bf16[512,256]{1,0:T(8,128)(2,1)S(1)}, u32[]{:S(2)}, u32[]{:S(2)}) collective-permute-start(bf16[512,256]{1,0:T(8,128)(2,1)S(1)} %get-tuple-element.18), channel_id=1, source_target_pairs={{0,5},{8,13},{16,21},{24,29},{32,37},{40,45},{48,53},{56,61},{64,6... | collective-permute-start | bytes 786440 | tf_op jit(solution)/shard_map/ppermute | solution.py:219
  21.5 1.3 collective-permute-start
  22.9 4.1 %collective-permute-done.1 = bf16[512,256]{1,0:T(8,128)(2,1)S(1)} collective-permute-done((bf16[512,256]{1,0:T(8,128)(2,1)S(1)}, bf16[512,256]{1,0:T(8,128)(2,1)S(1)}, u32[]{:S(2)}, u32[]{:S(2)}) %collective-permute-start.1) | collective-permute-done | bytes 262176 | tf_op jit(solution)/shard_map/ppermute | solution.py:219
  27.0 1.3 collective-permute-done
  28.3 0.0 copy-start.4
  28.3 2.0 %collective-permute-start.3 = (bf16[512,256]{1,0:T(8,128)(2,1)S(1)}, bf16[512,256]{1,0:T(8,128)(2,1)}, u32[]{:S(2)}, u32[]{:S(2)}) collective-permute-start(bf16[512,256]{1,0:T(8,128)(2,1)S(1)} %select_select_fusion.1), channel_id=1, source_target_pairs={{0,7},{3,2},{8,15},{11,10},{16,23},{19,18},{24,31},{27,26},{32,39}... | collective-permute-start | bytes 786440 | tf_op jit(solution)/shard_map/ppermute | solution.py:222
  30.3 2.0 %collective-permute-start.2 = (bf16[512,256]{1,0:T(8,128)(2,1)S(1)}, bf16[512,256]{1,0:T(8,128)(2,1)}, u32[]{:S(2)}, u32[]{:S(2)}) collective-permute-start(bf16[512,256]{1,0:T(8,128)(2,1)S(1)} %select_select_fusion.1), channel_id=1, source_target_pairs={{0,1},{3,4},{5,6},{8,9},{11,12},{13,14},{16,17},{19,20},{21,22},{2... | collective-permute-start | bytes 786440 | tf_op jit(solution)/shard_map/ppermute | solution.py:221
  32.3 0.8 shard_map.46
  33.2 1.3 collective-permute-done.3
  34.5 0.0 copy-done.4
  34.5 2.0 %collective-permute-done.2 = bf16[512,256]{1,0:T(8,128)(2,1)} collective-permute-done((bf16[512,256]{1,0:T(8,128)(2,1)S(1)}, bf16[512,256]{1,0:T(8,128)(2,1)}, u32[]{:S(2)}, u32[]{:S(2)}) %collective-permute-start.2) | collective-permute-done | bytes 262176 | tf_op jit(solution)/shard_map/ppermute | solution.py:221
  36.5 1.0 select_select_fusion.head_ref
  37.5 4.7 %all-to-all-done.arrived_ref.got_ref = bf16[32,264,128]{2,1,0:T(8,128)(2,1)S(1)} async-done(((bf16[32,264,128]{2,1,0:T(8,128)(2,1)}), bf16[32,264,128]{2,1,0:T(8,128)(2,1)S(1)}, u32[]{:S(2)}, u32[]{:S(2)}) %all-to-all-start) | async-done | bytes 2162720 | tf_op jit(solution)/shard_map/all_to_all | solution.py:229
  42.1 0.4 shard_map.48
  42.6 15.3 %all_to_all.20.got_head_ref = bf16[32,64,128]{2,1,0:T(8,128)(2,1)S(1)} all-to-all(bf16[32,64,128]{2,1,0:T(8,128)(2,1)S(1)} %shard_map.48), channel_id=1, replica_groups=mesh['y'=4,'x'=4,'core'=2,'gcol'=8] {'x','y','core'}, dimensions={0} | all-to-all | bytes 1048576 | tf_op jit(solution)/shard_map/all_to_all | solution.py:229
  57.9 1.2 shard_map.49
  59.1 0.2 collective-permute-start.4
  59.3 4.5 %shard_map.50.spectral_ref = bf16[32,4,16,512]{3,2,1,0:T(8,128)(2,1)S(1)} custom-call(bf16[256,1024]{1,0:T(8,128)(2,1)S(1)} %get-tuple-element.19.head_ref, f32[16,1024]{1,0:T(8,128)S(1)} %get-tuple-element.20.weight_ref, bf16[3072,512]{1,0:T(8,128)(2,1)S(1)} %get-tuple-element.21.rows_ref), custom_call_target="tpu_custom_call" | custom-call | tf_op jit(solution)/shard_map/pallas_call | solution.py:286
  63.8 0.0 collective-permute-done.4.upper_ref
  63.8 1.0 shard_map.51
  64.8 33.6 %all_to_all.21.in_ref = bf16[32,4,16,512]{3,2,1,0:T(8,128)(2,1)S(1)} all-to-all(bf16[32,4,16,512]{3,2,1,0:T(8,128)(2,1)S(1)} %shard_map.51), channel_id=1, replica_groups=mesh['y'=4,'x'=4,'core'=2,'gcol'=8] {'x','y','core'}, dimensions={0} | all-to-all | bytes 4194304 | tf_op jit(solution)/shard_map/all_to_all | solution.py:229
  98.4 2.3 %shard_map.52 = bf16[32,4,16,512]{3,2,1,0:T(8,128)(2,1)S(1)} custom-call(bf16[512,512]{1,0:T(8,128)(2,1)S(1)} %get-tuple-element.14.high_ref.high, bf16[512,512]{1,0:T(8,128)(2,1)S(1)} %get-tuple-element.15.low_ref.low, bf16[32,4,16,512]{3,2,1,0:T(8,128)(2,1)S(1)} %all_to_all.21.in_ref), custom_call_target="tpu_custom_call" | custom-call | tf_op jit(solution)/shard_map/pallas_call | solution.py:298
  100.8 31.9 %all_to_all.22.in_ref = bf16[32,4,16,512]{3,2,1,0:T(8,128)(2,1)S(1)} all-to-all(bf16[32,4,16,512]{3,2,1,0:T(8,128)(2,1)S(1)} %shard_map.52), channel_id=1, replica_groups=mesh['y'=4,'x'=4,'core'=2,'gcol'=8] {'x','y','core'}, dimensions={0} | all-to-all | bytes 4194304 | tf_op jit(solution)/shard_map/all_to_all | solution.py:229
  132.6 3.1 %shard_map.53 = f32[8,2,128,512]{3,2,1,0:T(8,128)} custom-call(bf16[32,4,16,512]{3,2,1,0:T(8,128)(2,1)S(1)} %all_to_all.22.in_ref), custom_call_target="tpu_custom_call" | custom-call | tf_op jit(solution)/shard_map/pallas_call | solution.py:299
  (4 shorter events, 0.0 us)
Async XLA Ops:
  0.0 1.5 %copy-start.3 = (f32[512]{0:T(512)S(1)}, f32[512]{0:T(512)}, u32[]{:S(2)}) copy-start(f32[512]{0:T(512)} %param.7) | copy-start | bytes 6148
  0.0 1.5 %copy-start.2 = (s32[512]{0:T(512)S(1)}, s32[512]{0:T(512)}, u32[]{:S(2)}) copy-start(s32[512]{0:T(512)} %param.6) | copy-start | bytes 6148
  0.0 1.5 %copy-start.1 = (s32[512,1]{0,1:T(1,128)S(1)}, s32[512,1]{0,1:T(1,128)}, u32[]{:S(2)}) copy-start(s32[512,1]{0,1:T(1,128)} %param.5) | copy-start | bytes 6148
  3.2 1.3 copy-start
  4.5 37.6 %all-to-all-start = ((bf16[32,264,128]{2,1,0:T(8,128)(2,1)}), bf16[32,264,128]{2,1,0:T(8,128)(2,1)S(1)}, u32[]{:S(2)}, u32[]{:S(2)}) async-start(bf16[32,264,128]{2,1,0:T(8,128)(2,1)} %copy-done), calls=%async_computation | async-start | bytes 4325376 | tf_op jit(solution)/shard_map/all_to_all | solution.py:229
  13.1 13.8 %collective-permute-start.1 = (bf16[512,256]{1,0:T(8,128)(2,1)S(1)}, bf16[512,256]{1,0:T(8,128)(2,1)S(1)}, u32[]{:S(2)}, u32[]{:S(2)}) collective-permute-start(bf16[512,256]{1,0:T(8,128)(2,1)S(1)} %get-tuple-element.18), channel_id=1, source_target_pairs={{0,5},{8,13},{16,21},{24,29},{32,37},{40,45},{48,53},{56,61},{64,6... | collective-permute-start | bytes 786440 | tf_op jit(solution)/shard_map/ppermute | solution.py:219
  21.5 6.8 %collective-permute-start = (bf16[512,256]{1,0:T(8,128)(2,1)S(1)}, bf16[512,256]{1,0:T(8,128)(2,1)S(1)}, u32[]{:S(2)}, u32[]{:S(2)}) collective-permute-start(bf16[512,256]{1,0:T(8,128)(2,1)S(1)} %get-tuple-element.18), channel_id=1, source_target_pairs={{0,3},{8,11},{16,19},{24,27},{32,35},{40,43},{48,51},{56,59},{64,6... | collective-permute-start | bytes 786440 | tf_op jit(solution)/shard_map/ppermute | solution.py:218
  28.3 6.2 %copy-start.4 = (bf16[512,256]{1,0:T(8,128)(2,1)}, bf16[512,256]{1,0:T(8,128)(2,1)S(1)}, u32[]{:S(2)}) copy-start(bf16[512,256]{1,0:T(8,128)(2,1)S(1)} %select_select_fusion.1) | copy-start | bytes 786436
  28.3 6.2 %collective-permute-start.3 = (bf16[512,256]{1,0:T(8,128)(2,1)S(1)}, bf16[512,256]{1,0:T(8,128)(2,1)}, u32[]{:S(2)}, u32[]{:S(2)}) collective-permute-start(bf16[512,256]{1,0:T(8,128)(2,1)S(1)} %select_select_fusion.1), channel_id=1, source_target_pairs={{0,7},{3,2},{8,15},{11,10},{16,23},{19,18},{24,31},{27,26},{32,39}... | collective-permute-start | bytes 786440 | tf_op jit(solution)/shard_map/ppermute | solution.py:222
  30.3 6.1 %collective-permute-start.2 = (bf16[512,256]{1,0:T(8,128)(2,1)S(1)}, bf16[512,256]{1,0:T(8,128)(2,1)}, u32[]{:S(2)}, u32[]{:S(2)}) collective-permute-start(bf16[512,256]{1,0:T(8,128)(2,1)S(1)} %select_select_fusion.1), channel_id=1, source_target_pairs={{0,1},{3,4},{5,6},{8,9},{11,12},{13,14},{16,17},{19,20},{21,22},{2... | collective-permute-start | bytes 786440 | tf_op jit(solution)/shard_map/ppermute | solution.py:221
  59.1 4.8 %collective-permute-start.4 = (bf16[2,128,512]{2,1,0:T(8,128)(2,1)S(1)}, bf16[2,128,512]{2,1,0:T(8,128)(2,1)S(1)}, u32[]{:S(2)}, u32[]{:S(2)}) collective-permute-start(bf16[2,128,512]{2,1,0:T(8,128)(2,1)S(1)} %get-tuple-element.22), channel_id=1, source_target_pairs={{0,8},{8,64},{64,72},{72,128},{128,136},{136,192},{192,200},{200,2... | collective-permute-start | bytes 786440 | tf_op jit(solution)/shard_map/ppermute | solution.py:285

commit v8 on v7

--- a/solution.py
+++ b/solution.py
@@ -97,7 +97,7 @@
         out_ref[group, depth - EXTRA :] = tile.astype(BF16)
 
 
-def pack_heads_kernel(target_ref, head_ref, arrived_ref, high_ref, low_ref, out_ref):
+def pack_heads_kernel(target_ref, head_ref, arrived_ref, table_ref, out_ref):
     groups, double, lanes = out_ref.shape
     capacity = double // 2
     onehot = slot_onehot(target_ref[...], groups * capacity)
@@ -171,8 +171,8 @@
     out_ref[...] = values.reshape(groups, per, bins, width)
 
 
-def table_kernel(own_bins, high_ref, low_ref):
-    shape = high_ref.shape
+def table_kernel(own_bins, out_ref):
+    shape = (out_ref.shape[0] // 2, out_ref.shape[1])
     row = iota(shape, 0)
     column = iota(shape, 1)
     group = 2 * own_bins
@@ -189,15 +189,16 @@
     crossed = jnp.where(row_imag, imag_part, -imag_part)
     table = jnp.where(row_imag == column_imag, real_part, crossed)
     high = table.astype(BF16)
-    high_ref[...] = high
-    low_ref[...] = (table - high.astype(F32)).astype(BF16)
-
-
-def hilbert_kernel(high, low, in_ref, out_ref):
+    out_ref[: shape[0]] = high
+    out_ref[shape[0] :] = (table - high.astype(F32)).astype(BF16)
+
+
+def hilbert_kernel(table_ref, in_ref, out_ref):
     groups, per, bins, width = out_ref.shape
     for g in range(per):
         values = in_ref[:, g].reshape(groups * bins, width)
-        result = dot(high[...], values) + dot(low[...], values)
+        result = dot(table_ref[...], values)
+        result = result[: groups * bins] + result[groups * bins :]
         out_ref[:, g] = result.astype(BF16).reshape(groups, bins, width)
 
 
@@ -260,15 +261,15 @@
     )
     got = exchange(packed)
     head = from_first(head, "gcol")
-    high, low = call(
-        functools.partial(table_kernel, own_bins), [shape((2 * NB, 2 * NB), BF16)] * 2
+    table = call(
+        functools.partial(table_kernel, own_bins), shape((4 * NB, 2 * NB), BF16)
     )()
     got_head = exchange(
         call(
             pack_heads_kernel,
             shape((groups, 2 * capacity, GW), BF16),
-            in_specs=[here] * 2 + [pl.BlockSpec(memory_space=pl.ANY)] * 3,
-        )(target, head, got, high, low)
+            in_specs=[here] * 2 + [pl.BlockSpec(memory_space=pl.ANY)] * 2,
+        )(target, head, got, table)
     )
 
     whole = lambda *dims: pl.BlockSpec(dims, lambda i: (0,) * len(dims))
@@ -295,7 +296,7 @@
     spectral = call(
         carry_kernel, shape(spectral.shape, BF16), input_output_aliases={0: 0}
     )(spectral, upper)
-    chi = call(hilbert_kernel, shape(spectral.shape, BF16))(high, low, exchange(spectral))
+    chi = call(hilbert_kernel, shape(spectral.shape, BF16))(table, exchange(spectral))
     return call(
         final_kernel,
         shape((own_bins, 2, GW, columns), F32),

time: 136 us -> 136 us (level)
  no operation moved by 1% of the time
where the time goes in v8:
time: 136 us
  blocking collectives  80.8 us (59%)
  starting transfers between devices  22.5 us (17%)
  Pallas kernels  15 us (11%)
  waiting for transfers between devices  13.4 us (10%)
  local copies, waits for them, and re-layouts  2.76 us (2%)
    all_to_all x3, blocking collectives, exchange(): return lax.all_to_all(block, ORDER, split_axis=0, concat_axis=0, tiled=True)  80.8 us
    all_to_all x1, starting transfers between devices, exchange(): return lax.all_to_all(block, ORDER, split_axis=0, concat_axis=0, tiled=True)  8.59 us
    ppermute x1, starting transfers between devices, from_first(): behind = lax.ppermute(block, axis, [(0, 5)])  8.38 us
    all_to_all x1, waiting for transfers between devices, exchange(): return lax.all_to_all(block, ORDER, split_axis=0, concat_axis=0, tiled=True)  4.67 us
    pallas_call x1, Pallas kernels, on_device(): call(functools.partial(spectral_kernel, own_bins), shape((groups, per, 2...  4.5 us
    ppermute x1, waiting for transfers between devices, from_first(): behind = lax.ppermute(block, axis, [(0, 5)])  4.12 us
    pallas_call x1, Pallas kernels, on_device(): call(final_kernel, shape((own_bins, 2, GW, columns), F32), grid=(2,), in_...  3.07 us
    unnamed x11, local copies, waits for them, and re-layouts  2.76 us
  transfers between devices with their start and end apart: 6, of which 5 were waited for; matrix products, arithmetic and copies ran while one was open for 1% of the time, Pallas kernels for 4%

profile of v8, /device:TPU:1, one launch (start us, length us, event | category | flops | bytes accessed | tf_op | source)
XLA Modules:
  0.0 135.7 jit_solution(15456646290395591334)
XLA Ops:
  0.0 1.4 %copy.8 = bf16[512,2,512]{2,0,1:T(8,128)(2,1)S(1)} copy(bf16[512,2,512]{2,1,0:T(2,128)(2,1)} %param.4) | data formatting | bytes 2097152 | tf_op args[0]
  1.4 0.0 copy-done.3
  1.5 0.0 copy-done.2
  1.5 0.0 copy-done.1
  1.5 1.7 %shard_map.47 = (s32[1,512]{1,0:T(1,128)S(1)}, bf16[512,256]{1,0:T(8,128)(2,1)S(1)}, bf16[32,264,128]{2,1,0:T(8,128)(2,1)S(1)}) custom-call(s32[1]{0:T(128)} %bitcast.quarter_ref, s32[1,512]{1,0:T(1,128)S(1)} %bitcast.8, s32[1,512]{1,0:T(1,128)S(1)} %bitcast.9, f32[1,512]{1,0:T(1,128)S(1)} %bitcast.10, bf16[2,512,512]{2,1,0:T(8,128)(2,1)S(1)} %bitcast.7), custom_call_target="tpu_custom_call" | custom-call | tf_op jit(solution)/shard_map/pallas_call | solution.py:247
  3.2 0.0 copy-start
  3.2 1.3 copy-done
  4.5 8.6 %all-to-all-start = ((bf16[32,264,128]{2,1,0:T(8,128)(2,1)}), bf16[32,264,128]{2,1,0:T(8,128)(2,1)S(1)}, u32[]{:S(2)}, u32[]{:S(2)}) async-start(bf16[32,264,128]{2,1,0:T(8,128)(2,1)} %copy-done), calls=%async_computation | async-start | bytes 4325376 | tf_op jit(solution)/shard_map/all_to_all | solution.py:230
  13.1 8.4 %collective-permute-start.1 = (bf16[512,256]{1,0:T(8,128)(2,1)S(1)}, bf16[512,256]{1,0:T(8,128)(2,1)S(1)}, u32[]{:S(2)}, u32[]{:S(2)}) collective-permute-start(bf16[512,256]{1,0:T(8,128)(2,1)S(1)} %get-tuple-element.14), channel_id=1, source_target_pairs={{0,5},{8,13},{16,21},{24,29},{32,37},{40,45},{48,53},{56,61},{64,6... | collective-permute-start | bytes 786440 | tf_op jit(solution)/shard_map/ppermute | solution.py:220
  21.5 1.3 collective-permute-start
  22.9 4.1 %collective-permute-done.1 = bf16[512,256]{1,0:T(8,128)(2,1)S(1)} collective-permute-done((bf16[512,256]{1,0:T(8,128)(2,1)S(1)}, bf16[512,256]{1,0:T(8,128)(2,1)S(1)}, u32[]{:S(2)}, u32[]{:S(2)}) %collective-permute-start.1) | collective-permute-done | bytes 262176 | tf_op jit(solution)/shard_map/ppermute | solution.py:220
  27.0 1.3 collective-permute-done
  28.3 0.0 copy-start.4
  28.3 2.0 %collective-permute-start.3 = (bf16[512,256]{1,0:T(8,128)(2,1)S(1)}, bf16[512,256]{1,0:T(8,128)(2,1)}, u32[]{:S(2)}, u32[]{:S(2)}) collective-permute-start(bf16[512,256]{1,0:T(8,128)(2,1)S(1)} %select_select_fusion.1), channel_id=1, source_target_pairs={{0,7},{3,2},{8,15},{11,10},{16,23},{19,18},{24,31},{27,26},{32,39}... | collective-permute-start | bytes 786440 | tf_op jit(solution)/shard_map/ppermute | solution.py:223
  30.3 2.0 %collective-permute-start.2 = (bf16[512,256]{1,0:T(8,128)(2,1)S(1)}, bf16[512,256]{1,0:T(8,128)(2,1)}, u32[]{:S(2)}, u32[]{:S(2)}) collective-permute-start(bf16[512,256]{1,0:T(8,128)(2,1)S(1)} %select_select_fusion.1), channel_id=1, source_target_pairs={{0,1},{3,4},{5,6},{8,9},{11,12},{13,14},{16,17},{19,20},{21,22},{2... | collective-permute-start | bytes 786440 | tf_op jit(solution)/shard_map/ppermute | solution.py:222
  32.3 0.8 shard_map.46.table_ref
  33.2 1.3 collective-permute-done.3
  34.5 0.0 copy-done.4
  34.5 2.0 %collective-permute-done.2 = bf16[512,256]{1,0:T(8,128)(2,1)} collective-permute-done((bf16[512,256]{1,0:T(8,128)(2,1)S(1)}, bf16[512,256]{1,0:T(8,128)(2,1)}, u32[]{:S(2)}, u32[]{:S(2)}) %collective-permute-start.2) | collective-permute-done | bytes 262176 | tf_op jit(solution)/shard_map/ppermute | solution.py:222
  36.5 1.0 select_select_fusion.head_ref
  37.5 4.7 %all-to-all-done.arrived_ref.got_ref = bf16[32,264,128]{2,1,0:T(8,128)(2,1)S(1)} async-done(((bf16[32,264,128]{2,1,0:T(8,128)(2,1)}), bf16[32,264,128]{2,1,0:T(8,128)(2,1)S(1)}, u32[]{:S(2)}, u32[]{:S(2)}) %all-to-all-start) | async-done | bytes 2162720 | tf_op jit(solution)/shard_map/all_to_all | solution.py:230
  42.1 0.4 shard_map.48
  42.6 15.3 %all_to_all.20.got_head_ref = bf16[32,64,128]{2,1,0:T(8,128)(2,1)S(1)} all-to-all(bf16[32,64,128]{2,1,0:T(8,128)(2,1)S(1)} %shard_map.48), channel_id=1, replica_groups=mesh['y'=4,'x'=4,'core'=2,'gcol'=8] {'x','y','core'}, dimensions={0} | all-to-all | bytes 1048576 | tf_op jit(solution)/shard_map/all_to_all | solution.py:230
  57.9 1.2 shard_map.49
  59.1 0.2 collective-permute-start.4
  59.3 4.5 %shard_map.50.spectral_ref = bf16[32,4,16,512]{3,2,1,0:T(8,128)(2,1)S(1)} custom-call(bf16[256,1024]{1,0:T(8,128)(2,1)S(1)} %get-tuple-element.15.head_ref, f32[16,1024]{1,0:T(8,128)S(1)} %get-tuple-element.16.weight_ref, bf16[3072,512]{1,0:T(8,128)(2,1)S(1)} %get-tuple-element.17.rows_ref), custom_call_target="tpu_custom_call" | custom-call | tf_op jit(solution)/shard_map/pallas_call | solution.py:287
  63.8 0.0 collective-permute-done.4.upper_ref
  63.8 1.0 shard_map.51
  64.8 33.6 %all_to_all.21.in_ref = bf16[32,4,16,512]{3,2,1,0:T(8,128)(2,1)S(1)} all-to-all(bf16[32,4,16,512]{3,2,1,0:T(8,128)(2,1)S(1)} %shard_map.51), channel_id=1, replica_groups=mesh['y'=4,'x'=4,'core'=2,'gcol'=8] {'x','y','core'}, dimensions={0} | all-to-all | bytes 4194304 | tf_op jit(solution)/shard_map/all_to_all | solution.py:230
  98.4 2.3 %shard_map.52 = bf16[32,4,16,512]{3,2,1,0:T(8,128)(2,1)S(1)} custom-call(bf16[1024,512]{1,0:T(8,128)(2,1)S(1)} %shard_map.46.table_ref, bf16[32,4,16,512]{3,2,1,0:T(8,128)(2,1)S(1)} %all_to_all.21.in_ref), custom_call_target="tpu_custom_call" | custom-call | tf_op jit(solution)/shard_map/pallas_call | solution.py:299
  100.8 31.9 %all_to_all.22.in_ref = bf16[32,4,16,512]{3,2,1,0:T(8,128)(2,1)S(1)} all-to-all(bf16[32,4,16,512]{3,2,1,0:T(8,128)(2,1)S(1)} %shard_map.52), channel_id=1, replica_groups=mesh['y'=4,'x'=4,'core'=2,'gcol'=8] {'x','y','core'}, dimensions={0} | all-to-all | bytes 4194304 | tf_op jit(solution)/shard_map/all_to_all | solution.py:230
  132.6 3.1 %shard_map.53 = f32[8,2,128,512]{3,2,1,0:T(8,128)} custom-call(bf16[32,4,16,512]{3,2,1,0:T(8,128)(2,1)S(1)} %all_to_all.22.in_ref), custom_call_target="tpu_custom_call" | custom-call | tf_op jit(solution)/shard_map/pallas_call | solution.py:300
  (4 shorter events, 0.0 us)
Async XLA Ops:
  0.0 1.5 %copy-start.3 = (f32[512]{0:T(512)S(1)}, f32[512]{0:T(512)}, u32[]{:S(2)}) copy-start(f32[512]{0:T(512)} %param.7) | copy-start | bytes 6148
  0.0 1.5 %copy-start.2 = (s32[512]{0:T(512)S(1)}, s32[512]{0:T(512)}, u32[]{:S(2)}) copy-start(s32[512]{0:T(512)} %param.6) | copy-start | bytes 6148
  0.0 1.5 %copy-start.1 = (s32[512,1]{0,1:T(1,128)S(1)}, s32[512,1]{0,1:T(1,128)}, u32[]{:S(2)}) copy-start(s32[512,1]{0,1:T(1,128)} %param.5) | copy-start | bytes 6148
  3.2 1.3 copy-start
  4.5 37.6 %all-to-all-start = ((bf16[32,264,128]{2,1,0:T(8,128)(2,1)}), bf16[32,264,128]{2,1,0:T(8,128)(2,1)S(1)}, u32[]{:S(2)}, u32[]{:S(2)}) async-start(bf16[32,264,128]{2,1,0:T(8,128)(2,1)} %copy-done), calls=%async_computation | async-start | bytes 4325376 | tf_op jit(solution)/shard_map/all_to_all | solution.py:230
  13.1 13.8 %collective-permute-start.1 = (bf16[512,256]{1,0:T(8,128)(2,1)S(1)}, bf16[512,256]{1,0:T(8,128)(2,1)S(1)}, u32[]{:S(2)}, u32[]{:S(2)}) collective-permute-start(bf16[512,256]{1,0:T(8,128)(2,1)S(1)} %get-tuple-element.14), channel_id=1, source_target_pairs={{0,5},{8,13},{16,21},{24,29},{32,37},{40,45},{48,53},{56,61},{64,6... | collective-permute-start | bytes 786440 | tf_op jit(solution)/shard_map/ppermute | solution.py:220
  21.5 6.8 %collective-permute-start = (bf16[512,256]{1,0:T(8,128)(2,1)S(1)}, bf16[512,256]{1,0:T(8,128)(2,1)S(1)}, u32[]{:S(2)}, u32[]{:S(2)}) collective-permute-start(bf16[512,256]{1,0:T(8,128)(2,1)S(1)} %get-tuple-element.14), channel_id=1, source_target_pairs={{0,3},{8,11},{16,19},{24,27},{32,35},{40,43},{48,51},{56,59},{64,6... | collective-permute-start | bytes 786440 | tf_op jit(solution)/shard_map/ppermute | solution.py:219
  28.3 6.2 %copy-start.4 = (bf16[512,256]{1,0:T(8,128)(2,1)}, bf16[512,256]{1,0:T(8,128)(2,1)S(1)}, u32[]{:S(2)}) copy-start(bf16[512,256]{1,0:T(8,128)(2,1)S(1)} %select_select_fusion.1) | copy-start | bytes 786436
  28.3 6.2 %collective-permute-start.3 = (bf16[512,256]{1,0:T(8,128)(2,1)S(1)}, bf16[512,256]{1,0:T(8,128)(2,1)}, u32[]{:S(2)}, u32[]{:S(2)}) collective-permute-start(bf16[512,256]{1,0:T(8,128)(2,1)S(1)} %select_select_fusion.1), channel_id=1, source_target_pairs={{0,7},{3,2},{8,15},{11,10},{16,23},{19,18},{24,31},{27,26},{32,39}... | collective-permute-start | bytes 786440 | tf_op jit(solution)/shard_map/ppermute | solution.py:223
  30.3 6.1 %collective-permute-start.2 = (bf16[512,256]{1,0:T(8,128)(2,1)S(1)}, bf16[512,256]{1,0:T(8,128)(2,1)}, u32[]{:S(2)}, u32[]{:S(2)}) collective-permute-start(bf16[512,256]{1,0:T(8,128)(2,1)S(1)} %select_select_fusion.1), channel_id=1, source_target_pairs={{0,1},{3,4},{5,6},{8,9},{11,12},{13,14},{16,17},{19,20},{21,22},{2... | collective-permute-start | bytes 786440 | tf_op jit(solution)/shard_map/ppermute | solution.py:222
  59.1 4.7 %collective-permute-start.4 = (bf16[2,128,512]{2,1,0:T(8,128)(2,1)S(1)}, bf16[2,128,512]{2,1,0:T(8,128)(2,1)S(1)}, u32[]{:S(2)}, u32[]{:S(2)}) collective-permute-start(bf16[2,128,512]{2,1,0:T(8,128)(2,1)S(1)} %get-tuple-element.18), channel_id=1, source_target_pairs={{0,8},{8,64},{64,72},{72,128},{128,136},{136,192},{192,200},{200,2... | collective-permute-start | bytes 786440 | tf_op jit(solution)/shard_map/ppermute | solution.py:286
